TPU v7x, 512 devices: a whole 4x8x8 slice. The times are simulated.
512 devices in a mesh: pipe: 4 (over y_lo), dp: 16 (over x, y_hi, core), tensor: 8 (over z).
Axes of the slice: x: 4, y: 8 (y_hi: 2, y_lo: 4; y = y_hi * 4 + y_lo), z: 8, core: 2. Of those that a mesh axis runs over, the one named last changes fastest.
Arguments:
- saved: bfloat16 [4, 4, 96, 4096], P('pipe', None, 'dp', 'tensor'), may hold values from -6 to 6
- pool: bfloat16 [8, 96, 4096], P(None, 'dp', 'tensor'), may hold values from -6 to 6
- picked: int32 [4], replicated, may hold values from 0 to 7
- w_up: bfloat16 [4, 4096, 14336], P('pipe', 'tensor', 'dp'), may hold values from -0.09375 to 0.09375
- w_down: bfloat16 [4, 14336, 4096], P('pipe', 'dp', 'tensor'), may hold values from -0.046875 to 0.046875
Outputs:
- input_grads: bfloat16 [4, 4, 96, 4096], P('pipe', None, 'dp', 'tensor')
- grad_up: bfloat16 [4, 4096, 14336], P('pipe', 'tensor', 'dp')
- grad_down: bfloat16 [4, 14336, 4096], P('pipe', 'dp', 'tensor')
All inputs are finite; a program needn't handle non-finite values.
Results may differ from a plain program's by a relative error of at most 0.034.
Values may be sent and summed in bfloat16 or wider, within the bound.
No kernel may reach another device: no remote copies, remote signals or barrier semaphores. Data moves between devices by JAX's collectives and lax.ppermute only.
A program may use at most 128 MiB of HBM per device.

v0:
```python
import jax
import jax.numpy as jnp
from jax import lax
from jax.sharding import PartitionSpec as P


def passed_along(shard, axis, by):
    peers = lax.axis_size(axis)
    pairs = [(i, i + by) for i in range(peers) if 0 <= i + by < peers]
    return lax.ppermute(shard, axis, pairs)


def local_grads(up, back):
    sig = jax.nn.sigmoid(up)
    hidden = (up * sig).astype(jnp.bfloat16)
    d_up = (back * sig * (1.0 + up * (1.0 - sig))).astype(jnp.bfloat16)
    return (hidden, d_up)


def contract_rows(left, right):
    return lax.dot_general(
        left, right, (((0,), (0,)), ((), ())), preferred_element_type=jnp.float32
    )


def contract_cols(left, right):
    return lax.dot_general(
        left, right, (((1,), (1,)), ((), ())), preferred_element_type=jnp.float32
    )


def body(saved, pool, picked, w_up, w_down):
    segments = lax.axis_size("pipe")
    segment = lax.axis_index("pipe")
    micro_count = saved.shape[1]
    rows = saved.shape[2]
    width = saved.shape[3]
    units = w_up.shape[2]
    up_w = w_up[0]
    down_w = w_down[0]
    carried = jnp.zeros((rows, width), jnp.bfloat16)
    grads_in = jnp.zeros((micro_count, rows, width), jnp.bfloat16)
    acc_up = jnp.zeros((width, units), jnp.float32)
    acc_down = jnp.zeros((units, width), jnp.float32)
    for tick in range(micro_count + segments - 1):
        micro = tick - (segments - 1 - segment)
        valid = jnp.logical_and(micro >= 0, micro < micro_count)
        slot = jnp.clip(micro, 0, micro_count - 1)
        received = passed_along(carried, "pipe", -1)
        chosen = lax.dynamic_index_in_dim(picked, slot, 0, keepdims=False)
        fresh = lax.dynamic_index_in_dim(pool, chosen, 0, keepdims=False)
        arriving = jnp.where(segment == segments - 1, fresh, received)
        inputs = lax.dynamic_index_in_dim(saved[0], slot, 0, keepdims=False)
        full_in, full_back = (
            lax.all_gather(inputs, "dp", axis=0, tiled=True),
            lax.all_gather(arriving, "dp", axis=0, tiled=True),
        )
        up_part = jnp.dot(full_in, up_w, preferred_element_type=jnp.float32)
        back_part = contract_cols(full_back, down_w)
        up, back = (
            lax.psum(up_part.astype(jnp.bfloat16), "tensor").astype(jnp.float32),
            lax.psum(back_part.astype(jnp.bfloat16), "tensor").astype(jnp.float32),
        )
        hidden, d_up = local_grads(up, back)
        mixed = lax.psum_scatter(
            contract_cols(d_up, up_w).astype(jnp.bfloat16), "dp", scatter_dimension=0, tiled=True
        ).astype(jnp.float32)
        result = (arriving.astype(jnp.float32) + mixed).astype(jnp.bfloat16)
        carried = result
        grads_in = jnp.where(
            valid, lax.dynamic_update_index_in_dim(grads_in, result, slot, 0), grads_in
        )
        acc_up = jnp.where(valid, acc_up + contract_rows(full_in, d_up), acc_up)
        acc_down = jnp.where(valid, acc_down + contract_rows(hidden, full_back), acc_down)
    return (grads_in[None], acc_up.astype(jnp.bfloat16)[None], acc_down.astype(jnp.bfloat16)[None])


def solution(mesh):
    return jax.shard_map(
        body,
        mesh=mesh,
        in_specs=(
            P("pipe", None, "dp", "tensor"),
            P(None, "dp", "tensor"),
            P(),
            P("pipe", "tensor", "dp"),
            P("pipe", "dp", "tensor"),
        ),
        out_specs=(
            P("pipe", None, "dp", "tensor"),
            P("pipe", "tensor", "dp"),
            P("pipe", "dp", "tensor"),
        ),
        check_vma=False,
    )
```

profile of v0, /device:TPU:1, one launch (start us, length us, event | category | flops | bytes accessed | tf_op | source)
XLA Modules:
  0.0 1355.5 jit_solution(16440202860064931354)
XLA Ops:
  19.0 1.7 constant_dynamic-slice_fusion.9
  20.7 33.9 %all-gather = bf16[1,1,96,512]{3,1,0,2:T(2,128)(2,1)S(1)} all-gather(bf16[1,1,6,512]{3,1,0,2:T(2,128)(2,1)S(1)} %get-tuple-element.51), channel_id=2, replica_groups=mesh['pipe'=4,'dp'=16,'tensor'=8] {'dp'}, dimensions={2}, use_global_device_ids=true | all-gather | bytes 104448 | tf_op jit(solution)/shard_map/all_gather | solution.py:55
  59.9 1.9 constant_dynamic-slice_fusion.12
  61.8 27.5 %all-gather.7 = bf16[16,6,512]{2,1,0:T(8,128)(2,1)S(1)} all-gather(bf16[1,6,512]{2,1,0:T(8,128)(2,1)S(1)} %fusion.158), channel_id=1, replica_groups=mesh['pipe'=4,'dp'=16,'tensor'=8] {'dp'}, dimensions={0}, use_global_device_ids=true | all-gather | bytes 104448 | tf_op jit(solution)/shard_map/all_gather | solution.py:56
  90.6 74.3 %all-reduce.41.cloned.1.call-done = (bf16[96,896]{1,0:T(8,128)(2,1)}, bf16[96,896]{1,0:T(8,128)(2,1)}) async-done(((bf16[96,896]{1,0:T(8,128)(2,1)}, bf16[96,896]{1,0:T(8,128)(2,1)}), (bf16[96,896]{1,0:T(8,128)(2,1)}, bf16[96,896]{1,0:T(8,128)(2,1)})) %all-reduce.41.cloned.1.call-update) | async-done | bytes 344080 | tf_op jit(solution)/shard_map/psum | solution.py:61
  166.3 50.2 %fusion = bf16[8,512]{1,0:T(8,128)(2,1)S(1)} fusion(bf16[96,512]{1,0:T(8,128)(2,1)S(1)} %convolution_convert_fusion.20), kind=kCustom, calls=%all-reduce-scatter | all-reduce-scatter fusion | flops 65537 | bytes 108544
  216.6 2.1 collective-permute-start.9
  219.9 7.9 collective-permute-start.7
  227.9 3.2 collective-permute-start.10
  231.1 27.9 %all-gather.1 = bf16[1,1,96,512]{3,1,0,2:T(2,128)(2,1)S(1)} all-gather(bf16[1,1,6,512]{3,1,0,2:T(2,128)(2,1)S(1)} %get-tuple-element.50), channel_id=3, replica_groups=mesh['pipe'=4,'dp'=16,'tensor'=8] {'dp'}, dimensions={2}, use_global_device_ids=true | all-gather | bytes 104448 | tf_op jit(solution)/shard_map/all_gather | solution.py:55
  263.7 2.1 collective-permute-done.1
  265.8 27.4 %all-gather.8 = bf16[16,6,512]{2,1,0:T(8,128)(2,1)S(1)} all-gather(bf16[1,6,512]{2,1,0:T(8,128)(2,1)S(1)} %fusion.159), channel_id=1, replica_groups=mesh['pipe'=4,'dp'=16,'tensor'=8] {'dp'}, dimensions={0}, use_global_device_ids=true | all-gather | bytes 104448 | tf_op jit(solution)/shard_map/all_gather | solution.py:56
  294.4 68.2 %all-reduce.39.cloned.1.call-done = (bf16[96,896]{1,0:T(8,128)(2,1)}, bf16[96,896]{1,0:T(8,128)(2,1)}) async-done(((bf16[96,896]{1,0:T(8,128)(2,1)}, bf16[96,896]{1,0:T(8,128)(2,1)}), (bf16[96,896]{1,0:T(8,128)(2,1)}, bf16[96,896]{1,0:T(8,128)(2,1)})) %all-reduce.39.cloned.1.call-update) | async-done | bytes 344080 | tf_op jit(solution)/shard_map/psum | solution.py:61
  364.1 50.2 %fusion.1 = bf16[8,512]{1,0:T(8,128)(2,1)S(1)} fusion(bf16[96,512]{1,0:T(8,128)(2,1)S(1)} %convolution_convert_fusion.19), kind=kCustom, calls=%all-reduce-scatter.1 | all-reduce-scatter fusion | flops 65537 | bytes 108544
  414.3 2.1 collective-permute-start.13
  417.7 7.9 collective-permute-start.11
  425.6 3.2 collective-permute-start.14
  428.8 27.9 %all-gather.2 = bf16[1,1,96,512]{3,1,0,2:T(2,128)(2,1)S(1)} all-gather(bf16[1,1,6,512]{3,1,0,2:T(2,128)(2,1)S(1)} %get-tuple-element.49), channel_id=4, replica_groups=mesh['pipe'=4,'dp'=16,'tensor'=8] {'dp'}, dimensions={2}, use_global_device_ids=true | all-gather | bytes 104448 | tf_op jit(solution)/shard_map/all_gather | solution.py:55
  459.5 2.1 collective-permute-done.2
  461.6 27.4 %all-gather.9 = bf16[16,6,512]{2,1,0:T(8,128)(2,1)S(1)} all-gather(bf16[1,6,512]{2,1,0:T(8,128)(2,1)S(1)} %fusion.160), channel_id=1, replica_groups=mesh['pipe'=4,'dp'=16,'tensor'=8] {'dp'}, dimensions={0}, use_global_device_ids=true | all-gather | bytes 104448 | tf_op jit(solution)/shard_map/all_gather | solution.py:56
  490.2 28.5 %all-gather.6 = bf16[1,1,96,512]{3,1,0,2:T(2,128)(2,1)S(1)} all-gather(bf16[1,1,6,512]{3,1,0,2:T(2,128)(2,1)S(1)} %get-tuple-element.45), channel_id=8, replica_groups=mesh['pipe'=4,'dp'=16,'tensor'=8] {'dp'}, dimensions={2}, use_global_device_ids=true | all-gather | bytes 104448 | tf_op jit(solution)/shard_map/all_gather | solution.py:55
  518.7 26.9 %all-gather.3 = bf16[1,1,96,512]{3,1,0,2:T(2,128)(2,1)S(1)} all-gather(bf16[1,1,6,512]{3,1,0,2:T(2,128)(2,1)S(1)} %get-tuple-element.48), channel_id=5, replica_groups=mesh['pipe'=4,'dp'=16,'tensor'=8] {'dp'}, dimensions={2}, use_global_device_ids=true | all-gather | bytes 104448 | tf_op jit(solution)/shard_map/all_gather | solution.py:55
  546.6 12.3 all-reduce.37.cloned.1.call-done
  560.3 49.7 %fusion.2 = bf16[8,512]{1,0:T(8,128)(2,1)S(1)} fusion(bf16[96,512]{1,0:T(8,128)(2,1)S(1)} %convolution_convert_fusion.18), kind=kCustom, calls=%all-reduce-scatter.2 | all-reduce-scatter fusion | flops 65537 | bytes 108544
  610.1 2.1 collective-permute-start.17
  613.5 7.9 collective-permute-start.15
  621.4 3.2 collective-permute-start.18
  627.4 32.1 %all-gather.5 = bf16[1,1,96,512]{3,1,0,2:T(2,128)(2,1)S(1)} all-gather(bf16[1,1,6,512]{3,1,0,2:T(2,128)(2,1)S(1)} %copy-done.31), channel_id=7, replica_groups=mesh['pipe'=4,'dp'=16,'tensor'=8] {'dp'}, dimensions={2}, use_global_device_ids=true | all-gather | bytes 104448 | tf_op jit(solution)/shard_map/all_gather | solution.py:55
  660.1 24.6 %all-gather.10 = bf16[16,6,512]{2,1,0:T(8,128)(2,1)S(1)} all-gather(bf16[1,6,512]{2,1,0:T(8,128)(2,1)S(1)} %fusion.161), channel_id=1, replica_groups=mesh['pipe'=4,'dp'=16,'tensor'=8] {'dp'}, dimensions={0}, use_global_device_ids=true | all-gather | bytes 104448 | tf_op jit(solution)/shard_map/all_gather | solution.py:56
  686.9 30.5 %all-gather.4 = bf16[1,1,96,512]{3,1,0,2:T(2,128)(2,1)S(1)} all-gather(bf16[1,1,6,512]{3,1,0,2:T(2,128)(2,1)S(1)} %copy-done.30), channel_id=6, replica_groups=mesh['pipe'=4,'dp'=16,'tensor'=8] {'dp'}, dimensions={2}, use_global_device_ids=true | all-gather | bytes 104448 | tf_op jit(solution)/shard_map/all_gather | solution.py:55
  719.1 37.7 %all-reduce.35.cloned.1.call-done = (bf16[96,896]{1,0:T(8,128)(2,1)}, bf16[96,896]{1,0:T(8,128)(2,1)}) async-done(((bf16[96,896]{1,0:T(8,128)(2,1)}, bf16[96,896]{1,0:T(8,128)(2,1)}), (bf16[96,896]{1,0:T(8,128)(2,1)}, bf16[96,896]{1,0:T(8,128)(2,1)})) %all-reduce.35.cloned.1.call-update) | async-done | bytes 344080 | tf_op jit(solution)/shard_map/psum | solution.py:61
  758.2 50.2 %fusion.3 = bf16[8,512]{1,0:T(8,128)(2,1)S(1)} fusion(bf16[96,512]{1,0:T(8,128)(2,1)S(1)} %convolution_convert_fusion.17), kind=kCustom, calls=%all-reduce-scatter.3 | all-reduce-scatter fusion | flops 65537 | bytes 108544
  808.5 2.2 collective-permute-start.21
  812.0 7.9 collective-permute-start.19
  819.9 3.2 collective-permute-start.22
  823.1 2.7 fusion.118
  829.1 2.6 fusion.92
  832.2 30.7 %all-gather.11 = bf16[16,6,512]{2,1,0:T(8,128)(2,1)S(1)} all-gather(bf16[1,6,512]{2,1,0:T(8,128)(2,1)S(1)} %fusion.162), channel_id=1, replica_groups=mesh['pipe'=4,'dp'=16,'tensor'=8] {'dp'}, dimensions={0}, use_global_device_ids=true | all-gather | bytes 104448 | tf_op jit(solution)/shard_map/all_gather | solution.py:56
  864.3 1.7 fusion.90
  866.0 1.7 fusion.115
  867.8 61.9 %all-reduce.33.cloned.1.call-done = (bf16[96,896]{1,0:T(8,128)(2,1)}, bf16[96,896]{1,0:T(8,128)(2,1)}) async-done(((bf16[96,896]{1,0:T(8,128)(2,1)}, bf16[96,896]{1,0:T(8,128)(2,1)}), (bf16[96,896]{1,0:T(8,128)(2,1)}, bf16[96,896]{1,0:T(8,128)(2,1)})) %all-reduce.33.cloned.1.call-update) | async-done | bytes 344080 | tf_op jit(solution)/shard_map/psum | solution.py:61
  931.1 50.3 %fusion.4 = bf16[8,512]{1,0:T(8,128)(2,1)S(1)} fusion(bf16[96,512]{1,0:T(8,128)(2,1)S(1)} %convolution_convert_fusion.16), kind=kCustom, calls=%all-reduce-scatter.4 | all-reduce-scatter fusion | flops 65537 | bytes 108544
  981.4 2.1 collective-permute-start.25
  984.8 7.9 collective-permute-start.23
  992.7 3.2 collective-permute-start.26
  999.6 1.7 fusion.88
  1002.7 31.8 %all-gather.12 = bf16[16,6,512]{2,1,0:T(8,128)(2,1)S(1)} all-gather(bf16[1,6,512]{2,1,0:T(8,128)(2,1)S(1)} %fusion.163), channel_id=1, replica_groups=mesh['pipe'=4,'dp'=16,'tensor'=8] {'dp'}, dimensions={0}, use_global_device_ids=true | all-gather | bytes 104448 | tf_op jit(solution)/shard_map/all_gather | solution.py:56
  1035.8 1.8 fusion.86
  1039.3 61.5 %all-reduce.31.cloned.1.call-done = (bf16[96,896]{1,0:T(8,128)(2,1)}, bf16[96,896]{1,0:T(8,128)(2,1)}) async-done(((bf16[96,896]{1,0:T(8,128)(2,1)}, bf16[96,896]{1,0:T(8,128)(2,1)}), (bf16[96,896]{1,0:T(8,128)(2,1)}, bf16[96,896]{1,0:T(8,128)(2,1)})) %all-reduce.31.cloned.1.call-update) | async-done | bytes 344080 | tf_op jit(solution)/shard_map/psum | solution.py:61
  1102.2 50.2 %fusion.5 = bf16[8,512]{1,0:T(8,128)(2,1)S(1)} fusion(bf16[96,512]{1,0:T(8,128)(2,1)S(1)} %convolution_convert_fusion.15), kind=kCustom, calls=%all-reduce-scatter.5 | all-reduce-scatter fusion | flops 65537 | bytes 108544
  1152.4 2.2 collective-permute-start.29
  1155.9 7.9 collective-permute-start.27
  1163.8 3.2 collective-permute-start.30
  1167.1 1.7 fusion.106
  1173.9 31.8 %all-gather.13 = bf16[16,6,512]{2,1,0:T(8,128)(2,1)S(1)} all-gather(bf16[1,6,512]{2,1,0:T(8,128)(2,1)S(1)} %fusion.164), channel_id=1, replica_groups=mesh['pipe'=4,'dp'=16,'tensor'=8] {'dp'}, dimensions={0}, use_global_device_ids=true | all-gather | bytes 104448 | tf_op jit(solution)/shard_map/all_gather | solution.py:56
  1207.3 2.6 fusion.103
  1209.9 61.9 %all-reduce.29.cloned.1.call-done = (bf16[96,896]{1,0:T(8,128)(2,1)}, bf16[96,896]{1,0:T(8,128)(2,1)}) async-done(((bf16[96,896]{1,0:T(8,128)(2,1)}, bf16[96,896]{1,0:T(8,128)(2,1)}), (bf16[96,896]{1,0:T(8,128)(2,1)}, bf16[96,896]{1,0:T(8,128)(2,1)})) %all-reduce.29.cloned.1.call-update) | async-done | bytes 344080 | tf_op jit(solution)/shard_map/psum | solution.py:61
  1271.9 2.1 convolution_convert_fusion.14
  1274.0 50.8 %fusion.6 = bf16[8,512]{1,0:T(8,128)(2,1)S(1)} fusion(bf16[96,512]{1,0:T(8,128)(2,1)} %convolution_convert_fusion.14), kind=kCustom, calls=%all-reduce-scatter.6 | all-reduce-scatter fusion | flops 65537 | bytes 108544
  1324.8 2.0 collective-permute-start.33
  1328.2 8.0 collective-permute-start.31
  1336.2 3.6 collective-permute-start.34
  1339.9 5.6 fusion.10
  1345.5 2.0 fusion.9
  (198 shorter events, 60.8 us)
Async XLA Ops:
  7.2 51.8 %copy-start = (bf16[1,512,896]{2,1,0:T(8,128)(2,1)S(1)}, bf16[1,512,896]{2,1,0:T(8,128)(2,1)}, u32[]{:S(2)}) copy-start(bf16[1,512,896]{2,1,0:T(8,128)(2,1)} %param.8) | copy-start | bytes 2752516
  7.2 82.2 %copy-start.1 = (bf16[1,896,512]{2,1,0:T(8,128)(2,1)S(1)}, bf16[1,896,512]{2,1,0:T(8,128)(2,1)}, u32[]{:S(2)}) copy-start(bf16[1,896,512]{2,1,0:T(8,128)(2,1)} %param.9) | copy-start | bytes 2752516
  7.2 157.7 %all-reduce.41.cloned.1.call-start = ((), (), s32[]{:S(2)}) async-start(), calls=%async_computation.6 | async-start | bytes 688128 | tf_op jit(solution)/shard_map/psum | solution.py:61
  7.2 54.5 %collective-permute-start = (bf16[6,512]{1,0:T(8,128)(2,1)S(1)}, bf16[6,512]{1,0:T(8,128)(2,1)S(1)}, u32[]{:S(2)}, u32[]{:S(2)}) collective-permute-start(bf16[6,512]{1,0:T(8,128)(2,1)S(1)} %broadcast_in_dim.44), channel_id=1, source_target_pairs={{128,0},{256,128},{384,256},{129,1},{257,129},{385,257},{130,2},{2... | collective-permute-start | bytes 18440 | tf_op jit(solution)/shard_map/ppermute | solution.py:10
  61.8 597.8 %copy-start.26 = (bf16[1,6,512]{2,0,1:T(2,128)(2,1)}, bf16[1,6,512]{2,0,1:T(2,128)(2,1)S(1)}, u32[]{:S(2)}) copy-start(bf16[1,6,512]{2,0,1:T(2,128)(2,1)S(1)} %get-tuple-element.41) | copy-start | bytes 18436
  90.5 272.1 %all-reduce.39.cloned.1.call-start = ((), (), s32[]{:S(2)}) async-start(), calls=%async_computation.5 | async-start | bytes 688128 | tf_op jit(solution)/shard_map/psum | solution.py:61
  216.6 44.4 %collective-permute-start.9 = (bf16[8,512]{1,0:T(8,128)(2,1)S(1)}, bf16[8,512]{1,0:T(8,128)(2,1)S(1)}, u32[]{:S(2)}, u32[]{:S(2)}) collective-permute-start(bf16[8,512]{1,0:T(8,128)(2,1)S(1)} %fusion), channel_id=1, source_target_pairs={{0,24},{8,32},{16,40},{24,48},{32,56},{40,64},{48,72},{56,80},{64,... | collective-permute-start | bytes 24584
  218.6 42.3 %collective-permute-start.8 = (bf16[8,512]{1,0:T(8,128)(2,1)S(1)}, bf16[8,512]{1,0:T(8,128)(2,1)S(1)}, u32[]{:S(2)}, u32[]{:S(2)}) collective-permute-start(bf16[8,512]{1,0:T(8,128)(2,1)S(1)} %fusion), channel_id=1, source_target_pairs={{0,16},{8,24},{16,32},{24,40},{32,48},{40,56},{48,64},{56,72},{64,... | collective-permute-start | bytes 24584
  219.9 41.0 %collective-permute-start.7 = (bf16[8,512]{1,0:T(8,128)(2,1)S(1)}, bf16[8,512]{1,0:T(8,128)(2,1)S(1)}, u32[]{:S(2)}, u32[]{:S(2)}) collective-permute-start(bf16[8,512]{1,0:T(8,128)(2,1)S(1)} %fusion), channel_id=1, source_target_pairs={{0,8},{8,16},{16,24},{24,32},{32,40},{40,48},{48,56},{56,64},{64,7... | collective-permute-start | bytes 24584
  227.9 33.1 %collective-permute-start.10 = (bf16[6,512]{1,0:T(8,128)(2,1)S(1)}, bf16[6,512]{1,0:T(8,128)(2,1)S(1)}, u32[]{:S(2)}, u32[]{:S(2)}) collective-permute-start(bf16[6,512]{1,0:T(8,128)(2,1)S(1)} %slice), channel_id=1, source_target_pairs={{0,32},{8,40},{16,48},{24,56},{32,64},{40,72},{48,80},{56,88},{64,... | collective-permute-start | bytes 18440
  261.4 4.4 collective-permute-start.1
  294.4 264.5 %all-reduce.37.cloned.1.call-start = ((), (), s32[]{:S(2)}) async-start(), calls=%async_computation.4 | async-start | bytes 688128 | tf_op jit(solution)/shard_map/psum | solution.py:61
  414.3 42.4 %collective-permute-start.13 = (bf16[8,512]{1,0:T(8,128)(2,1)S(1)}, bf16[8,512]{1,0:T(8,128)(2,1)S(1)}, u32[]{:S(2)}, u32[]{:S(2)}) collective-permute-start(bf16[8,512]{1,0:T(8,128)(2,1)S(1)} %fusion.1), channel_id=1, source_target_pairs={{0,24},{8,32},{16,40},{24,48},{32,56},{40,64},{48,72},{56,80},{64,... | collective-permute-start | bytes 24584
  416.4 40.4 %collective-permute-start.12 = (bf16[8,512]{1,0:T(8,128)(2,1)S(1)}, bf16[8,512]{1,0:T(8,128)(2,1)S(1)}, u32[]{:S(2)}, u32[]{:S(2)}) collective-permute-start(bf16[8,512]{1,0:T(8,128)(2,1)S(1)} %fusion.1), channel_id=1, source_target_pairs={{0,16},{8,24},{16,32},{24,40},{32,48},{40,56},{48,64},{56,72},{64,... | collective-permute-start | bytes 24584
  417.7 39.1 %collective-permute-start.11 = (bf16[8,512]{1,0:T(8,128)(2,1)S(1)}, bf16[8,512]{1,0:T(8,128)(2,1)S(1)}, u32[]{:S(2)}, u32[]{:S(2)}) collective-permute-start(bf16[8,512]{1,0:T(8,128)(2,1)S(1)} %fusion.1), channel_id=1, source_target_pairs={{0,8},{8,16},{16,24},{24,32},{32,40},{40,48},{48,56},{56,64},{64,7... | collective-permute-start | bytes 24584
  425.6 31.1 %collective-permute-start.14 = (bf16[6,512]{1,0:T(8,128)(2,1)S(1)}, bf16[6,512]{1,0:T(8,128)(2,1)S(1)}, u32[]{:S(2)}, u32[]{:S(2)}) collective-permute-start(bf16[6,512]{1,0:T(8,128)(2,1)S(1)} %slice.1), channel_id=1, source_target_pairs={{0,32},{8,40},{16,48},{24,56},{32,64},{40,72},{48,80},{56,88},{64,... | collective-permute-start | bytes 18440
  457.2 4.4 collective-permute-start.2
  490.2 266.6 %all-reduce.35.cloned.1.call-start = ((), (), s32[]{:S(2)}) async-start(), calls=%async_computation.3 | async-start | bytes 688128 | tf_op jit(solution)/shard_map/psum | solution.py:61
  558.9 68.5 %copy-start.31 = (bf16[1,1,6,512]{3,1,0,2:T(2,128)(2,1)S(1)}, bf16[1,1,6,512]{3,1,0,2:T(2,128)(2,1)}, u32[]{:S(2)}) copy-start(bf16[1,1,6,512]{3,1,0,2:T(2,128)(2,1)} %get-tuple-element.46) | copy-start | bytes 18436
  610.1 15.5 %collective-permute-start.17 = (bf16[8,512]{1,0:T(8,128)(2,1)S(1)}, bf16[8,512]{1,0:T(8,128)(2,1)S(1)}, u32[]{:S(2)}, u32[]{:S(2)}) collective-permute-start(bf16[8,512]{1,0:T(8,128)(2,1)S(1)} %fusion.2), channel_id=1, source_target_pairs={{0,24},{8,32},{16,40},{24,48},{32,56},{40,64},{48,72},{56,80},{64,... | collective-permute-start | bytes 24584
  612.2 13.4 collective-permute-start.16
  613.5 12.1 collective-permute-start.15
  621.4 4.2 collective-permute-start.18
  626.1 33.5 %copy-start.15 = (bf16[4,6,512]{2,1,0:T(8,128)(2,1)}, bf16[4,6,512]{2,1,0:T(8,128)(2,1)S(1)}, u32[]{:S(2)}) copy-start(bf16[4,6,512]{2,1,0:T(8,128)(2,1)S(1)} %get-tuple-element.32) | copy-start | bytes 73732
  626.1 33.4 %collective-permute-start.3 = (bf16[6,512]{1,0:T(8,128)(2,1)S(1)}, bf16[6,512]{1,0:T(8,128)(2,1)S(1)}, u32[]{:S(2)}, u32[]{:S(2)}) collective-permute-start(bf16[6,512]{1,0:T(8,128)(2,1)S(1)} %get-tuple-element.33), channel_id=1, source_target_pairs={{128,0},{256,128},{384,256},{129,1},{257,129},{385,257},{130,2},{2... | collective-permute-start | bytes 18440 | tf_op jit(solution)/shard_map/ppermute | solution.py:10
  685.9 243.7 %all-reduce.33.cloned.1.call-start = ((), (), s32[]{:S(2)}) async-start(), calls=%async_computation.2 | async-start | bytes 688128 | tf_op jit(solution)/shard_map/psum | solution.py:61
  758.2 68.1 %copy-start.27 = (bf16[1,6,512]{2,0,1:T(2,128)(2,1)S(1)}, bf16[1,6,512]{2,0,1:T(2,128)(2,1)}, u32[]{:S(2)}) copy-start(bf16[1,6,512]{2,0,1:T(2,128)(2,1)} %copy-done.26) | copy-start | bytes 18436
  808.5 23.7 %copy-start.24 = (bf16[1,6,512]{2,0,1:T(2,128)(2,1)S(1)}, bf16[1,6,512]{2,0,1:T(2,128)(2,1)}, u32[]{:S(2)}) copy-start(bf16[1,6,512]{2,0,1:T(2,128)(2,1)} %get-tuple-element.40) | copy-start | bytes 18436
  808.5 17.4 %collective-permute-start.21 = (bf16[8,512]{1,0:T(8,128)(2,1)S(1)}, bf16[8,512]{1,0:T(8,128)(2,1)S(1)}, u32[]{:S(2)}, u32[]{:S(2)}) collective-permute-start(bf16[8,512]{1,0:T(8,128)(2,1)S(1)} %fusion.3), channel_id=1, source_target_pairs={{0,24},{8,32},{16,40},{24,48},{32,56},{40,64},{48,72},{56,80},{64,... | collective-permute-start | bytes 24584
  810.7 15.2 %collective-permute-start.20 = (bf16[8,512]{1,0:T(8,128)(2,1)S(1)}, bf16[8,512]{1,0:T(8,128)(2,1)S(1)}, u32[]{:S(2)}, u32[]{:S(2)}) collective-permute-start(bf16[8,512]{1,0:T(8,128)(2,1)S(1)} %fusion.3), channel_id=1, source_target_pairs={{0,16},{8,24},{16,32},{24,40},{32,48},{40,56},{48,64},{56,72},{64,... | collective-permute-start | bytes 24584
  812.0 13.9 %collective-permute-start.19 = (bf16[8,512]{1,0:T(8,128)(2,1)S(1)}, bf16[8,512]{1,0:T(8,128)(2,1)S(1)}, u32[]{:S(2)}, u32[]{:S(2)}) collective-permute-start(bf16[8,512]{1,0:T(8,128)(2,1)S(1)} %fusion.3), channel_id=1, source_target_pairs={{0,8},{8,16},{16,24},{24,32},{32,40},{40,48},{48,56},{56,64},{64,7... | collective-permute-start | bytes 24584
  819.9 5.9 collective-permute-start.22
  827.6 36.7 %copy-start.10 = (bf16[96,896]{1,0:T(8,128)(2,1)S(1)}, bf16[96,896]{1,0:T(8,128)(2,1)}, u32[]{:S(2)}) copy-start(bf16[96,896]{1,0:T(8,128)(2,1)} %get-tuple-element.22) | copy-start | bytes 516100
  827.6 4.5 collective-permute-start.4
  832.2 33.9 %copy-start.34 = (bf16[6,512]{1,0:T(8,128)(2,1)}, bf16[6,512]{1,0:T(8,128)(2,1)S(1)}, u32[]{:S(2)}) copy-start(bf16[6,512]{1,0:T(8,128)(2,1)S(1)} %collective-permute-done.4) | copy-start | bytes 18436
  864.1 236.7 %all-reduce.31.cloned.1.call-start = ((), (), s32[]{:S(2)}) async-start(), calls=%async_computation.1 | async-start | bytes 688128 | tf_op jit(solution)/shard_map/psum | solution.py:61
  867.7 128.2 %copy-start.11 = (bf16[96,896]{1,0:T(8,128)(2,1)S(1)}, bf16[96,896]{1,0:T(8,128)(2,1)}, u32[]{:S(2)}) copy-start(bf16[96,896]{1,0:T(8,128)(2,1)} %get-tuple-element.20) | copy-start | bytes 516100
  867.7 128.2 %copy-start.20 = (bf16[96,896]{1,0:T(8,128)(2,1)S(1)}, bf16[96,896]{1,0:T(8,128)(2,1)}, u32[]{:S(2)}) copy-start(bf16[96,896]{1,0:T(8,128)(2,1)} %get-tuple-element.21) | copy-start | bytes 516100
  931.0 67.1 %copy-start.16 = (bf16[4,6,512]{2,1,0:T(8,128)(2,1)S(1)}, bf16[4,6,512]{2,1,0:T(8,128)(2,1)}, u32[]{:S(2)}) copy-start(bf16[4,6,512]{2,1,0:T(8,128)(2,1)} %get-tuple-element.30) | copy-start | bytes 73732
  931.1 67.1 %copy-start.25 = (bf16[1,6,512]{2,0,1:T(2,128)(2,1)S(1)}, bf16[1,6,512]{2,0,1:T(2,128)(2,1)}, u32[]{:S(2)}) copy-start(bf16[1,6,512]{2,0,1:T(2,128)(2,1)} %get-tuple-element.40) | copy-start | bytes 18436
  931.1 67.1 %copy-start.35 = (bf16[6,512]{1,0:T(8,128)(2,1)S(1)}, bf16[6,512]{1,0:T(8,128)(2,1)}, u32[]{:S(2)}) copy-start(bf16[6,512]{1,0:T(8,128)(2,1)} %copy-done.34) | copy-start | bytes 18436
  981.4 16.2 %collective-permute-start.25 = (bf16[8,512]{1,0:T(8,128)(2,1)S(1)}, bf16[8,512]{1,0:T(8,128)(2,1)S(1)}, u32[]{:S(2)}, u32[]{:S(2)}) collective-permute-start(bf16[8,512]{1,0:T(8,128)(2,1)S(1)} %fusion.4), channel_id=1, source_target_pairs={{0,24},{8,32},{16,40},{24,48},{32,56},{40,64},{48,72},{56,80},{64,... | collective-permute-start | bytes 24584
  983.5 14.2 %collective-permute-start.24 = (bf16[8,512]{1,0:T(8,128)(2,1)S(1)}, bf16[8,512]{1,0:T(8,128)(2,1)S(1)}, u32[]{:S(2)}, u32[]{:S(2)}) collective-permute-start(bf16[8,512]{1,0:T(8,128)(2,1)S(1)} %fusion.4), channel_id=1, source_target_pairs={{0,16},{8,24},{16,32},{24,40},{32,48},{40,56},{48,64},{56,72},{64,... | collective-permute-start | bytes 24584
  984.8 12.9 collective-permute-start.23
  992.7 4.9 collective-permute-start.26
  998.2 37.6 %copy-start.12 = (bf16[96,896]{1,0:T(8,128)(2,1)S(1)}, bf16[96,896]{1,0:T(8,128)(2,1)}, u32[]{:S(2)}) copy-start(bf16[96,896]{1,0:T(8,128)(2,1)} %get-tuple-element.18) | copy-start | bytes 516100
  998.2 4.5 collective-permute-start.5
  1035.8 236.1 %all-reduce.29.cloned.1.call-start = ((), (), s32[]{:S(2)}) async-start(), calls=%async_computation | async-start | bytes 688128 | tf_op jit(solution)/shard_map/psum | solution.py:61
  1039.3 127.8 %copy-start.8 = (bf16[1,1,96,512]{3,1,0,2:T(2,128)(2,1)S(1)}, bf16[1,1,96,512]{3,1,0,2:T(2,128)(2,1)}, u32[]{:S(2)}) copy-start(bf16[1,1,96,512]{3,1,0,2:T(2,128)(2,1)} %copy-done.7) | copy-start | bytes 294916
  1039.3 127.8 %copy-start.13 = (bf16[96,896]{1,0:T(8,128)(2,1)S(1)}, bf16[96,896]{1,0:T(8,128)(2,1)}, u32[]{:S(2)}) copy-start(bf16[96,896]{1,0:T(8,128)(2,1)} %get-tuple-element.16) | copy-start | bytes 516100
  1039.3 127.8 %copy-start.22 = (bf16[96,896]{1,0:T(8,128)(2,1)S(1)}, bf16[96,896]{1,0:T(8,128)(2,1)}, u32[]{:S(2)}) copy-start(bf16[96,896]{1,0:T(8,128)(2,1)} %get-tuple-element.17) | copy-start | bytes 516100
  1152.4 21.5 %copy-start.28 = (bf16[1,6,512]{2,0,1:T(2,128)(2,1)S(1)}, bf16[1,6,512]{2,0,1:T(2,128)(2,1)}, u32[]{:S(2)}) copy-start(bf16[1,6,512]{2,0,1:T(2,128)(2,1)} %get-tuple-element.38) | copy-start | bytes 18436
  1152.4 16.4 %collective-permute-start.29 = (bf16[8,512]{1,0:T(8,128)(2,1)S(1)}, bf16[8,512]{1,0:T(8,128)(2,1)S(1)}, u32[]{:S(2)}, u32[]{:S(2)}) collective-permute-start(bf16[8,512]{1,0:T(8,128)(2,1)S(1)} %fusion.5), channel_id=1, source_target_pairs={{0,24},{8,32},{16,40},{24,48},{32,56},{40,64},{48,72},{56,80},{64,... | collective-permute-start | bytes 24584
  1154.6 14.2 %collective-permute-start.28 = (bf16[8,512]{1,0:T(8,128)(2,1)S(1)}, bf16[8,512]{1,0:T(8,128)(2,1)S(1)}, u32[]{:S(2)}, u32[]{:S(2)}) collective-permute-start(bf16[8,512]{1,0:T(8,128)(2,1)S(1)} %fusion.5), channel_id=1, source_target_pairs={{0,16},{8,24},{16,32},{24,40},{32,48},{40,56},{48,64},{56,72},{64,... | collective-permute-start | bytes 24584
  1155.9 12.9 collective-permute-start.27
  1163.8 5.0 collective-permute-start.30
  1169.3 37.5 %copy-start.14 = (bf16[96,896]{1,0:T(8,128)(2,1)S(1)}, bf16[96,896]{1,0:T(8,128)(2,1)}, u32[]{:S(2)}) copy-start(bf16[96,896]{1,0:T(8,128)(2,1)} %get-tuple-element.14) | copy-start | bytes 516100
  1169.3 4.5 collective-permute-start.6
  1271.9 68.0 %copy-start.9 = (bf16[96,896]{1,0:T(8,128)(2,1)S(1)}, bf16[96,896]{1,0:T(8,128)(2,1)}, u32[]{:S(2)}) copy-start(bf16[96,896]{1,0:T(8,128)(2,1)} %get-tuple-element.12) | copy-start | bytes 516100
  1271.9 68.0 %copy-start.23 = (bf16[96,896]{1,0:T(8,128)(2,1)S(1)}, bf16[96,896]{1,0:T(8,128)(2,1)}, u32[]{:S(2)}) copy-start(bf16[96,896]{1,0:T(8,128)(2,1)} %get-tuple-element.13) | copy-start | bytes 516100
  1324.8 22.7 %collective-permute-start.33 = (bf16[8,512]{1,0:T(8,128)(2,1)S(1)}, bf16[8,512]{1,0:T(8,128)(2,1)S(1)}, u32[]{:S(2)}, u32[]{:S(2)}) collective-permute-start(bf16[8,512]{1,0:T(8,128)(2,1)S(1)} %fusion.6), channel_id=1, source_target_pairs={{0,24},{8,32},{16,40},{24,48},{32,56},{40,64},{48,72},{56,80},{64,... | collective-permute-start | bytes 24584
  1326.8 20.8 %collective-permute-start.32 = (bf16[8,512]{1,0:T(8,128)(2,1)S(1)}, bf16[8,512]{1,0:T(8,128)(2,1)S(1)}, u32[]{:S(2)}, u32[]{:S(2)}) collective-permute-start(bf16[8,512]{1,0:T(8,128)(2,1)S(1)} %fusion.6), channel_id=1, source_target_pairs={{0,16},{8,24},{16,32},{24,40},{32,48},{40,56},{48,64},{56,72},{64,... | collective-permute-start | bytes 24584
  1328.2 19.4 %collective-permute-start.31 = (bf16[8,512]{1,0:T(8,128)(2,1)S(1)}, bf16[8,512]{1,0:T(8,128)(2,1)S(1)}, u32[]{:S(2)}, u32[]{:S(2)}) collective-permute-start(bf16[8,512]{1,0:T(8,128)(2,1)S(1)} %fusion.6), channel_id=1, source_target_pairs={{0,8},{8,16},{16,24},{24,32},{32,40},{40,48},{48,56},{56,64},{64,7... | collective-permute-start | bytes 24584
  1336.2 11.3 collective-permute-start.34
  (14 other events, 139.8 us)
Sparse Core Ops, SparseCore 0:
  90.6 74.2 all-reduce.40
  294.5 68.1 all-reduce.38
  490.3 68.5 all-reduce.36
  686.0 70.7 all-reduce.34
  864.2 65.4 all-reduce.32
  1035.9 64.8 all-reduce.30
  1207.0 64.8 all-reduce.28
where the time goes:
time: 1360 us
  blocking collectives  761 us (56%)
  waiting for transfers between devices  386 us (28%)
  starting transfers between devices  112 us (8%)
  matrix products  54.9 us (4%)
  between operations  28.8 us (2%)
    psum x7, waiting for transfers between devices, body(): lax.psum(up_part.astype(jnp.bfloat16), 'tensor').astype(jnp.float32)  378 us
    unnamed x7, blocking collectives  352 us
    all_gather x7, blocking collectives, body(): lax.all_gather(inputs, 'dp', axis=0, tiled=True)  208 us
    all_gather x7, blocking collectives, body(): lax.all_gather(arriving, 'dp', axis=0, tiled=True)  201 us
    unnamed x28, starting transfers between devices  102 us
    dot_general x14, matrix products, contract_rows(): lax.dot_general(left, right, (((0,), (0,)), ((), ())), preferred_element_...  29.7 us
  transfers between devices with their start and end apart: 42, of which 12 were waited for; matrix products, arithmetic and copies ran while one was open for 3% of the time, Pallas kernels for 0%

commit v1 on v0

v1 whole, which is shorter than its diff:
```python
import jax
import jax.numpy as jnp
from jax import lax
from jax.sharding import PartitionSpec as P

GROUPS = 1
BF16 = jnp.bfloat16
F32 = jnp.float32


def swap_cores(x):
    peers = lax.axis_size("dp")
    return lax.ppermute(x, "dp", [(i, i ^ 1) for i in range(peers)])


def chips_exchange(x):
    peers = lax.axis_size("dp")
    groups = [[i for i in range(peers) if i % 2 == core] for core in range(2)]
    return lax.all_to_all(x, "dp", 0, 0, axis_index_groups=groups, tiled=True)


def features_exchange(x):
    return lax.all_to_all(x, "tensor", 0, 0, tiled=True)


def copies(x, count):
    return jnp.broadcast_to(x[None], (count,) + x.shape)


def add_blocks(x):
    return jnp.sum(x.astype(F32), axis=0)


def by_cols(left, right):
    return lax.dot_general(
        left, right, (((left.ndim - 1,), (1,)), ((), ())), preferred_element_type=F32
    ).astype(BF16)


def by_rows(left, right):
    dims = tuple(range(left.ndim - 1))
    return lax.dot_general(left, right, ((dims, dims), ((), ())), preferred_element_type=F32)


def body(saved, pool, picked, w_up, w_down):
    segments = lax.axis_size("pipe")
    segment = lax.axis_index("pipe")
    chips = lax.axis_size("dp") // 2
    parts = lax.axis_size("tensor")
    micro_count, rows, width = saved.shape[1:]
    units = w_up.shape[2]
    size = micro_count // GROUPS
    block = size * rows

    up_w = jnp.concatenate([w_up[0], swap_cores(w_up[0])], axis=1)
    down_w = jnp.concatenate([w_down[0], swap_cores(w_down[0])], axis=0)

    full_in = chips_exchange(copies(saved[0].reshape(micro_count * rows, width), chips))
    up_part = lax.dot_general(
        full_in, up_w, (((2,), (0,)), ((), ())), preferred_element_type=F32
    ).astype(BF16)
    up = add_blocks(features_exchange(up_part))
    sig = jax.nn.sigmoid(up)
    hidden = (up * sig).astype(BF16)
    slope = (sig * (1.0 + up * (1.0 - sig))).reshape(GROUPS, block, 2 * units)

    fresh = jnp.stack(
        [lax.dynamic_index_in_dim(pool, picked[m], 0, keepdims=False) for m in range(micro_count)]
    ).reshape(GROUPS, block, width)

    pad = segments - 1
    slots = GROUPS + 2 * pad
    all_in = full_in.reshape(chips, GROUPS, block, width)
    kept_out = jnp.zeros((slots, block, width), BF16)
    kept_back = jnp.zeros((slots, chips, block, width), BF16)
    kept_d_up = jnp.zeros((slots, chips, block, 2 * units), BF16)
    carried = jnp.zeros((block, width), BF16)
    for tick in range(GROUPS + pad):
        group = tick - (pad - segment)
        slot = jnp.clip(group, 0, GROUPS - 1)
        last = lax.dynamic_index_in_dim(fresh, slot, 0, keepdims=False)
        if tick == 0:
            arriving = last
        else:
            pairs = [(i, i - 1) for i in range(1, segments)]
            received = lax.ppermute(carried, "pipe", pairs)
            arriving = jnp.where(segment == segments - 1, last, received)
        full_back = chips_exchange(copies(arriving, chips))
        back = add_blocks(features_exchange(by_cols(full_back, down_w)))
        here = lax.dynamic_index_in_dim(slope, slot, 0, keepdims=False)
        d_up = (back * here).astype(BF16)
        full_d_up = features_exchange(copies(d_up, parts))
        mixed = add_blocks(chips_exchange(by_cols(full_d_up, up_w)))
        carried = (arriving.astype(F32) + mixed).astype(BF16)
        kept_out = lax.dynamic_update_index_in_dim(kept_out, carried, group + pad, 0)
        kept_back = lax.dynamic_update_index_in_dim(kept_back, full_back, group + pad, 0)
        kept_d_up = lax.dynamic_update_index_in_dim(kept_d_up, full_d_up, group + pad, 0)

    grads_in = kept_out[pad : pad + GROUPS].reshape(micro_count, rows, width)
    all_back = kept_back[pad : pad + GROUPS]
    all_d_up = kept_d_up[pad : pad + GROUPS]
    full_hidden = features_exchange(copies(hidden, parts)).reshape(chips, GROUPS, block, 2 * units)
    all_in = jnp.swapaxes(all_in, 0, 1)
    full_hidden = jnp.swapaxes(full_hidden, 0, 1)

    grad_up = by_rows(all_in, all_d_up[..., :units]) + by_rows(
        swap_cores(all_in), swap_cores(all_d_up[..., units:])
    )
    grad_down = by_rows(full_hidden[..., :units], all_back) + by_rows(
        swap_cores(full_hidden[..., units:]), swap_cores(all_back)
    )
    return (grads_in[None], grad_up.astype(BF16)[None], grad_down.astype(BF16)[None])


def solution(mesh):
    return jax.shard_map(
        body,
        mesh=mesh,
        in_specs=(
            P("pipe", None, "dp", "tensor"),
            P(None, "dp", "tensor"),
            P(),
            P("pipe", "tensor", "dp"),
            P("pipe", "dp", "tensor"),
        ),
        out_specs=(
            P("pipe", None, "dp", "tensor"),
            P("pipe", "tensor", "dp"),
            P("pipe", "dp", "tensor"),
        ),
        check_vma=False,
    )
```

time: 1360 us -> 408 us (0.30)
  blocking collectives: 761 us -> 154 us
  waiting for transfers between devices: 386 us -> 94.6 us
  matrix products: 54.9 us -> 23.5 us
  between operations: 28.8 us -> 8.85 us
  starting transfers between devices: 112 us -> 94.2 us
    all_gather x14 -> x0, blocking collectives: 409 us -> none  [the longest x7 208 us: body(): lax.all_gather(inputs, 'dp', axis=0, tiled=True)]
    psum x7 -> x0, waiting for transfers between devices: 378 us -> none  [body(): lax.psum(up_part.astype(jnp.bfloat16), 'tensor').astype(jnp.float32)]
    unnamed x7 -> x0, blocking collectives: 352 us -> none
    all_to_all x0 -> x9, blocking collectives: none -> 154 us  [the longest x5 91.9 us: features_exchange(): return lax.all_to_all(x, 'tensor', 0, 0, tiled=True)]
    unnamed x28 -> x0, starting transfers between devices: 102 us -> none
    all_to_all x0 -> x10, waiting for transfers between devices: none -> 79.5 us  [the longest x5 46.2 us: features_exchange(): return lax.all_to_all(x, 'tensor', 0, 0, tiled=True)]
    all_to_all x0 -> x10, starting transfers between devices: none -> 45.2 us  [the longest x5 27.6 us: features_exchange(): return lax.all_to_all(x, 'tensor', 0, 0, tiled=True)]
    ppermute x7 -> x9, starting transfers between devices: 9.56 us -> 49 us  [the longest x6 45.1 us: swap_cores(): return lax.ppermute(x, 'dp', [(i, i ^ 1) for i in range(peers)])]
  transfers between devices with their start and end apart: 42 -> 19, of which waited for: 12 -> 12; matrix products, arithmetic and copies ran while one was open for 3% -> 9% of each run, Pallas kernels for 0% -> 0%
where the time goes in v1:
time: 408 us; the launch traced here: 400 us
  blocking collectives  154 us (38%)
  waiting for transfers between devices  94.6 us (23%)
  starting transfers between devices  94.2 us (23%)
  matrix products  23.5 us (6%)
  local copies, waits for them, and re-layouts  23.2 us (6%)
  between operations  8.85 us (2%)
    all_to_all x5, blocking collectives, features_exchange(): return lax.all_to_all(x, 'tensor', 0, 0, tiled=True)  91.9 us
    all_to_all x4, blocking collectives, chips_exchange(): return lax.all_to_all(x, 'dp', 0, 0, axis_index_groups=groups, tiled=True)  62.2 us
    all_to_all x5, waiting for transfers between devices, features_exchange(): return lax.all_to_all(x, 'tensor', 0, 0, tiled=True)  46.2 us
    ppermute x6, starting transfers between devices, swap_cores(): return lax.ppermute(x, 'dp', [(i, i ^ 1) for i in range(peers)])  45.1 us
    all_to_all x5, waiting for transfers between devices, chips_exchange(): return lax.all_to_all(x, 'dp', 0, 0, axis_index_groups=groups, tiled=True)  33.2 us
    all_to_all x5, starting transfers between devices, features_exchange(): return lax.all_to_all(x, 'tensor', 0, 0, tiled=True)  27.6 us
    all_to_all x5, starting transfers between devices, chips_exchange(): return lax.all_to_all(x, 'dp', 0, 0, axis_index_groups=groups, tiled=True)  17.6 us
    dot_general x8, matrix products, by_cols(): lax.dot_general(left, right, (((left.ndim - 1,), (1,)), ((), ())), prefer...  15.4 us
  transfers between devices with their start and end apart: 19, of which 12 were waited for; matrix products, arithmetic and copies ran while one was open for 9% of the time, Pallas kernels for 0%

profile of v1, /device:TPU:1, one launch (start us, length us, event | category | flops | bytes accessed | tf_op | source)
XLA Modules:
  0.0 400.0 jit_solution(16542503068334656735)
XLA Ops:
  0.6 8.8 %collective-permute-start = (bf16[896,512]{1,0:T(8,128)(2,1)}, bf16[896,512]{1,0:T(8,128)(2,1)}, u32[]{:S(2)}, u32[]{:S(2)}) collective-permute-start(bf16[896,512]{1,0:T(8,128)(2,1)} %bitcast.113), channel_id=1, source_target_pairs={{0,8},{8,0},{16,24},{24,16},{32,40},{40,32},{48,56},{56,48},{64,72... | collective-permute-start | bytes 2752520 | tf_op jit(solution)/shard_map/ppermute | solution.py:13
  9.4 1.4 fusion.17
  18.6 1.0 constant_dynamic-slice_fusion
  20.4 3.9 all-to-all-start
  25.0 9.8 %all-to-all-done = bf16[8,24,512]{2,1,0:T(8,128)(2,1)S(1)} async-done(((bf16[8,24,512]{2,1,0:T(8,128)(2,1)}), bf16[8,24,512]{2,1,0:T(8,128)(2,1)S(1)}, u32[]{:S(2)}, u32[]{:S(2)}) %all-to-all-start) | async-done | bytes 196640 | tf_op jit(solution)/shard_map/all_to_all | solution.py:19
  35.5 3.4 all-to-all-start.2
  38.9 3.1 collective-permute-start.1
  42.0 3.1 convolution_convert_fusion.4
  45.0 3.5 all-to-all-done.2
  48.5 10.0 %all-to-all-start.1 = ((bf16[8,24,1792]{2,1,0:T(8,128)(2,1)}), bf16[8,24,1792]{2,1,0:T(8,128)(2,1)S(1)}, u32[]{:S(2)}, u32[]{:S(2)}) async-start(bf16[8,24,1792]{2,1,0:T(8,128)(2,1)} %convolution_convert_fusion.4), calls=%async_computation.1 | async-start | bytes 1376256 | tf_op jit(solution)/shard_map/all_to_all | solution.py:23
  58.6 1.4 fusion
  60.0 17.5 %all-to-all-done.1 = bf16[8,24,1792]{2,1,0:T(8,128)(2,1)S(1)} async-done(((bf16[8,24,1792]{2,1,0:T(8,128)(2,1)}), bf16[8,24,1792]{2,1,0:T(8,128)(2,1)S(1)}, u32[]{:S(2)}, u32[]{:S(2)}) %all-to-all-start.1) | async-done | bytes 688160 | tf_op jit(solution)/shard_map/all_to_all | solution.py:23
  77.5 3.5 all-to-all-start.3
  81.2 18.4 %all-to-all-done.3 = bf16[8,24,1792]{2,1,0:T(8,128)(2,1)S(1)} async-done(((bf16[8,24,1792]{2,1,0:T(8,128)(2,1)}), bf16[8,24,1792]{2,1,0:T(8,128)(2,1)S(1)}, u32[]{:S(2)}, u32[]{:S(2)}) %all-to-all-start.3) | async-done | bytes 688160 | tf_op jit(solution)/shard_map/all_to_all | solution.py:23
  99.8 19.6 %all_to_all.95 = bf16[8,24,1792]{2,1,0:T(8,128)(2,1)S(1)} all-to-all(bf16[8,24,1792]{2,1,0:T(8,128)(2,1)S(1)} %broadcast_in_dim.120), channel_id=1, replica_groups=mesh['pipe'=4,'dp'=16,'tensor'=8] {'tensor'}, dimensions={0} | all-to-all | bytes 1376256 | tf_op jit(solution)/shard_map/all_to_all | solution.py:23
  120.1 25.1 %all_to_all.96 = bf16[8,24,512]{2,1,0:T(8,128)(2,1)S(1)} all-to-all(bf16[8,24,512]{2,1,0:T(8,128)(2,1)S(1)} %convolution_convert_fusion.8), channel_id=1, replica_groups={{0,16,32,48,64,80,96,112},{8,24,40,56,72,88,104,120},{1,17,33,49,65,81,..., dimensions={0} | all-to-all | bytes 393216 | tf_op jit(solution)/shard_map/all_to_all | solution.py:19
  145.3 1.3 collective-permute-start.2
  146.6 5.1 %collective-permute-done.2 = bf16[24,512]{1,0:T(8,128)(2,1)S(1)} collective-permute-done((bf16[24,512]{1,0:T(8,128)(2,1)S(1)}, bf16[24,512]{1,0:T(8,128)(2,1)S(1)}, u32[]{:S(2)}, u32[]{:S(2)}) %collective-permute-start.2) | collective-permute-done | bytes 24608 | tf_op jit(solution)/shard_map/ppermute | solution.py:86
  151.7 12.1 %all_to_all.97 = bf16[8,24,512]{2,1,0:T(8,128)(2,1)S(1)} all-to-all(bf16[8,24,512]{2,1,0:T(8,128)(2,1)S(1)} %broadcast_in_dim.121), channel_id=1, replica_groups={{0,16,32,48,64,80,96,112},{8,24,40,56,72,88,104,120},{1,17,33,49,65,81,..., dimensions={0} | all-to-all | bytes 393216 | tf_op jit(solution)/shard_map/all_to_all | solution.py:19
  163.8 1.9 convolution_convert_fusion.2
  165.7 19.5 %all_to_all.98 = bf16[8,24,1792]{2,1,0:T(8,128)(2,1)S(1)} all-to-all(bf16[8,24,1792]{2,1,0:T(8,128)(2,1)S(1)} %convolution_convert_fusion.2), channel_id=1, replica_groups=mesh['pipe'=4,'dp'=16,'tensor'=8] {'tensor'}, dimensions={0} | all-to-all | bytes 1376256 | tf_op jit(solution)/shard_map/all_to_all | solution.py:23
  185.4 19.7 %all_to_all.99 = bf16[8,24,1792]{2,1,0:T(8,128)(2,1)S(1)} all-to-all(bf16[8,24,1792]{2,1,0:T(8,128)(2,1)S(1)} %broadcast_in_dim.122), channel_id=1, replica_groups=mesh['pipe'=4,'dp'=16,'tensor'=8] {'tensor'}, dimensions={0} | all-to-all | bytes 1376256 | tf_op jit(solution)/shard_map/all_to_all | solution.py:23
  205.2 1.4 convolution_convert_fusion.7
  206.6 3.4 all-to-all-start.9
  210.1 9.6 %all-to-all-done.9 = bf16[8,24,512]{2,1,0:T(8,128)(2,1)S(1)} async-done(((bf16[8,24,512]{2,1,0:T(8,128)(2,1)}), bf16[8,24,512]{2,1,0:T(8,128)(2,1)S(1)}, u32[]{:S(2)}, u32[]{:S(2)}) %all-to-all-start.9) | async-done | bytes 196640 | tf_op jit(solution)/shard_map/all_to_all | solution.py:19
  219.7 1.3 collective-permute-start.3
  221.0 6.1 %collective-permute-done.3 = bf16[24,512]{1,0:T(8,128)(2,1)S(1)} collective-permute-done((bf16[24,512]{1,0:T(8,128)(2,1)S(1)}, bf16[24,512]{1,0:T(8,128)(2,1)S(1)}, u32[]{:S(2)}, u32[]{:S(2)}) %collective-permute-start.3) | collective-permute-done | bytes 24608 | tf_op jit(solution)/shard_map/ppermute | solution.py:86
  227.2 12.2 %all_to_all.100 = bf16[8,24,512]{2,1,0:T(8,128)(2,1)S(1)} all-to-all(bf16[8,24,512]{2,1,0:T(8,128)(2,1)S(1)} %broadcast_in_dim.124), channel_id=1, replica_groups={{0,16,32,48,64,80,96,112},{8,24,40,56,72,88,104,120},{1,17,33,49,65,81,..., dimensions={0} | all-to-all | bytes 393216 | tf_op jit(solution)/shard_map/all_to_all | solution.py:19
  239.4 2.2 convolution_convert_fusion.1
  241.6 16.6 %all_to_all.101 = bf16[8,24,1792]{2,1,0:T(8,128)(2,1)S(1)} all-to-all(bf16[8,24,1792]{2,1,0:T(8,128)(2,1)S(1)} %convolution_convert_fusion.1), channel_id=1, replica_groups=mesh['pipe'=4,'dp'=16,'tensor'=8] {'tensor'}, dimensions={0} | all-to-all | bytes 1376256 | tf_op jit(solution)/shard_map/all_to_all | solution.py:23
  258.4 16.5 %all_to_all.102 = bf16[8,24,1792]{2,1,0:T(8,128)(2,1)S(1)} all-to-all(bf16[8,24,1792]{2,1,0:T(8,128)(2,1)S(1)} %broadcast_in_dim.125), channel_id=1, replica_groups=mesh['pipe'=4,'dp'=16,'tensor'=8] {'tensor'}, dimensions={0} | all-to-all | bytes 1376256 | tf_op jit(solution)/shard_map/all_to_all | solution.py:23
  274.9 1.4 convolution_convert_fusion.6
  276.4 3.4 all-to-all-start.13
  279.8 9.7 %all-to-all-done.13 = bf16[8,24,512]{2,1,0:T(8,128)(2,1)S(1)} async-done(((bf16[8,24,512]{2,1,0:T(8,128)(2,1)}), bf16[8,24,512]{2,1,0:T(8,128)(2,1)S(1)}, u32[]{:S(2)}, u32[]{:S(2)}) %all-to-all-start.13) | async-done | bytes 196640 | tf_op jit(solution)/shard_map/all_to_all | solution.py:19
  289.6 1.3 collective-permute-start.4
  290.9 3.9 collective-permute-done.4
  294.8 12.8 %all_to_all.103 = bf16[8,24,512]{2,1,0:T(8,128)(2,1)} all-to-all(bf16[8,24,512]{2,1,0:T(8,128)(2,1)S(1)} %broadcast_in_dim.127), channel_id=1, replica_groups={{0,16,32,48,64,80,96,112},{8,24,40,56,72,88,104,120},{1,17,33,49,65,81,..., dimensions={0} | all-to-all | bytes 393216 | tf_op jit(solution)/shard_map/all_to_all | solution.py:19
  307.6 0.9 broadcast_in_dim.136
  308.6 3.5 all-to-all-start.18
  312.1 15.0 %collective-permute-start.6 = (bf16[1,8,24,512]{3,2,1,0:T(8,128)(2,1)}, bf16[1,8,24,512]{3,2,1,0:T(8,128)(2,1)}, u32[]{:S(2)}, u32[]{:S(2)}) collective-permute-start(bf16[1,8,24,512]{3,2,1,0:T(8,128)(2,1)} %bitcast.112), channel_id=1, source_target_pairs={{0,8},{8,0},{16,24},{24,16},{32,40},{40,32},{48,56},{56,48},{64,72... | collective-permute-start | bytes 589832 | tf_op jit(solution)/shard_map/ppermute | solution.py:13
  327.1 1.2 broadcast_in_dim.137
  329.0 3.2 convolution_convert_fusion
  333.1 6.8 %all-to-all-start.15 = ((bf16[8,24,1792]{2,1,0:T(8,128)(2,1)}), bf16[8,24,1792]{2,1,0:T(8,128)(2,1)S(1)}, u32[]{:S(2)}, u32[]{:S(2)}) async-start(bf16[8,24,1792]{2,1,0:T(8,128)(2,1)} %convolution_convert_fusion), calls=%async_computation.15 | async-start | bytes 1376256 | tf_op jit(solution)/shard_map/all_to_all | solution.py:23
  339.9 2.5 broadcast_in_dim.130
  342.4 0.9 bitcast_dynamic-update-slice_fusion.3
  344.8 6.6 %collective-permute-start.7 = (bf16[1,8,24,896]{3,2,1,0:T(8,128)(2,1)}, bf16[1,8,24,896]{3,2,1,0:T(8,128)(2,1)}, u32[]{:S(2)}, u32[]{:S(2)}) collective-permute-start(bf16[1,8,24,896]{3,2,1,0:T(8,128)(2,1)} %slice.48), channel_id=1, source_target_pairs={{0,8},{8,0},{16,24},{24,16},{32,40},{40,32},{48,56},{56,48},{64,72... | collective-permute-start | bytes 1032200 | tf_op jit(solution)/shard_map/ppermute | solution.py:13
  351.4 0.9 bitcast_dynamic-update-slice_fusion.2
  353.0 4.7 %all-to-all-done.15 = bf16[8,24,1792]{2,1,0:T(8,128)(2,1)S(1)} async-done(((bf16[8,24,1792]{2,1,0:T(8,128)(2,1)}), bf16[8,24,1792]{2,1,0:T(8,128)(2,1)S(1)}, u32[]{:S(2)}, u32[]{:S(2)}) %all-to-all-start.15) | async-done | bytes 688160 | tf_op jit(solution)/shard_map/all_to_all | solution.py:23
  357.9 0.9 broadcast_in_dim.128
  358.8 3.7 all-to-all-start.16
  362.5 0.9 bitcast_dynamic-update-slice_fusion.1
  364.1 0.9 slice.47
  365.0 6.1 %collective-permute-start.8 = (bf16[1,8,24,512]{3,2,1,0:T(8,128)(2,1)S(1)}, bf16[1,8,24,512]{3,2,1,0:T(8,128)(2,1)S(1)}, u32[]{:S(2)}, u32[]{:S(2)}) collective-permute-start(bf16[1,8,24,512]{3,2,1,0:T(8,128)(2,1)S(1)} %slice.47), channel_id=1, source_target_pairs={{0,8},{8,0},{16,24},{24,16},{32,40},{40,32},{48,56},{56,48},{64,72... | collective-permute-start | bytes 589832 | tf_op jit(solution)/shard_map/ppermute | solution.py:13
  371.1 1.4 fusion.5
  372.6 2.5 fusion.4
  375.0 5.7 %all-to-all-done.16 = bf16[8,24,1792]{2,1,0:T(8,128)(2,1)S(1)} async-done(((bf16[8,24,1792]{2,1,0:T(8,128)(2,1)}), bf16[8,24,1792]{2,1,0:T(8,128)(2,1)S(1)}, u32[]{:S(2)}, u32[]{:S(2)}) %all-to-all-start.16) | async-done | bytes 688160 | tf_op jit(solution)/shard_map/all_to_all | solution.py:23
  380.7 1.4 convolution_convert_fusion.5
  382.1 3.5 all-to-all-start.17
  385.7 0.9 bitcast_dynamic-update-slice_fusion
  386.6 1.0 slice.45
  387.6 5.6 %collective-permute-start.5 = (bf16[1,8,24,896]{3,2,1,0:T(8,128)(2,1)S(1)}, bf16[1,8,24,896]{3,2,1,0:T(8,128)(2,1)S(1)}, u32[]{:S(2)}, u32[]{:S(2)}) collective-permute-start(bf16[1,8,24,896]{3,2,1,0:T(8,128)(2,1)S(1)} %slice.45), channel_id=1, source_target_pairs={{0,8},{8,0},{16,24},{24,16},{32,40},{40,32},{48,56},{56,48},{64,72... | collective-permute-start | bytes 1032200 | tf_op jit(solution)/shard_map/ppermute | solution.py:13
  393.2 1.4 fusion.6
  397.4 1.4 fusion.3
  398.7 1.3 copy.20
  (95 shorter events, 11.3 us)
Async XLA Ops:
  0.6 41.4 %collective-permute-start = (bf16[896,512]{1,0:T(8,128)(2,1)}, bf16[896,512]{1,0:T(8,128)(2,1)}, u32[]{:S(2)}, u32[]{:S(2)}) collective-permute-start(bf16[896,512]{1,0:T(8,128)(2,1)} %bitcast.113), channel_id=1, source_target_pairs={{0,8},{8,0},{16,24},{24,16},{32,40},{40,32},{48,56},{56,48},{64,72... | collective-permute-start | bytes 2752520 | tf_op jit(solution)/shard_map/ppermute | solution.py:13
  20.4 14.4 %all-to-all-start = ((bf16[8,24,512]{2,1,0:T(8,128)(2,1)}), bf16[8,24,512]{2,1,0:T(8,128)(2,1)S(1)}, u32[]{:S(2)}, u32[]{:S(2)}) async-start(bf16[8,24,512]{2,1,0:T(8,128)(2,1)} %broadcast_in_dim.117), calls=%async_computation | async-start | bytes 393216 | tf_op jit(solution)/shard_map/all_to_all | solution.py:19
  35.5 13.0 %all-to-all-start.2 = ((bf16[8,24,512]{2,1,0:T(8,128)(2,1)}), bf16[8,24,512]{2,1,0:T(8,128)(2,1)S(1)}, u32[]{:S(2)}, u32[]{:S(2)}) async-start(bf16[8,24,512]{2,1,0:T(8,128)(2,1)} %broadcast_in_dim.119), calls=%async_computation.2 | async-start | bytes 393216 | tf_op jit(solution)/shard_map/all_to_all | solution.py:19
  38.9 19.7 %copy-start.10 = (bf16[1,512,896]{2,1,0:T(8,128)(2,1)S(1)}, bf16[1,512,896]{2,1,0:T(8,128)(2,1)}, u32[]{:S(2)}) copy-start(bf16[1,512,896]{2,1,0:T(8,128)(2,1)} %param.8) | copy-start | bytes 2752516
  38.9 19.7 %collective-permute-start.1 = (bf16[512,896]{1,0:T(8,128)(2,1)}, bf16[512,896]{1,0:T(8,128)(2,1)S(1)}, u32[]{:S(2)}, u32[]{:S(2)}) collective-permute-start(bf16[512,896]{1,0:T(8,128)(2,1)} %bitcast.118), channel_id=1, source_target_pairs={{0,8},{8,0},{16,24},{24,16},{32,40},{40,32},{48,56},{56,48},{64,72... | collective-permute-start | bytes 2752520 | tf_op jit(solution)/shard_map/ppermute | solution.py:13
  48.5 29.0 %copy-start.7 = (bf16[8,24,512]{2,1,0:T(8,128)(2,1)}, bf16[8,24,512]{2,1,0:T(8,128)(2,1)S(1)}, u32[]{:S(2)}) copy-start(bf16[8,24,512]{2,1,0:T(8,128)(2,1)S(1)} %all-to-all-done.2) | copy-start | bytes 589828
  48.5 29.0 %all-to-all-start.1 = ((bf16[8,24,1792]{2,1,0:T(8,128)(2,1)}), bf16[8,24,1792]{2,1,0:T(8,128)(2,1)S(1)}, u32[]{:S(2)}, u32[]{:S(2)}) async-start(bf16[8,24,1792]{2,1,0:T(8,128)(2,1)} %convolution_convert_fusion.4), calls=%async_computation.1 | async-start | bytes 1376256 | tf_op jit(solution)/shard_map/all_to_all | solution.py:23
  58.6 1.5 copy-start.15
  77.5 22.0 %all-to-all-start.3 = ((bf16[8,24,1792]{2,1,0:T(8,128)(2,1)}), bf16[8,24,1792]{2,1,0:T(8,128)(2,1)S(1)}, u32[]{:S(2)}, u32[]{:S(2)}) async-start(bf16[8,24,1792]{2,1,0:T(8,128)(2,1)} %fusion), calls=%async_computation.3 | async-start | bytes 1376256 | tf_op jit(solution)/shard_map/all_to_all | solution.py:23
  99.5 19.9 %copy-start.11 = (bf16[1,512,896]{2,1,0:T(8,128)(2,1)S(1)}, bf16[1,512,896]{2,1,0:T(8,128)(2,1)}, u32[]{:S(2)}) copy-start(bf16[1,512,896]{2,1,0:T(8,128)(2,1)} %param.8) | copy-start | bytes 2752516
  99.5 19.9 %copy-start.16 = (bf16[512,896]{1,0:T(8,128)(2,1)S(1)}, bf16[512,896]{1,0:T(8,128)(2,1)}, u32[]{:S(2)}) copy-start(bf16[512,896]{1,0:T(8,128)(2,1)} %copy-done.15) | copy-start | bytes 2752516
  119.4 44.4 %copy-start.9 = (bf16[1,896,512]{2,1,0:T(8,128)(2,1)S(1)}, bf16[1,896,512]{2,1,0:T(8,128)(2,1)}, u32[]{:S(2)}) copy-start(bf16[1,896,512]{2,1,0:T(8,128)(2,1)} %param.9) | copy-start | bytes 2752516
  145.3 6.4 %collective-permute-start.2 = (bf16[24,512]{1,0:T(8,128)(2,1)S(1)}, bf16[24,512]{1,0:T(8,128)(2,1)S(1)}, u32[]{:S(2)}, u32[]{:S(2)}) collective-permute-start(bf16[24,512]{1,0:T(8,128)(2,1)S(1)} %add_convert_fusion.3), channel_id=1, source_target_pairs={{128,0},{256,128},{384,256},{129,1},{257,129},{385,257},{130,2},{2... | collective-permute-start | bytes 73736 | tf_op jit(solution)/shard_map/ppermute | solution.py:86
  185.2 20.0 %copy-start.12 = (bf16[1,512,896]{2,1,0:T(8,128)(2,1)S(1)}, bf16[1,512,896]{2,1,0:T(8,128)(2,1)}, u32[]{:S(2)}) copy-start(bf16[1,512,896]{2,1,0:T(8,128)(2,1)} %param.8) | copy-start | bytes 2752516
  185.2 20.0 %copy-start.17 = (bf16[512,896]{1,0:T(8,128)(2,1)S(1)}, bf16[512,896]{1,0:T(8,128)(2,1)}, u32[]{:S(2)}) copy-start(bf16[512,896]{1,0:T(8,128)(2,1)} %copy-done.15) | copy-start | bytes 2752516
  206.6 13.0 %all-to-all-start.9 = ((bf16[8,24,512]{2,1,0:T(8,128)(2,1)}), bf16[8,24,512]{2,1,0:T(8,128)(2,1)S(1)}, u32[]{:S(2)}, u32[]{:S(2)}) async-start(bf16[8,24,512]{2,1,0:T(8,128)(2,1)} %convolution_convert_fusion.7), calls=%async_computation.9 | async-start | bytes 393216 | tf_op jit(solution)/shard_map/all_to_all | solution.py:19
  219.7 7.4 %collective-permute-start.3 = (bf16[24,512]{1,0:T(8,128)(2,1)S(1)}, bf16[24,512]{1,0:T(8,128)(2,1)S(1)}, u32[]{:S(2)}, u32[]{:S(2)}) collective-permute-start(bf16[24,512]{1,0:T(8,128)(2,1)S(1)} %get-tuple-element.15), channel_id=1, source_target_pairs={{128,0},{256,128},{384,256},{129,1},{257,129},{385,257},{130,2},{2... | collective-permute-start | bytes 73736 | tf_op jit(solution)/shard_map/ppermute | solution.py:86
  258.2 16.8 %copy-start.13 = (bf16[1,512,896]{2,1,0:T(8,128)(2,1)S(1)}, bf16[1,512,896]{2,1,0:T(8,128)(2,1)}, u32[]{:S(2)}) copy-start(bf16[1,512,896]{2,1,0:T(8,128)(2,1)} %param.8) | copy-start | bytes 2752516
  258.2 16.8 %copy-start.18 = (bf16[512,896]{1,0:T(8,128)(2,1)S(1)}, bf16[512,896]{1,0:T(8,128)(2,1)}, u32[]{:S(2)}) copy-start(bf16[512,896]{1,0:T(8,128)(2,1)} %copy-done.15) | copy-start | bytes 2752516
  276.4 13.2 %all-to-all-start.13 = ((bf16[8,24,512]{2,1,0:T(8,128)(2,1)}), bf16[8,24,512]{2,1,0:T(8,128)(2,1)S(1)}, u32[]{:S(2)}, u32[]{:S(2)}) async-start(bf16[8,24,512]{2,1,0:T(8,128)(2,1)} %convolution_convert_fusion.6), calls=%async_computation.13 | async-start | bytes 393216 | tf_op jit(solution)/shard_map/all_to_all | solution.py:19
  289.6 19.0 %copy-start.4 = (bf16[7,24,512]{2,1,0:T(8,128)(2,1)}, bf16[7,24,512]{2,1,0:T(8,128)(2,1)S(1)}, u32[]{:S(2)}) copy-start(bf16[7,24,512]{2,1,0:T(8,128)(2,1)S(1)} %get-tuple-element.12) | copy-start | bytes 516100
  289.6 5.2 %collective-permute-start.4 = (bf16[24,512]{1,0:T(8,128)(2,1)S(1)}, bf16[24,512]{1,0:T(8,128)(2,1)S(1)}, u32[]{:S(2)}, u32[]{:S(2)}) collective-permute-start(bf16[24,512]{1,0:T(8,128)(2,1)S(1)} %get-tuple-element.13), channel_id=1, source_target_pairs={{128,0},{256,128},{384,256},{129,1},{257,129},{385,257},{130,2},{2... | collective-permute-start | bytes 73736 | tf_op jit(solution)/shard_map/ppermute | solution.py:86
  294.8 13.8 %copy-start.5 = (bf16[24,512]{1,0:T(8,128)(2,1)}, bf16[24,512]{1,0:T(8,128)(2,1)S(1)}, u32[]{:S(2)}) copy-start(bf16[24,512]{1,0:T(8,128)(2,1)S(1)} %broadcast_select_fusion) | copy-start | bytes 73732
  308.6 23.6 %all-to-all-start.18 = ((bf16[8,24,1792]{2,1,0:T(8,128)(2,1)}), bf16[8,24,1792]{2,1,0:T(8,128)(2,1)S(1)}, u32[]{:S(2)}, u32[]{:S(2)}) async-start(bf16[8,24,1792]{2,1,0:T(8,128)(2,1)} %broadcast_in_dim.136), calls=%async_computation.18 | async-start | bytes 1376256 | tf_op jit(solution)/shard_map/all_to_all | solution.py:23
  312.1 85.2 %collective-permute-start.6 = (bf16[1,8,24,512]{3,2,1,0:T(8,128)(2,1)}, bf16[1,8,24,512]{3,2,1,0:T(8,128)(2,1)}, u32[]{:S(2)}, u32[]{:S(2)}) collective-permute-start(bf16[1,8,24,512]{3,2,1,0:T(8,128)(2,1)} %bitcast.112), channel_id=1, source_target_pairs={{0,8},{8,0},{16,24},{24,16},{32,40},{40,32},{48,56},{56,48},{64,72... | collective-permute-start | bytes 589832 | tf_op jit(solution)/shard_map/ppermute | solution.py:13
  332.2 0.9 copy-start
  333.1 24.6 %all-to-all-start.15 = ((bf16[8,24,1792]{2,1,0:T(8,128)(2,1)}), bf16[8,24,1792]{2,1,0:T(8,128)(2,1)S(1)}, u32[]{:S(2)}, u32[]{:S(2)}) async-start(bf16[8,24,1792]{2,1,0:T(8,128)(2,1)} %convolution_convert_fusion), calls=%async_computation.15 | async-start | bytes 1376256 | tf_op jit(solution)/shard_map/all_to_all | solution.py:23
  342.4 1.6 copy-start.1
  344.8 27.7 %collective-permute-start.7 = (bf16[1,8,24,896]{3,2,1,0:T(8,128)(2,1)}, bf16[1,8,24,896]{3,2,1,0:T(8,128)(2,1)}, u32[]{:S(2)}, u32[]{:S(2)}) collective-permute-start(bf16[1,8,24,896]{3,2,1,0:T(8,128)(2,1)} %slice.48), channel_id=1, source_target_pairs={{0,8},{8,0},{16,24},{24,16},{32,40},{40,32},{48,56},{56,48},{64,72... | collective-permute-start | bytes 1032200 | tf_op jit(solution)/shard_map/ppermute | solution.py:13
  357.9 5.5 %copy-start.3 = (bf16[8,24,512]{2,1,0:T(8,128)(2,1)S(1)}, bf16[8,24,512]{2,1,0:T(8,128)(2,1)}, u32[]{:S(2)}) copy-start(bf16[8,24,512]{2,1,0:T(8,128)(2,1)} %all_to_all.103) | copy-start | bytes 589828
  358.8 12.3 %copy-start.2 = (bf16[8,24,1792]{2,1,0:T(8,128)(2,1)S(1)}, bf16[8,24,1792]{2,1,0:T(8,128)(2,1)}, u32[]{:S(2)}) copy-start(bf16[8,24,1792]{2,1,0:T(8,128)(2,1)} %copy-done) | copy-start | bytes 2064388
  358.8 21.9 %all-to-all-start.16 = ((bf16[8,24,1792]{2,1,0:T(8,128)(2,1)}), bf16[8,24,1792]{2,1,0:T(8,128)(2,1)S(1)}, u32[]{:S(2)}, u32[]{:S(2)}) async-start(bf16[8,24,1792]{2,1,0:T(8,128)(2,1)} %broadcast_in_dim.128), calls=%async_computation.16 | async-start | bytes 1376256 | tf_op jit(solution)/shard_map/all_to_all | solution.py:23
  365.0 7.5 %collective-permute-start.8 = (bf16[1,8,24,512]{3,2,1,0:T(8,128)(2,1)S(1)}, bf16[1,8,24,512]{3,2,1,0:T(8,128)(2,1)S(1)}, u32[]{:S(2)}, u32[]{:S(2)}) collective-permute-start(bf16[1,8,24,512]{3,2,1,0:T(8,128)(2,1)S(1)} %slice.47), channel_id=1, source_target_pairs={{0,8},{8,0},{16,24},{24,16},{32,40},{40,32},{48,56},{56,48},{64,72... | collective-permute-start | bytes 589832 | tf_op jit(solution)/shard_map/ppermute | solution.py:13
  372.5 8.2 %copy-start.14 = (bf16[1,512,896]{2,1,0:T(8,128)(2,1)S(1)}, bf16[1,512,896]{2,1,0:T(8,128)(2,1)}, u32[]{:S(2)}) copy-start(bf16[1,512,896]{2,1,0:T(8,128)(2,1)} %param.8) | copy-start | bytes 2752516
  372.5 8.2 %copy-start.19 = (bf16[512,896]{1,0:T(8,128)(2,1)S(1)}, bf16[512,896]{1,0:T(8,128)(2,1)}, u32[]{:S(2)}) copy-start(bf16[512,896]{1,0:T(8,128)(2,1)} %copy-done.15) | copy-start | bytes 2752516
  382.1 11.1 %copy-start.8 = (bf16[8,24,512]{2,1,0:T(8,128)(2,1)S(1)}, bf16[8,24,512]{2,1,0:T(8,128)(2,1)}, u32[]{:S(2)}) copy-start(bf16[8,24,512]{2,1,0:T(8,128)(2,1)} %copy-done.7) | copy-start | bytes 589828
  382.1 13.2 %all-to-all-start.17 = ((bf16[8,24,512]{2,1,0:T(8,128)(2,1)}), bf16[8,24,512]{2,1,0:T(8,128)(2,1)S(1)}, u32[]{:S(2)}, u32[]{:S(2)}) async-start(bf16[8,24,512]{2,1,0:T(8,128)(2,1)} %convolution_convert_fusion.5), calls=%async_computation.17 | async-start | bytes 393216 | tf_op jit(solution)/shard_map/all_to_all | solution.py:19
  387.6 7.8 %copy-start.6 = (bf16[24,512]{1,0:T(8,128)(2,1)S(1)}, bf16[24,512]{1,0:T(8,128)(2,1)}, u32[]{:S(2)}) copy-start(bf16[24,512]{1,0:T(8,128)(2,1)} %copy-done.5) | copy-start | bytes 73732
  387.6 9.8 %collective-permute-start.5 = (bf16[1,8,24,896]{3,2,1,0:T(8,128)(2,1)S(1)}, bf16[1,8,24,896]{3,2,1,0:T(8,128)(2,1)S(1)}, u32[]{:S(2)}, u32[]{:S(2)}) collective-permute-start(bf16[1,8,24,896]{3,2,1,0:T(8,128)(2,1)S(1)} %slice.45), channel_id=1, source_target_pairs={{0,8},{8,0},{16,24},{24,16},{32,40},{40,32},{48,56},{56,48},{64,72... | collective-permute-start | bytes 1032200 | tf_op jit(solution)/shard_map/ppermute | solution.py:13

commit v2 on v1

v2 whole, which is shorter than its diff:
```python
import jax
import jax.numpy as jnp
from jax import lax
from jax.sharding import PartitionSpec as P

BF16 = jnp.bfloat16
F32 = jnp.float32


def swap_cores(x):
    peers = lax.axis_size("dp")
    return lax.ppermute(x, "dp", [(i, i ^ 1) for i in range(peers)])


def chips_exchange(x):
    peers = lax.axis_size("dp")
    groups = [[i for i in range(peers) if i % 2 == core] for core in range(2)]
    return lax.all_to_all(x, "dp", 0, 0, axis_index_groups=groups, tiled=True)


def features_exchange(x):
    return lax.all_to_all(x, "tensor", 0, 0, tiled=True)


def copies(x, count):
    return jnp.broadcast_to(x[None], (count,) + x.shape)


def add_blocks(x):
    return jnp.sum(x.astype(F32), axis=0)


def by_cols(left, right):
    return lax.dot_general(
        left, right, (((left.ndim - 1,), (1,)), ((), ())), preferred_element_type=F32
    ).astype(BF16)


def by_rows(left, right):
    dims = tuple(range(left.ndim - 1))
    return lax.dot_general(left, right, ((dims, dims), ((), ())), preferred_element_type=F32)


def body(saved, pool, picked, w_up, w_down):
    segments = lax.axis_size("pipe")
    segment = lax.axis_index("pipe")
    chips = lax.axis_size("dp") // 2
    parts = lax.axis_size("tensor")
    micro_count, rows, width = saved.shape[1:]
    units = w_up.shape[2]
    block = micro_count * rows
    last = segments - 1

    up_w = jnp.concatenate([w_up[0], swap_cores(w_up[0])], axis=1)
    down_w = jnp.concatenate([w_down[0], swap_cores(w_down[0])], axis=0)

    fresh = jnp.zeros((micro_count, rows, width), BF16)
    for sample in range(pool.shape[0]):
        fresh = jnp.where((picked == sample)[:, None, None], pool[sample][None], fresh)
    fresh = fresh.reshape(block, width)

    gathered = chips_exchange(
        copies(jnp.concatenate([saved[0].reshape(block, width), fresh], axis=0), chips)
    )
    full_in = gathered[:, :block]
    full_back = gathered[:, block:]
    up_part = lax.dot_general(
        full_in, up_w, (((2,), (0,)), ((), ())), preferred_element_type=F32
    ).astype(BF16)
    back_part = by_cols(full_back, down_w)
    sums = add_blocks(features_exchange(jnp.concatenate([up_part, back_part], axis=1)))
    up = sums[:block]
    sig = jax.nn.sigmoid(up)
    hidden = (up * sig).astype(BF16)
    slope = sig * (1.0 + up * (1.0 - sig))

    def second_half(arriving, back):
        d_up = (back * slope).astype(BF16)
        full_d_up = features_exchange(copies(d_up, parts))
        mixed = add_blocks(chips_exchange(by_cols(full_d_up, up_w)))
        return (arriving.astype(F32) + mixed).astype(BF16), full_d_up

    def gather_hidden():
        return features_exchange(copies(hidden, parts))

    def tick(arriving):
        full_back = chips_exchange(copies(arriving, chips))
        back = add_blocks(features_exchange(by_cols(full_back, down_w)))
        out, full_d_up = second_half(arriving, back)
        return out, full_back, full_d_up

    def first_tick():
        out, full_d_up = second_half(fresh, sums[block:])
        return out, full_d_up, jnp.zeros((parts, block, 2 * units), BF16)

    def wait_first():
        return (
            jnp.zeros((block, width), BF16),
            jnp.zeros((parts, block, 2 * units), BF16),
            gather_hidden(),
        )

    out, full_d_up, full_hidden = lax.cond(segment == last, first_tick, wait_first)
    for at in range(last - 1, -1, -1):
        received = lax.ppermute(out, "pipe", [(at + 1, at)])
        out, full_back, full_d_up = lax.cond(
            segment == at,
            lambda received, out, full_back, full_d_up: tick(received),
            lambda received, out, full_back, full_d_up: (out, full_back, full_d_up),
            received,
            out,
            full_back,
            full_d_up,
        )
    full_hidden = lax.cond(segment == last, gather_hidden, lambda: full_hidden)

    grad_up = by_rows(full_in, full_d_up[..., :units]) + by_rows(
        swap_cores(full_in), swap_cores(full_d_up[..., units:])
    )
    grad_down = by_rows(full_hidden[..., :units], full_back) + by_rows(
        swap_cores(full_hidden[..., units:]), swap_cores(full_back)
    )
    grads_in = out.reshape(micro_count, rows, width)
    return (grads_in[None], grad_up.astype(BF16)[None], grad_down.astype(BF16)[None])


def solution(mesh):
    return jax.shard_map(
        body,
        mesh=mesh,
        in_specs=(
            P("pipe", None, "dp", "tensor"),
            P(None, "dp", "tensor"),
            P(),
            P("pipe", "tensor", "dp"),
            P("pipe", "dp", "tensor"),
        ),
        out_specs=(
            P("pipe", None, "dp", "tensor"),
            P("pipe", "tensor", "dp"),
            P("pipe", "dp", "tensor"),
        ),
        check_vma=False,
    )
```

time: 408 us -> 362 us (0.89); the launches traced: 400 us -> 361 us
  waiting for transfers between devices: 94.6 us -> 187 us
  blocking collectives: 154 us -> 86.4 us
  starting transfers between devices: 94.2 us -> 55.3 us
  local copies, waits for them, and re-layouts: 23.2 us -> 7.79 us
  between operations: 8.85 us -> 1.06 us
  matrix products: 23.5 us -> 16.9 us
  other arithmetic: 1.6 us -> 6.81 us
    ppermute x3, waiting for transfers between devices: 15.1 us -> 141 us  [body(): received = lax.ppermute(out, 'pipe', [(at + 1, at)])]
    all_to_all x4 -> x2, blocking collectives: 62.2 us -> 24.2 us  [chips_exchange(): return lax.all_to_all(x, 'dp', 0, 0, axis_index_groups=groups, tiled=True)]
    all_to_all x5 -> x3, blocking collectives: 91.9 us -> 62.2 us  [features_exchange(): return lax.all_to_all(x, 'tensor', 0, 0, tiled=True)]
    all_to_all x5 -> x1, waiting for transfers between devices: 33.2 us -> 11.9 us  [chips_exchange(): return lax.all_to_all(x, 'dp', 0, 0, axis_index_groups=groups, tiled=True)]
    all_to_all x5 -> x1, starting transfers between devices: 27.6 us -> 10 us  [features_exchange(): return lax.all_to_all(x, 'tensor', 0, 0, tiled=True)]
    all_to_all x5 -> x1, starting transfers between devices: 17.6 us -> 3.91 us  [chips_exchange(): return lax.all_to_all(x, 'dp', 0, 0, axis_index_groups=groups, tiled=True)]
    all_to_all x5 -> x1, waiting for transfers between devices: 46.2 us -> 33.9 us  [features_exchange(): return lax.all_to_all(x, 'tensor', 0, 0, tiled=True)]
    dot_general x8 -> x3, matrix products: 15.4 us -> 6.23 us  [by_cols(): lax.dot_general(left, right, (((left.ndim - 1,), (1,)), ((), ())), prefer...]
  transfers between devices with their start and end apart: 19 -> 11, of which waited for: 12 -> 3; matrix products, arithmetic and copies ran while one was open for 9% -> 7% of each run, Pallas kernels for 0% -> 0%
where the time goes in v2:
time: 362 us; the launch traced here: 361 us
  waiting for transfers between devices  187 us (52%)
  blocking collectives  86.4 us (24%)
  starting transfers between devices  55.3 us (15%)
  matrix products  16.9 us (5%)
  local copies, waits for them, and re-layouts  7.79 us (2%)
  other arithmetic  6.81 us (2%)
    ppermute x3, waiting for transfers between devices, body(): received = lax.ppermute(out, 'pipe', [(at + 1, at)])  141 us
    all_to_all x3, blocking collectives, features_exchange(): return lax.all_to_all(x, 'tensor', 0, 0, tiled=True)  62.2 us
    ppermute x6, starting transfers between devices, swap_cores(): return lax.ppermute(x, 'dp', [(i, i ^ 1) for i in range(peers)])  38.7 us
    all_to_all x1, waiting for transfers between devices, features_exchange(): return lax.all_to_all(x, 'tensor', 0, 0, tiled=True)  33.9 us
    all_to_all x2, blocking collectives, chips_exchange(): return lax.all_to_all(x, 'dp', 0, 0, axis_index_groups=groups, tiled=True)  24.2 us
    all_to_all x1, waiting for transfers between devices, chips_exchange(): return lax.all_to_all(x, 'dp', 0, 0, axis_index_groups=groups, tiled=True)  11.9 us
    all_to_all x1, starting transfers between devices, features_exchange(): return lax.all_to_all(x, 'tensor', 0, 0, tiled=True)  10 us
    dot_general x4, matrix products, by_rows(): lax.dot_general(left, right, ((dims, dims), ((), ())), preferred_element_...  8.92 us
  transfers between devices with their start and end apart: 11, of which 3 were waited for; matrix products, arithmetic and copies ran while one was open for 7% of the time, Pallas kernels for 0%

profile of v2, /device:TPU:1, one launch (start us, length us, event | category | flops | bytes accessed | tf_op | source)
XLA Modules:
  0.0 361.0 jit_solution(2407288452677810459)
XLA Ops:
  0.6 0.0 copy-start.7
  0.6 0.0 copy-start.6
  0.7 8.9 %collective-permute-start.1 = (bf16[896,512]{1,0:T(8,128)(2,1)}, bf16[896,512]{1,0:T(8,128)(2,1)}, u32[]{:S(2)}, u32[]{:S(2)}) collective-permute-start(bf16[896,512]{1,0:T(8,128)(2,1)} %bitcast.92), channel_id=1, source_target_pairs={{0,8},{8,0},{16,24},{24,16},{32,40},{40,32},{48,56},{56,48},{64,72... | collective-permute-start | bytes 2752520 | tf_op jit(solution)/shard_map/ppermute | solution.py:12
  9.6 1.3 fusion.37
  11.3 0.7 broadcast_compare_fusion.7
  11.9 0.1 broadcast_in_dim.227
  12.0 0.1 broadcast_in_dim.228
  12.1 0.1 broadcast_in_dim.233
  12.2 0.1 broadcast_in_dim.234
  12.3 0.1 broadcast_in_dim.239
  12.3 0.1 broadcast_in_dim.240
  12.4 0.1 broadcast_in_dim.245
  12.5 0.1 broadcast_in_dim.246
  12.6 0.1 broadcast_in_dim.251
  12.6 0.1 broadcast_in_dim.252
  12.7 0.1 broadcast_in_dim.257
  12.8 0.1 broadcast_in_dim.258
  12.9 0.1 broadcast_in_dim.263
  13.0 0.1 broadcast_in_dim.264
  13.1 0.1 broadcast_in_dim.269
  13.1 0.1 broadcast_in_dim.270
  13.2 0.8 copy.10
  14.0 0.1 select_select_fusion
  14.1 0.8 broadcast_in_dim.276
  14.9 3.9 %all-to-all-start.16 = ((bf16[8,48,512]{2,1,0:T(8,128)(2,1)}), bf16[8,48,512]{2,1,0:T(8,128)(2,1)S(1)}, u32[]{:S(2)}, u32[]{:S(2)}) async-start(bf16[8,48,512]{2,1,0:T(8,128)(2,1)} %broadcast_in_dim.276), calls=%async_computation.16 | async-start | bytes 786432 | tf_op jit(solution)/shard_map/all_to_all | solution.py:18
  18.8 2.2 collective-permute-start
  21.0 11.9 %all-to-all-done.16 = bf16[8,48,512]{2,1,0:T(8,128)(2,1)S(1)} async-done(((bf16[8,48,512]{2,1,0:T(8,128)(2,1)}), bf16[8,48,512]{2,1,0:T(8,128)(2,1)S(1)}, u32[]{:S(2)}, u32[]{:S(2)}) %all-to-all-start.16) | async-done | bytes 393248 | tf_op jit(solution)/shard_map/all_to_all | solution.py:18
  33.0 2.1 convolution_convert_fusion.3
  35.1 1.7 convolution_convert_fusion.4
  36.8 1.2 pad_maximum_fusion.2
  38.0 10.0 %all-to-all-start.17 = ((bf16[8,48,1792]{2,1,0:T(8,128)(2,1)}), bf16[8,48,1792]{2,1,0:T(8,128)(2,1)S(1)}, u32[]{:S(2)}, u32[]{:S(2)}) async-start(bf16[8,48,1792]{2,1,0:T(8,128)(2,1)} %pad_maximum_fusion.2), calls=%async_computation.17 | async-start | bytes 2752512 | tf_op jit(solution)/shard_map/all_to_all | solution.py:22
  48.0 0.7 fusion.36
  48.7 1.6 pad_maximum_fusion
  50.3 33.9 %all-to-all-done.17 = bf16[8,48,1792]{2,1,0:T(8,128)(2,1)S(1)} async-done(((bf16[8,48,1792]{2,1,0:T(8,128)(2,1)}), bf16[8,48,1792]{2,1,0:T(8,128)(2,1)S(1)}, u32[]{:S(2)}, u32[]{:S(2)}) %all-to-all-start.17) | async-done | bytes 1376288 | tf_op jit(solution)/shard_map/all_to_all | solution.py:22
  84.2 0.2 convert_reduce_fusion.7
  84.4 0.1 add_multiply_fusion
  84.5 23.9 %conditional.5 = (bf16[24,512]{1,0:T(8,128)(2,1)S(1)}, bf16[8,24,1792]{2,1,0:T(8,128)(2,1)}, bf16[8,24,1792]{2,1,0:T(8,128)(2,1)S(1)}) conditional(s32[]{:T(128)} %convert_element_type.118, bf16[24,1792]{1,0:T(8,128)(2,1)S(1)} %get-tuple-element.119, (bf16[24,512]{1,0:T(8,128)(2,1)S(1)}, f32[48,1792]{1,0:T(8,128)S(1)}, f32[24,1792]{1,0:T(8,128)S(1)}, ...), branch_computations={%region_1.2_spmd, %region_2.4_spmd} | conditional | flops 352727040 | bytes 6725658 | solution.py:103
  84.5 22.9 %all_to_all.74 = bf16[8,24,1792]{2,1,0:T(8,128)(2,1)S(1)} all-to-all(bf16[8,24,1792]{2,1,0:T(8,128)(2,1)S(1)} %broadcast_in_dim.166), channel_id=1, replica_groups=mesh['pipe'=4,'dp'=16,'tensor'=8] {'tensor'}, dimensions={0} | all-to-all | bytes 1376256 | tf_op jit(solution)/shard_map/cond/branch_0_fun/all_to_all | solution.py:22
  107.4 0.9 broadcast.68
  108.3 0.7 collective-permute-start.2
  109.0 2.8 pad_maximum_fusion.1
  111.8 0.7 collective-permute-start.3
  112.5 1.3 collective-permute-start.4
  113.8 3.4 collective-permute-start.5
  117.3 1.9 collective-permute-start.7
  119.2 140.8 %collective-permute-done.4 = bf16[24,512]{1,0:T(8,128)(2,1)S(1)} collective-permute-done((bf16[24,512]{1,0:T(8,128)(2,1)S(1)}, bf16[24,512]{1,0:T(8,128)(2,1)S(1)}, u32[]{:S(2)}, u32[]{:S(2)}) %collective-permute-start.4) | collective-permute-done | bytes 24608 | tf_op jit(solution)/shard_map/ppermute | solution.py:105
  260.1 68.0 %conditional.8 = ((bf16[8,24,512]{2,1,0:T(8,128)(2,1)}, bf16[8,24,1792]{2,1,0:T(8,128)(2,1)}, bf16[24,512]{1,0:T(8,128)(2,1)S(1)})) conditional(s32[]{:T(128)} %convert_element_type.115, (bf16[8,24,512]{2,1,0:T(8,128)(2,1)}, bf16[8,24,1792]{2,1,0:T(8,128)(2,1)}, bf16[24,512]{1,0:T(8,128)(2,1)S(1)}) %tuple.55, (bf16[24,512]{1,0:T(8,128)(2,1)S(1)}, ...), branch_computations={%region_12.13_spmd, %region_13.16_spmd} | conditional | flops 706037760 | bytes 12394556 | solution.py:106
  260.1 12.1 %all_to_all.85 = bf16[8,24,512]{2,1,0:T(8,128)(2,1)S(1)} all-to-all(bf16[8,24,512]{2,1,0:T(8,128)(2,1)S(1)} %broadcast_in_dim.172), channel_id=1, replica_groups={{0,16,32,48,64,80,96,112},{8,24,40,56,72,88,104,120},{1,17,33,49,65,81,..., dimensions={0} | all-to-all | bytes 393216 | tf_op jit(solution)/shard_map/cond/branch_1_fun/all_to_all | solution.py:18
  272.2 2.3 convolution_convert_fusion.2
  274.5 16.3 %all_to_all.86 = bf16[8,24,1792]{2,1,0:T(8,128)(2,1)S(1)} all-to-all(bf16[8,24,1792]{2,1,0:T(8,128)(2,1)S(1)} %convolution_convert_fusion.2), channel_id=1, replica_groups=mesh['pipe'=4,'dp'=16,'tensor'=8] {'tensor'}, dimensions={0} | all-to-all | bytes 1376256 | tf_op jit(solution)/shard_map/cond/branch_1_fun/all_to_all | solution.py:22
  290.8 0.1 convert_reduce_fusion.5
  291.0 23.0 %all_to_all.87 = bf16[8,24,1792]{2,1,0:T(8,128)(2,1)} all-to-all(bf16[8,24,1792]{2,1,0:T(8,128)(2,1)S(1)} %broadcast_in_dim.173), channel_id=1, replica_groups=mesh['pipe'=4,'dp'=16,'tensor'=8] {'tensor'}, dimensions={0} | all-to-all | bytes 1376256 | tf_op jit(solution)/shard_map/cond/branch_1_fun/all_to_all | solution.py:22
  314.0 1.8 fusion.20
  315.9 12.1 %all_to_all.88 = bf16[8,24,512]{2,1,0:T(8,128)(2,1)S(1)} all-to-all(bf16[8,24,512]{2,1,0:T(8,128)(2,1)S(1)} %fusion.20), channel_id=1, replica_groups={{0,16,32,48,64,80,96,112},{8,24,40,56,72,88,104,120},{1,17,33,49,65,81,..., dimensions={0} | all-to-all | bytes 393216 | tf_op jit(solution)/shard_map/cond/branch_1_fun/all_to_all | solution.py:18
  328.0 0.0 copy-start.3
  328.1 0.0 copy-start.5
  328.1 2.7 fusion.29
  330.8 20.4 %collective-permute-start.8 = (bf16[8,24,512]{2,1,0:T(8,128)(2,1)S(1)}, bf16[8,24,512]{2,1,0:T(8,128)(2,1)S(1)}, u32[]{:S(2)}, u32[]{:S(2)}) collective-permute-start(bf16[8,24,512]{2,1,0:T(8,128)(2,1)S(1)} %copy-done.3), channel_id=1, source_target_pairs={{0,8},{8,0},{16,24},{24,16},{32,40},{40,32},{48,56},{56,48},{64,72... | collective-permute-start | bytes 589832 | tf_op jit(solution)/shard_map/ppermute | solution.py:12
  351.1 1.0 slice.60
  352.2 1.9 collective-permute-start.6
  354.1 0.6 copy.19
  354.7 1.6 fusion.31
  356.3 2.3 fusion.28
  358.7 2.3 fusion.27
  (52 shorter events, 0.5 us)
Async XLA Ops:
  0.6 32.3 %copy-start.7 = (bf16[1,896,512]{2,1,0:T(8,128)(2,1)S(1)}, bf16[1,896,512]{2,1,0:T(8,128)(2,1)}, u32[]{:S(2)}) copy-start(bf16[1,896,512]{2,1,0:T(8,128)(2,1)} %param.19) | copy-start | bytes 2752516
  0.6 18.2 %copy-start.6 = (bf16[1,512,896]{2,1,0:T(8,128)(2,1)S(1)}, bf16[1,512,896]{2,1,0:T(8,128)(2,1)}, u32[]{:S(2)}) copy-start(bf16[1,512,896]{2,1,0:T(8,128)(2,1)} %param.18) | copy-start | bytes 2752516
  0.7 32.3 %collective-permute-start.1 = (bf16[896,512]{1,0:T(8,128)(2,1)}, bf16[896,512]{1,0:T(8,128)(2,1)}, u32[]{:S(2)}, u32[]{:S(2)}) collective-permute-start(bf16[896,512]{1,0:T(8,128)(2,1)} %bitcast.92), channel_id=1, source_target_pairs={{0,8},{8,0},{16,24},{24,16},{32,40},{40,32},{48,56},{56,48},{64,72... | collective-permute-start | bytes 2752520 | tf_op jit(solution)/shard_map/ppermute | solution.py:12
  14.9 18.1 %all-to-all-start.16 = ((bf16[8,48,512]{2,1,0:T(8,128)(2,1)}), bf16[8,48,512]{2,1,0:T(8,128)(2,1)S(1)}, u32[]{:S(2)}, u32[]{:S(2)}) async-start(bf16[8,48,512]{2,1,0:T(8,128)(2,1)} %broadcast_in_dim.276), calls=%async_computation.16 | async-start | bytes 786432 | tf_op jit(solution)/shard_map/all_to_all | solution.py:18
  18.8 16.2 %collective-permute-start = (bf16[512,896]{1,0:T(8,128)(2,1)S(1)}, bf16[512,896]{1,0:T(8,128)(2,1)}, u32[]{:S(2)}, u32[]{:S(2)}) collective-permute-start(bf16[512,896]{1,0:T(8,128)(2,1)S(1)} %bitcast.90), channel_id=1, source_target_pairs={{0,8},{8,0},{16,24},{24,16},{32,40},{40,32},{48,56},{56,48},{64,72... | collective-permute-start | bytes 2752520 | tf_op jit(solution)/shard_map/ppermute | solution.py:12
  33.0 15.0 %copy-start.4 = (bf16[8,48,512]{2,1,0:T(8,128)(2,1)}, bf16[8,48,512]{2,1,0:T(8,128)(2,1)S(1)}, u32[]{:S(2)}) copy-start(bf16[8,48,512]{2,1,0:T(8,128)(2,1)S(1)} %all-to-all-done.16) | copy-start | bytes 1179652
  38.0 46.2 %all-to-all-start.17 = ((bf16[8,48,1792]{2,1,0:T(8,128)(2,1)}), bf16[8,48,1792]{2,1,0:T(8,128)(2,1)S(1)}, u32[]{:S(2)}, u32[]{:S(2)}) async-start(bf16[8,48,1792]{2,1,0:T(8,128)(2,1)} %pad_maximum_fusion.2), calls=%async_computation.17 | async-start | bytes 2752512 | tf_op jit(solution)/shard_map/all_to_all | solution.py:22
  108.3 3.5 collective-permute-start.2
  111.8 0.7 collective-permute-start.3
  112.5 147.5 %collective-permute-start.4 = (bf16[24,512]{1,0:T(8,128)(2,1)S(1)}, bf16[24,512]{1,0:T(8,128)(2,1)S(1)}, u32[]{:S(2)}, u32[]{:S(2)}) collective-permute-start(bf16[24,512]{1,0:T(8,128)(2,1)S(1)} %get-tuple-element.98), channel_id=1, source_target_pairs={{128,0},{129,1},{130,2},{131,3},{132,4},{133,5},{134,6},{135,7},{1... | collective-permute-start | bytes 73736 | tf_op jit(solution)/shard_map/ppermute | solution.py:105
  113.8 244.8 %collective-permute-start.5 = (bf16[8,24,512]{2,1,0:T(8,128)(2,1)S(1)}, bf16[8,24,512]{2,1,0:T(8,128)(2,1)}, u32[]{:S(2)}, u32[]{:S(2)}) collective-permute-start(bf16[8,24,512]{2,1,0:T(8,128)(2,1)S(1)} %get-tuple-element.116), channel_id=1, source_target_pairs={{0,8},{8,0},{16,24},{24,16},{32,40},{40,32},{48,56},{56,48},{64,72... | collective-permute-start | bytes 589832 | tf_op jit(solution)/shard_map/ppermute | solution.py:12
  117.3 239.0 %collective-permute-start.7 = (bf16[8,24,896]{2,1,0:T(8,128)(2,1)S(1)}, bf16[8,24,896]{2,1,0:T(8,128)(2,1)}, u32[]{:S(2)}, u32[]{:S(2)}) collective-permute-start(bf16[8,24,896]{2,1,0:T(8,128)(2,1)S(1)} %slice.67), channel_id=1, source_target_pairs={{0,8},{8,0},{16,24},{24,16},{32,40},{40,32},{48,56},{56,48},{64,72... | collective-permute-start | bytes 1032200 | tf_op jit(solution)/shard_map/ppermute | solution.py:12
  272.2 18.6 %copy-start.2 = (bf16[8,24,512]{2,1,0:T(8,128)(2,1)}, bf16[8,24,512]{2,1,0:T(8,128)(2,1)S(1)}, u32[]{:S(2)}) copy-start(bf16[8,24,512]{2,1,0:T(8,128)(2,1)S(1)} %all_to_all.85) | copy-start | bytes 589828 | tf_op jit(solution)/shard_map/cond
  328.0 2.7 copy-start.3
  328.1 26.7 %copy-start.5 = (bf16[8,48,512]{2,1,0:T(8,128)(2,1)S(1)}, bf16[8,48,512]{2,1,0:T(8,128)(2,1)}, u32[]{:S(2)}) copy-start(bf16[8,48,512]{2,1,0:T(8,128)(2,1)} %copy-done.4) | copy-start | bytes 1179652
  330.8 25.6 %collective-permute-start.8 = (bf16[8,24,512]{2,1,0:T(8,128)(2,1)S(1)}, bf16[8,24,512]{2,1,0:T(8,128)(2,1)S(1)}, u32[]{:S(2)}, u32[]{:S(2)}) collective-permute-start(bf16[8,24,512]{2,1,0:T(8,128)(2,1)S(1)} %copy-done.3), channel_id=1, source_target_pairs={{0,8},{8,0},{16,24},{24,16},{32,40},{40,32},{48,56},{56,48},{64,72... | collective-permute-start | bytes 589832 | tf_op jit(solution)/shard_map/ppermute | solution.py:12
  352.2 6.5 %collective-permute-start.6 = (bf16[8,24,896]{2,1,0:T(8,128)(2,1)S(1)}, bf16[8,24,896]{2,1,0:T(8,128)(2,1)S(1)}, u32[]{:S(2)}, u32[]{:S(2)}) collective-permute-start(bf16[8,24,896]{2,1,0:T(8,128)(2,1)S(1)} %slice.60), channel_id=1, source_target_pairs={{0,8},{8,0},{16,24},{24,16},{32,40},{40,32},{48,56},{56,48},{64,72... | collective-permute-start | bytes 1032200 | tf_op jit(solution)/shard_map/ppermute | solution.py:12
  354.7 1.6 copy-start.8

commit v3 on v2

--- a/solution.py
+++ b/solution.py
@@ -54,14 +54,14 @@
     up_w = jnp.concatenate([w_up[0], swap_cores(w_up[0])], axis=1)
     down_w = jnp.concatenate([w_down[0], swap_cores(w_down[0])], axis=0)
 
-    fresh = jnp.zeros((micro_count, rows, width), BF16)
+    samples = jnp.swapaxes(pool, 0, 1)
+    fresh = jnp.zeros((rows, micro_count, width), BF16)
     for sample in range(pool.shape[0]):
-        fresh = jnp.where((picked == sample)[:, None, None], pool[sample][None], fresh)
+        fresh = jnp.where((picked == sample)[None, :, None], samples[:, sample][:, None], fresh)
     fresh = fresh.reshape(block, width)
+    inputs = jnp.swapaxes(saved[0], 0, 1).reshape(block, width)
 
-    gathered = chips_exchange(
-        copies(jnp.concatenate([saved[0].reshape(block, width), fresh], axis=0), chips)
-    )
+    gathered = chips_exchange(copies(jnp.concatenate([inputs, fresh], axis=0), chips))
     full_in = gathered[:, :block]
     full_back = gathered[:, block:]
     up_part = lax.dot_general(
@@ -80,8 +80,19 @@
         mixed = add_blocks(chips_exchange(by_cols(full_d_up, up_w)))
         return (arriving.astype(F32) + mixed).astype(BF16), full_d_up
 
-    def gather_hidden():
-        return features_exchange(copies(hidden, parts))
+    def both_cores(x):
+        return jnp.concatenate([x, swap_cores(x)], axis=0)
+
+    def own_units(x):
+        return jnp.concatenate([x[..., :units], swap_cores(x[..., units:])], axis=0)
+
+    def own_hidden():
+        return own_units(features_exchange(copies(hidden, parts)))
+
+    def weight_grads(all_in, all_hidden, full_back, full_d_up):
+        grad_up = by_rows(all_in, own_units(full_d_up)).astype(BF16)
+        grad_down = by_rows(all_hidden, both_cores(full_back)).astype(BF16)
+        return grad_up, grad_down
 
     def tick(arriving):
         full_back = chips_exchange(copies(arriving, chips))
@@ -91,17 +102,23 @@
 
     def first_tick():
         out, full_d_up = second_half(fresh, sums[block:])
-        return out, full_d_up, jnp.zeros((parts, block, 2 * units), BF16)
+        return (
+            out,
+            full_d_up,
+            jnp.zeros((2 * chips, block, width), BF16),
+            jnp.zeros((2 * parts, block, units), BF16),
+        )
 
     def wait_first():
         return (
             jnp.zeros((block, width), BF16),
             jnp.zeros((parts, block, 2 * units), BF16),
-            gather_hidden(),
+            both_cores(full_in),
+            own_hidden(),
         )
 
-    out, full_d_up, full_hidden = lax.cond(segment == last, first_tick, wait_first)
-    for at in range(last - 1, -1, -1):
+    out, full_d_up, all_in, all_hidden = lax.cond(segment == last, first_tick, wait_first)
+    for at in range(last - 1, 0, -1):
         received = lax.ppermute(out, "pipe", [(at + 1, at)])
         out, full_back, full_d_up = lax.cond(
             segment == at,
@@ -112,16 +129,22 @@
             full_back,
             full_d_up,
         )
-    full_hidden = lax.cond(segment == last, gather_hidden, lambda: full_hidden)
+    received = lax.ppermute(out, "pipe", [(1, 0)])
 
-    grad_up = by_rows(full_in, full_d_up[..., :units]) + by_rows(
-        swap_cores(full_in), swap_cores(full_d_up[..., units:])
-    )
-    grad_down = by_rows(full_hidden[..., :units], full_back) + by_rows(
-        swap_cores(full_hidden[..., units:]), swap_cores(full_back)
-    )
-    grads_in = out.reshape(micro_count, rows, width)
-    return (grads_in[None], grad_up.astype(BF16)[None], grad_down.astype(BF16)[None])
+    def end_lowest():
+        out, full_back, full_d_up = tick(received)
+        return (out,) + weight_grads(all_in, all_hidden, full_back, full_d_up)
+
+    def end_middle():
+        return (out,) + weight_grads(all_in, all_hidden, full_back, full_d_up)
+
+    def end_highest():
+        return (out,) + weight_grads(both_cores(full_in), own_hidden(), full_back, full_d_up)
+
+    which = jnp.where(segment == 0, 0, jnp.where(segment == last, 2, 1))
+    out, grad_up, grad_down = lax.switch(which, (end_lowest, end_middle, end_highest))
+    grads_in = jnp.swapaxes(out.reshape(rows, micro_count, width), 0, 1)
+    return grads_in[None], grad_up[None], grad_down[None]
 
 
 def solution(mesh):

time: 362 us -> 350 us (0.967)
  blocking collectives: 86.4 us -> 51.4 us
  starting transfers between devices: 55.3 us -> 77.5 us
  matrix products: 16.9 us -> 10.8 us
    ppermute x3 -> x2, waiting for transfers between devices: 141 us -> 0.01 us  [body(): received = lax.ppermute(out, 'pipe', [(at + 1, at)])]
    ppermute x0 -> x1, waiting for transfers between devices: none -> 140 us  [body(): received = lax.ppermute(out, 'pipe', [(1, 0)])]
    all_to_all x3 -> x2, blocking collectives: 62.2 us -> 39.3 us  [features_exchange(): return lax.all_to_all(x, 'tensor', 0, 0, tiled=True)]
    ppermute x6, starting transfers between devices: 38.7 us -> 54.1 us  [swap_cores(): return lax.ppermute(x, 'dp', [(i, i ^ 1) for i in range(peers)])]
    all_to_all x2 -> x1, blocking collectives: 24.2 us -> 12.1 us  [chips_exchange(): return lax.all_to_all(x, 'dp', 0, 0, axis_index_groups=groups, tiled=True)]
    dot_general x4 -> x2, matrix products: 8.92 us -> 4.6 us  [by_rows(): lax.dot_general(left, right, ((dims, dims), ((), ())), preferred_element_...]
    all_to_all x1 -> x2, starting transfers between devices: 10 us -> 13.6 us  [features_exchange(): return lax.all_to_all(x, 'tensor', 0, 0, tiled=True)]
    all_to_all x1 -> x2, starting transfers between devices: 3.91 us -> 7.3 us  [chips_exchange(): return lax.all_to_all(x, 'dp', 0, 0, axis_index_groups=groups, tiled=True)]
  transfers between devices with their start and end apart: 11 -> 13, of which waited for: 3 -> 5; matrix products, arithmetic and copies ran while one was open for 7% -> 4% of each run, Pallas kernels for 0% -> 0%
where the time goes in v3:
time: 350 us; the launch traced here: 347 us
  waiting for transfers between devices  188 us (54%)
  starting transfers between devices  77.5 us (22%)
  blocking collectives  51.4 us (15%)
  matrix products  10.8 us (3%)
  local copies, waits for them, and re-layouts  9.96 us (3%)
  other arithmetic  8.22 us (2%)
    ppermute x1, waiting for transfers between devices, body(): received = lax.ppermute(out, 'pipe', [(1, 0)])  140 us
    ppermute x6, starting transfers between devices, swap_cores(): return lax.ppermute(x, 'dp', [(i, i ^ 1) for i in range(peers)])  54.1 us
    all_to_all x2, blocking collectives, features_exchange(): return lax.all_to_all(x, 'tensor', 0, 0, tiled=True)  39.3 us
    all_to_all x2, waiting for transfers between devices, features_exchange(): return lax.all_to_all(x, 'tensor', 0, 0, tiled=True)  33.9 us
    all_to_all x2, starting transfers between devices, features_exchange(): return lax.all_to_all(x, 'tensor', 0, 0, tiled=True)  13.6 us
    all_to_all x1, blocking collectives, chips_exchange(): return lax.all_to_all(x, 'dp', 0, 0, axis_index_groups=groups, tiled=True)  12.1 us
    all_to_all x2, waiting for transfers between devices, chips_exchange(): return lax.all_to_all(x, 'dp', 0, 0, axis_index_groups=groups, tiled=True)  11.9 us
    all_to_all x2, starting transfers between devices, chips_exchange(): return lax.all_to_all(x, 'dp', 0, 0, axis_index_groups=groups, tiled=True)  7.3 us
  transfers between devices with their start and end apart: 13, of which 5 were waited for; matrix products, arithmetic and copies ran while one was open for 4% of the time, Pallas kernels for 0%

profile of v3, /device:TPU:1, one launch (start us, length us, event | category | flops | bytes accessed | tf_op | source)
XLA Modules:
  0.0 347.2 jit_solution(9897744735878482197)
XLA Ops:
  0.6 0.0 copy-start.3
  0.6 0.0 copy-start.4
  0.7 8.9 %collective-permute-start.10 = (bf16[512,896]{1,0:T(8,128)(2,1)}, bf16[512,896]{1,0:T(8,128)(2,1)S(1)}, u32[]{:S(2)}, u32[]{:S(2)}) collective-permute-start(bf16[512,896]{1,0:T(8,128)(2,1)} %bitcast.117), channel_id=1, source_target_pairs={{0,8},{8,0},{16,24},{24,16},{32,40},{40,32},{48,56},{56,48},{64,72... | collective-permute-start | bytes 2752520 | tf_op jit(solution)/shard_map/ppermute | solution.py:12
  9.6 0.7 broadcast_compare_fusion.7
  10.3 0.1 broadcast_in_dim.245
  10.3 0.1 broadcast_in_dim.275
  10.4 0.1 broadcast_in_dim.269
  10.5 0.1 broadcast_in_dim.263
  10.6 0.1 broadcast_in_dim.257
  10.7 0.1 broadcast_in_dim.251
  10.8 0.1 broadcast_in_dim.287
  10.9 0.1 broadcast_in_dim.281
  11.0 0.8 reshape.47
  11.8 0.8 copy.24
  12.9 0.1 select_select_fusion
  13.0 0.8 broadcast_in_dim.293
  13.8 3.9 %all-to-all-start.16 = ((bf16[8,48,512]{2,1,0:T(8,128)(2,1)}), bf16[8,48,512]{2,1,0:T(8,128)(2,1)S(1)}, u32[]{:S(2)}, u32[]{:S(2)}) async-start(bf16[8,48,512]{2,1,0:T(8,128)(2,1)} %broadcast_in_dim.293), calls=%async_computation.16 | async-start | bytes 786432 | tf_op jit(solution)/shard_map/all_to_all | solution.py:18
  17.7 2.2 collective-permute-start.11
  19.9 11.9 %all-to-all-done.16 = bf16[8,48,512]{2,1,0:T(8,128)(2,1)S(1)} async-done(((bf16[8,48,512]{2,1,0:T(8,128)(2,1)}), bf16[8,48,512]{2,1,0:T(8,128)(2,1)S(1)}, u32[]{:S(2)}, u32[]{:S(2)}) %all-to-all-start.16) | async-done | bytes 393248 | tf_op jit(solution)/shard_map/all_to_all | solution.py:18
  31.9 0.5 convolution_convert_fusion.4
  32.4 1.9 convolution_convert_fusion.3
  34.4 1.2 pad_maximum_fusion.4
  35.6 10.0 %all-to-all-start.17 = ((bf16[8,48,1792]{2,1,0:T(8,128)(2,1)}), bf16[8,48,1792]{2,1,0:T(8,128)(2,1)S(1)}, u32[]{:S(2)}, u32[]{:S(2)}) async-start(bf16[8,48,1792]{2,1,0:T(8,128)(2,1)} %pad_maximum_fusion.4), calls=%async_computation.17 | async-start | bytes 2752512 | tf_op jit(solution)/shard_map/all_to_all | solution.py:22
  45.6 0.7 fusion.68
  46.3 1.6 pad_maximum_fusion.2
  47.9 33.9 %all-to-all-done.17 = bf16[8,48,1792]{2,1,0:T(8,128)(2,1)S(1)} async-done(((bf16[8,48,1792]{2,1,0:T(8,128)(2,1)}), bf16[8,48,1792]{2,1,0:T(8,128)(2,1)S(1)}, u32[]{:S(2)}, u32[]{:S(2)}) %all-to-all-start.17) | async-done | bytes 1376288 | tf_op jit(solution)/shard_map/all_to_all | solution.py:22
  81.8 0.2 convert_reduce_fusion.7
  82.0 0.1 add_multiply_fusion
  82.1 32.5 %conditional.4 = (bf16[24,512]{1,0:T(8,128)(2,1)S(1)}, bf16[8,24,1792]{2,1,0:T(8,128)(2,1)}, bf16[16,24,512]{2,1,0:T(8,128)(2,1)}, bf16[16,24,896]{2,1,0:T(8,128)(2,1)}) conditional(s32[]{:T(128)} %convert_element_type.131, (bf16[8,24,512]{2,1,0:T(8,128)(2,1)S(1)}, bf16[24,1792]{1,0:T(8,128)(2,1)S(1)}) %tuple.47, (bf16[24,512]{1,0:T(8,128)(2,1)S(1)}, ...), branch_computations={%region_1.2_spmd, %region_2.4_spmd} | conditional | flops 352727040 | bytes 8564852 | solution.py:120
  82.2 23.0 %all_to_all.74 = bf16[8,24,1792]{2,1,0:T(8,128)(2,1)S(1)} all-to-all(bf16[8,24,1792]{2,1,0:T(8,128)(2,1)S(1)} %broadcast_in_dim.178), channel_id=1, replica_groups=mesh['pipe'=4,'dp'=16,'tensor'=8] {'tensor'}, dimensions={0} | all-to-all | bytes 1376256 | tf_op jit(solution)/shard_map/cond/branch_0_fun/all_to_all | solution.py:22
  105.2 0.1 fusion.63
  105.2 3.4 collective-permute-start.1
  108.6 1.9 collective-permute-start
  110.6 1.4 collective-permute-done
  112.0 0.8 pad_maximum_fusion.1
  112.7 0.9 pad_maximum_fusion
  113.7 0.9 broadcast.70
  114.6 0.7 collective-permute-start.12
  115.2 2.5 pad_maximum_fusion.3
  117.8 0.7 collective-permute-start.13
  118.5 1.3 collective-permute-start.14
  119.8 139.6 %collective-permute-done.14 = bf16[24,512]{1,0:T(8,128)(2,1)S(1)} collective-permute-done((bf16[24,512]{1,0:T(8,128)(2,1)S(1)}, bf16[24,512]{1,0:T(8,128)(2,1)S(1)}, u32[]{:S(2)}, u32[]{:S(2)}) %collective-permute-start.14) | collective-permute-done | bytes 24608 | tf_op jit(solution)/shard_map/ppermute | solution.py:132
  259.4 86.6 %conditional.7 = (bf16[24,512]{1,0:T(8,128)(2,1)S(1)}, bf16[1,512,896]{2,1,0:T(8,128)(2,1)S(1)}, bf16[1,896,512]{2,1,0:T(8,128)(2,1)S(1)}) conditional(s32[]{:T(128)} %clamp.3, (bf16[24,512]{1,0:T(8,128)(2,1)S(1)}, bf16[1792,512]{1,0:T(8,128)(2,1)}, f32[24,1792]{1,0:T(8,128)S(1)}, bf16[512,1792]{1,0:T(8,128)(2,1)S(1)}, ...), branch_computations={%region_12.15_spmd, %region_15.16_spmd, %region_16.17_spmd} | conditional | flops 1412139008 | bytes 25469208 | solution.py:145
  259.4 12.1 %all_to_all.85 = bf16[8,24,512]{2,1,0:T(8,128)(2,1)S(1)} all-to-all(bf16[8,24,512]{2,1,0:T(8,128)(2,1)S(1)} %broadcast_in_dim.184), channel_id=1, replica_groups={{0,16,32,48,64,80,96,112},{8,24,40,56,72,88,104,120},{1,17,33,49,65,81,..., dimensions={0} | all-to-all | bytes 393216 | tf_op jit(solution)/shard_map/cond/branch_0_fun/all_to_all | solution.py:18
  271.5 2.3 convolution_convert_fusion.2
  273.9 16.3 %all_to_all.86 = bf16[8,24,1792]{2,1,0:T(8,128)(2,1)S(1)} all-to-all(bf16[8,24,1792]{2,1,0:T(8,128)(2,1)S(1)} %convolution_convert_fusion.2), channel_id=1, replica_groups=mesh['pipe'=4,'dp'=16,'tensor'=8] {'tensor'}, dimensions={0} | all-to-all | bytes 1376256 | tf_op jit(solution)/shard_map/cond/branch_0_fun/all_to_all | solution.py:22
  290.2 0.1 convert_reduce_fusion.5
  290.3 0.9 broadcast_in_dim.185
  291.2 3.5 %all-to-all-start.14 = ((bf16[8,24,1792]{2,1,0:T(8,128)(2,1)}), bf16[8,24,1792]{2,1,0:T(8,128)(2,1)S(1)}, u32[]{:S(2)}, u32[]{:S(2)}) async-start(bf16[8,24,1792]{2,1,0:T(8,128)(2,1)} %broadcast_in_dim.185), calls=%async_computation.14 | async-start | bytes 1376256 | tf_op jit(solution)/shard_map/cond/branch_0_fun/all_to_all | solution.py:22
  294.7 22.7 %collective-permute-start.7 = (bf16[8,24,512]{2,1,0:T(8,128)(2,1)S(1)}, bf16[8,24,512]{2,1,0:T(8,128)(2,1)S(1)}, u32[]{:S(2)}, u32[]{:S(2)}) collective-permute-start(bf16[8,24,512]{2,1,0:T(8,128)(2,1)S(1)} %all_to_all.85), channel_id=1, source_target_pairs={{0,8},{8,0},{16,24},{24,16},{32,40},{40,32},{48,56},{56,48},{64,72... | collective-permute-start | bytes 589832 | tf_op jit(solution)/shard_map/cond/branch_0_fun/ppermute | solution.py:12
  317.5 1.4 fusion.22
  318.9 3.4 all-to-all-start.15
  322.3 0.7 copy-done.14
  323.0 2.0 fusion.21
  325.0 0.5 copy.20
  325.6 0.1 fusion.64
  325.6 14.9 %collective-permute-start.6 = (bf16[8,24,896]{2,1,0:T(8,128)(2,1)S(1)}, bf16[8,24,896]{2,1,0:T(8,128)(2,1)S(1)}, u32[]{:S(2)}, u32[]{:S(2)}) collective-permute-start(bf16[8,24,896]{2,1,0:T(8,128)(2,1)S(1)} %get-tuple-element.146), channel_id=1, source_target_pairs={{0,8},{8,0},{16,24},{24,16},{32,40},{40,32},{48,56},{56,48},{64,72... | collective-permute-start | bytes 1032200 | tf_op jit(solution)/shard_map/cond/branch_0_fun/ppermute | solution.py:12
  340.6 1.2 collective-permute-done.6
  341.8 2.6 fusion.20
  344.4 1.5 copy.17
  346.0 0.0 copy-start.7
  346.0 0.7 reshape.48
  346.7 0.2 copy-done.7
  346.9 0.3 copy-done.8
  (56 shorter events, 0.4 us)
Async XLA Ops:
  0.6 31.2 %copy-start.3 = (bf16[1,512,896]{2,1,0:T(8,128)(2,1)S(1)}, bf16[1,512,896]{2,1,0:T(8,128)(2,1)}, u32[]{:S(2)}) copy-start(bf16[1,512,896]{2,1,0:T(8,128)(2,1)} %param.17) | copy-start | bytes 2752516
  0.6 17.1 %copy-start.4 = (bf16[1,896,512]{2,1,0:T(8,128)(2,1)S(1)}, bf16[1,896,512]{2,1,0:T(8,128)(2,1)}, u32[]{:S(2)}) copy-start(bf16[1,896,512]{2,1,0:T(8,128)(2,1)} %param.18) | copy-start | bytes 2752516
  0.7 31.2 %collective-permute-start.10 = (bf16[512,896]{1,0:T(8,128)(2,1)}, bf16[512,896]{1,0:T(8,128)(2,1)S(1)}, u32[]{:S(2)}, u32[]{:S(2)}) collective-permute-start(bf16[512,896]{1,0:T(8,128)(2,1)} %bitcast.117), channel_id=1, source_target_pairs={{0,8},{8,0},{16,24},{24,16},{32,40},{40,32},{48,56},{56,48},{64,72... | collective-permute-start | bytes 2752520 | tf_op jit(solution)/shard_map/ppermute | solution.py:12
  13.8 18.1 %all-to-all-start.16 = ((bf16[8,48,512]{2,1,0:T(8,128)(2,1)}), bf16[8,48,512]{2,1,0:T(8,128)(2,1)S(1)}, u32[]{:S(2)}, u32[]{:S(2)}) async-start(bf16[8,48,512]{2,1,0:T(8,128)(2,1)} %broadcast_in_dim.293), calls=%async_computation.16 | async-start | bytes 786432 | tf_op jit(solution)/shard_map/all_to_all | solution.py:18
  17.7 14.7 %collective-permute-start.11 = (bf16[896,512]{1,0:T(8,128)(2,1)S(1)}, bf16[896,512]{1,0:T(8,128)(2,1)}, u32[]{:S(2)}, u32[]{:S(2)}) collective-permute-start(bf16[896,512]{1,0:T(8,128)(2,1)S(1)} %bitcast.120), channel_id=1, source_target_pairs={{0,8},{8,0},{16,24},{24,16},{32,40},{40,32},{48,56},{56,48},{64,72... | collective-permute-start | bytes 2752520 | tf_op jit(solution)/shard_map/ppermute | solution.py:12
  31.9 3.7 %copy-start.6 = (bf16[512,896]{1,0:T(8,128)(2,1)}, bf16[512,896]{1,0:T(8,128)(2,1)S(1)}, u32[]{:S(2)}) copy-start(bf16[512,896]{1,0:T(8,128)(2,1)S(1)} %collective-permute-done.10) | copy-start | bytes 2752516
  35.6 46.3 %all-to-all-start.17 = ((bf16[8,48,1792]{2,1,0:T(8,128)(2,1)}), bf16[8,48,1792]{2,1,0:T(8,128)(2,1)S(1)}, u32[]{:S(2)}, u32[]{:S(2)}) async-start(bf16[8,48,1792]{2,1,0:T(8,128)(2,1)} %pad_maximum_fusion.4), calls=%async_computation.17 | async-start | bytes 2752512 | tf_op jit(solution)/shard_map/all_to_all | solution.py:22
  82.1 33.1 %copy-start.5 = (bf16[1,896,512]{2,1,0:T(8,128)(2,1)S(1)}, bf16[1,896,512]{2,1,0:T(8,128)(2,1)}, u32[]{:S(2)}) copy-start(bf16[1,896,512]{2,1,0:T(8,128)(2,1)} %param.18) | copy-start | bytes 2752516
  105.2 7.5 %collective-permute-start.1 = (bf16[8,24,896]{2,1,0:T(8,128)(2,1)S(1)}, bf16[8,24,896]{2,1,0:T(8,128)(2,1)S(1)}, u32[]{:S(2)}, u32[]{:S(2)}) collective-permute-start(bf16[8,24,896]{2,1,0:T(8,128)(2,1)S(1)} %get-tuple-element.144), channel_id=1, source_target_pairs={{0,8},{8,0},{16,24},{24,16},{32,40},{40,32},{48,56},{56,48},{64,72... | collective-permute-start | bytes 1032200 | tf_op jit(solution)/shard_map/cond/branch_0_fun/ppermute | solution.py:12
  108.6 3.3 collective-permute-start
  114.6 3.2 collective-permute-start.12
  117.8 0.7 collective-permute-start.13
  118.5 140.9 %collective-permute-start.14 = (bf16[24,512]{1,0:T(8,128)(2,1)S(1)}, bf16[24,512]{1,0:T(8,128)(2,1)S(1)}, u32[]{:S(2)}, u32[]{:S(2)}) collective-permute-start(bf16[24,512]{1,0:T(8,128)(2,1)S(1)} %get-tuple-element.121), channel_id=1, source_target_pairs={{128,0},{129,1},{130,2},{131,3},{132,4},{133,5},{134,6},{135,7},{1... | collective-permute-start | bytes 73736 | tf_op jit(solution)/shard_map/ppermute | solution.py:132
  259.4 30.8 %copy-start.10 = (bf16[24,512]{1,0:T(8,128)(2,1)}, bf16[24,512]{1,0:T(8,128)(2,1)S(1)}, u32[]{:S(2)}) copy-start(bf16[24,512]{1,0:T(8,128)(2,1)S(1)} %get-tuple-element.88) | copy-start | bytes 73732 | tf_op jit(solution)/shard_map/cond
  271.5 23.2 %copy-start.9 = (bf16[8,24,512]{2,1,0:T(8,128)(2,1)}, bf16[8,24,512]{2,1,0:T(8,128)(2,1)S(1)}, u32[]{:S(2)}) copy-start(bf16[8,24,512]{2,1,0:T(8,128)(2,1)S(1)} %all_to_all.85) | copy-start | bytes 589828 | tf_op jit(solution)/shard_map/cond
  291.2 26.3 %all-to-all-start.14 = ((bf16[8,24,1792]{2,1,0:T(8,128)(2,1)}), bf16[8,24,1792]{2,1,0:T(8,128)(2,1)S(1)}, u32[]{:S(2)}, u32[]{:S(2)}) async-start(bf16[8,24,1792]{2,1,0:T(8,128)(2,1)} %broadcast_in_dim.185), calls=%async_computation.14 | async-start | bytes 1376256 | tf_op jit(solution)/shard_map/cond/branch_0_fun/all_to_all | solution.py:22
  294.7 27.6 %collective-permute-start.7 = (bf16[8,24,512]{2,1,0:T(8,128)(2,1)S(1)}, bf16[8,24,512]{2,1,0:T(8,128)(2,1)S(1)}, u32[]{:S(2)}, u32[]{:S(2)}) collective-permute-start(bf16[8,24,512]{2,1,0:T(8,128)(2,1)S(1)} %all_to_all.85), channel_id=1, source_target_pairs={{0,8},{8,0},{16,24},{24,16},{32,40},{40,32},{48,56},{56,48},{64,72... | collective-permute-start | bytes 589832 | tf_op jit(solution)/shard_map/cond/branch_0_fun/ppermute | solution.py:12
  318.9 21.7 %all-to-all-start.15 = ((bf16[8,24,512]{2,1,0:T(8,128)(2,1)}), bf16[8,24,512]{2,1,0:T(8,128)(2,1)S(1)}, u32[]{:S(2)}, u32[]{:S(2)}) async-start(bf16[8,24,512]{2,1,0:T(8,128)(2,1)} %fusion.22), calls=%async_computation.15 | async-start | bytes 393216 | tf_op jit(solution)/shard_map/cond/branch_0_fun/all_to_all | solution.py:18
  322.3 0.7 copy-start.14
  325.0 15.6 %copy-start.11 = (bf16[24,512]{1,0:T(8,128)(2,1)S(1)}, bf16[24,512]{1,0:T(8,128)(2,1)}, u32[]{:S(2)}) copy-start(bf16[24,512]{1,0:T(8,128)(2,1)} %copy-done.10) | copy-start | bytes 73732 | tf_op jit(solution)/shard_map/cond
  325.6 16.2 %collective-permute-start.6 = (bf16[8,24,896]{2,1,0:T(8,128)(2,1)S(1)}, bf16[8,24,896]{2,1,0:T(8,128)(2,1)S(1)}, u32[]{:S(2)}, u32[]{:S(2)}) collective-permute-start(bf16[8,24,896]{2,1,0:T(8,128)(2,1)S(1)} %get-tuple-element.146), channel_id=1, source_target_pairs={{0,8},{8,0},{16,24},{24,16},{32,40},{40,32},{48,56},{56,48},{64,72... | collective-permute-start | bytes 1032200 | tf_op jit(solution)/shard_map/cond/branch_0_fun/ppermute | solution.py:12
  346.0 0.9 copy-start.7
  346.0 1.2 copy-start.8

commit v4 on v3

--- a/solution.py
+++ b/solution.py
@@ -18,6 +18,22 @@
     return lax.all_to_all(x, "dp", 0, 0, axis_index_groups=groups, tiled=True)
 
 
+def row_exchange(x):
+    peers = lax.axis_size("dp")
+    groups = [[4 * at + r for at in range(peers // 4)] for r in range(4)]
+    return lax.all_to_all(x, "dp", 0, 0, axis_index_groups=groups, tiled=True)
+
+
+def swap_middle(x, mate):
+    segments, peers = lax.axis_size("pipe"), lax.axis_size("dp")
+    pairs = [(p * peers + i, p * peers + (i ^ mate)) for p in range(1, segments - 1) for i in range(peers)]
+    return lax.ppermute(x, ("pipe", "dp"), pairs)
+
+
+def swap_mates(x, mate):
+    return lax.ppermute(x, "dp", [(i, i ^ mate) for i in range(lax.axis_size("dp"))])
+
+
 def features_exchange(x):
     return lax.all_to_all(x, "tensor", 0, 0, tiled=True)
 
@@ -30,10 +46,14 @@
     return jnp.sum(x.astype(F32), axis=0)
 
 
-def by_cols(left, right):
+def cols_product(left, right):
     return lax.dot_general(
         left, right, (((left.ndim - 1,), (1,)), ((), ())), preferred_element_type=F32
-    ).astype(BF16)
+    )
+
+
+def by_cols(left, right):
+    return cols_product(left, right).astype(BF16)
 
 
 def by_rows(left, right):
@@ -50,9 +70,15 @@
     units = w_up.shape[2]
     block = micro_count * rows
     last = segments - 1
+    peers = lax.axis_size("dp")
+    few = chips // 2
+    y_hi = (lax.axis_index("dp") // 2) % 2
 
     up_w = jnp.concatenate([w_up[0], swap_cores(w_up[0])], axis=1)
     down_w = jnp.concatenate([w_down[0], swap_cores(w_down[0])], axis=0)
+
+    up_other = swap_middle(w_up[0], 2)
+    down_other = swap_middle(w_down[0], 2)
 
     samples = jnp.swapaxes(pool, 0, 1)
     fresh = jnp.zeros((rows, micro_count, width), BF16)
@@ -74,11 +100,28 @@
     hidden = (up * sig).astype(BF16)
     slope = sig * (1.0 + up * (1.0 - sig))
 
+    moves = []
+    for group in range(1, last):
+        for i in range(peers):
+            for z in range(parts):
+                units_y, tokens_y = (i // 2) % 2, z % 2
+                to = i - 2 * units_y + 2 * tokens_y
+                place = (units_y ^ tokens_y) * few + z // 2
+                moves.append(((group * peers + i) * parts + z, (group * peers + to) * parts + place))
+
+    def middle_weights():
+        return (
+            jnp.concatenate([up_other, swap_middle(up_other, 1)], axis=1),
+            jnp.concatenate([down_other, swap_middle(down_other, 1)], axis=0),
+            lax.ppermute(slope, ("pipe", "dp", "tensor"), moves),
+        )
+
     def second_half(arriving, back):
         d_up = (back * slope).astype(BF16)
         full_d_up = features_exchange(copies(d_up, parts))
-        mixed = add_blocks(chips_exchange(by_cols(full_d_up, up_w)))
-        return (arriving.astype(F32) + mixed).astype(BF16), full_d_up
+        part = by_cols(full_d_up, up_w)
+        mixed = add_blocks(chips_exchange(part))
+        return (arriving.astype(F32) + mixed).astype(BF16), full_d_up, part
 
     def both_cores(x):
         return jnp.concatenate([x, swap_cores(x)], axis=0)
@@ -88,6 +131,10 @@
 
     def own_hidden():
         return own_units(features_exchange(copies(hidden, parts)))
+
+    def after(x, y):
+        first = y[(0,) * y.ndim]
+        return jnp.where(jnp.isnan(first), first, x)
 
     def weight_grads(all_in, all_hidden, full_back, full_d_up):
         grad_up = by_rows(all_in, own_units(full_d_up)).astype(BF16)
@@ -97,38 +144,66 @@
     def tick(arriving):
         full_back = chips_exchange(copies(arriving, chips))
         back = add_blocks(features_exchange(by_cols(full_back, down_w)))
-        out, full_d_up = second_half(arriving, back)
-        return out, full_back, full_d_up
+        out, full_d_up, part = second_half(arriving, back)
+        return out, after(full_back, part), full_d_up
+
+    def middle_tick(arriving):
+        row_back = row_exchange(copies(arriving, few))
+        part = jnp.concatenate([by_cols(row_back, down_w), by_cols(row_back, down_mate)], axis=0)
+        back = add_blocks(features_exchange(part))
+        d_up = (back * middle_slope).astype(BF16)
+        row_d_up = features_exchange(copies(d_up, parts))
+        part = cols_product(row_d_up[:few], up_w) + cols_product(row_d_up[few:], up_mate)
+        mixed = add_blocks(row_exchange(part.astype(BF16)))
+        return (arriving.astype(F32) + mixed).astype(BF16), row_back, row_d_up
+
+    def own_row_first(x):
+        x = x.reshape((few, 2) + x.shape[1:])
+        first, second = x[:, 0], x[:, 1]
+        return jnp.concatenate(
+            [jnp.where(y_hi == 0, first, second), jnp.where(y_hi == 0, second, first)], axis=0
+        )
+
+    def middle_grads(row_back, row_d_up):
+        all_back = jnp.concatenate([row_back, swap_mates(row_back, 2)], axis=0)
+        all_d_up = jnp.concatenate([row_d_up[:few], swap_mates(row_d_up[few:], 2)], axis=0)
+        all_hidden = own_units(own_row_first(features_exchange(copies(hidden, parts))))
+        return weight_grads(both_cores(own_row_first(full_in)), all_hidden, all_back, all_d_up)
 
     def first_tick():
-        out, full_d_up = second_half(fresh, sums[block:])
-        return (
+        return second_half(fresh, sums[block:])[:2]
+
+    out, full_d_up = lax.cond(
+        segment == last,
+        first_tick,
+        lambda: (jnp.zeros((block, width), BF16), jnp.zeros((parts, block, 2 * units), BF16)),
+    )
+    up_mate, down_mate, middle_slope = lax.cond(
+        jnp.logical_and(segment > 0, segment < last),
+        middle_weights,
+        lambda: (jnp.zeros_like(up_w), jnp.zeros_like(down_w), jnp.zeros_like(slope)),
+    )
+    row_back = jnp.zeros((few, block, width), BF16)
+    row_d_up = jnp.zeros((parts, block, 2 * units), BF16)
+    for at in range(last - 1, 0, -1):
+        received = lax.ppermute(out, "pipe", [(at + 1, at)])
+        out, row_back, row_d_up = lax.cond(
+            segment == at,
+            lambda received, out, row_back, row_d_up: middle_tick(received),
+            lambda received, out, row_back, row_d_up: (out, row_back, row_d_up),
+            received,
             out,
-            full_d_up,
+            row_back,
+            row_d_up,
+        )
+    all_in, all_hidden = lax.cond(
+        segment == 0,
+        lambda: (both_cores(full_in), own_hidden()),
+        lambda: (
             jnp.zeros((2 * chips, block, width), BF16),
             jnp.zeros((2 * parts, block, units), BF16),
-        )
-
-    def wait_first():
-        return (
-            jnp.zeros((block, width), BF16),
-            jnp.zeros((parts, block, 2 * units), BF16),
-            both_cores(full_in),
-            own_hidden(),
-        )
-
-    out, full_d_up, all_in, all_hidden = lax.cond(segment == last, first_tick, wait_first)
-    for at in range(last - 1, 0, -1):
-        received = lax.ppermute(out, "pipe", [(at + 1, at)])
-        out, full_back, full_d_up = lax.cond(
-            segment == at,
-            lambda received, out, full_back, full_d_up: tick(received),
-            lambda received, out, full_back, full_d_up: (out, full_back, full_d_up),
-            received,
-            out,
-            full_back,
-            full_d_up,
-        )
+        ),
+    )
     received = lax.ppermute(out, "pipe", [(1, 0)])
 
     def end_lowest():
@@ -136,7 +211,7 @@
         return (out,) + weight_grads(all_in, all_hidden, full_back, full_d_up)
 
     def end_middle():
-        return (out,) + weight_grads(all_in, all_hidden, full_back, full_d_up)
+        return (out,) + middle_grads(row_back, row_d_up)
 
     def end_highest():
         return (out,) + weight_grads(both_cores(full_in), own_hidden(), full_back, full_d_up)

time: 350 us -> 342 us (0.977)
  blocking collectives: 51.4 us -> 78.5 us
  waiting for transfers between devices: 188 us -> 166 us
  starting transfers between devices: 77.5 us -> 60.7 us
  local copies, waits for them, and re-layouts: 9.96 us -> 14.4 us
    all_to_all x2 -> x3, blocking collectives: 39.3 us -> 61.7 us  [features_exchange(): return lax.all_to_all(x, 'tensor', 0, 0, tiled=True)]
    ppermute x1, waiting for transfers between devices: 140 us -> 121 us  [body(): received = lax.ppermute(out, 'pipe', [(1, 0)])]
    ppermute x6, starting transfers between devices: 54.1 us -> 37.5 us  [swap_cores(): return lax.ppermute(x, 'dp', [(i, i ^ 1) for i in range(peers)])]
    another operation x2 -> x9, local copies, waits for them, and re-layouts: 0.9 us -> 6.99 us
    all_to_all x1, blocking collectives: 12.1 us -> 16.8 us  [chips_exchange(): return lax.all_to_all(x, 'dp', 0, 0, axis_index_groups=groups, tiled=True)]
    all_to_all x2 -> x1, starting transfers between devices: 13.6 us -> 10 us  [features_exchange(): return lax.all_to_all(x, 'tensor', 0, 0, tiled=True)]
    all_to_all x2 -> x1, waiting for transfers between devices: 33.9 us -> 31.4 us  [features_exchange(): return lax.all_to_all(x, 'tensor', 0, 0, tiled=True)]
  transfers between devices with their start and end apart: 13 -> 14, of which waited for: 5 -> 5; matrix products, arithmetic and copies ran while one was open for 4% -> 6% of each run, Pallas kernels for 0% -> 0%
where the time goes in v4:
time: 342 us; the launch traced here: 340 us
  waiting for transfers between devices  166 us (49%)
  blocking collectives  78.5 us (23%)
  starting transfers between devices  60.7 us (18%)
  local copies, waits for them, and re-layouts  14.4 us (4%)
  matrix products  10.5 us (3%)
  other arithmetic  7.32 us (2%)
    ppermute x1, waiting for transfers between devices, body(): received = lax.ppermute(out, 'pipe', [(1, 0)])  121 us
    all_to_all x3, blocking collectives, features_exchange(): return lax.all_to_all(x, 'tensor', 0, 0, tiled=True)  61.7 us
    ppermute x6, starting transfers between devices, swap_cores(): return lax.ppermute(x, 'dp', [(i, i ^ 1) for i in range(peers)])  37.5 us
    all_to_all x1, waiting for transfers between devices, features_exchange(): return lax.all_to_all(x, 'tensor', 0, 0, tiled=True)  31.4 us
    all_to_all x1, blocking collectives, chips_exchange(): return lax.all_to_all(x, 'dp', 0, 0, axis_index_groups=groups, tiled=True)  16.8 us
    all_to_all x2, waiting for transfers between devices, chips_exchange(): return lax.all_to_all(x, 'dp', 0, 0, axis_index_groups=groups, tiled=True)  12 us
    all_to_all x1, starting transfers between devices, features_exchange(): return lax.all_to_all(x, 'tensor', 0, 0, tiled=True)  10 us
    all_to_all x2, starting transfers between devices, chips_exchange(): return lax.all_to_all(x, 'dp', 0, 0, axis_index_groups=groups, tiled=True)  7.3 us
  transfers between devices with their start and end apart: 14, of which 5 were waited for; matrix products, arithmetic and copies ran while one was open for 6% of the time, Pallas kernels for 0%

profile of v4, /device:TPU:1, one launch (start us, length us, event | category | flops | bytes accessed | tf_op | source)
XLA Modules:
  0.0 340.2 jit_solution(13607417442095383599)
XLA Ops:
  0.6 8.8 %collective-permute-start.18 = (bf16[896,512]{1,0:T(8,128)(2,1)}, bf16[896,512]{1,0:T(8,128)(2,1)S(1)}, u32[]{:S(2)}, u32[]{:S(2)}) collective-permute-start(bf16[896,512]{1,0:T(8,128)(2,1)} %bitcast.45), channel_id=1, source_target_pairs={{0,8},{8,0},{16,24},{24,16},{32,40},{40,32},{48,56},{56,48},{64,72... | collective-permute-start | bytes 2752520 | tf_op jit(solution)/shard_map/ppermute | solution.py:12
  9.4 0.8 copy.22
  10.6 0.7 broadcast_compare_fusion.7
  11.2 0.1 broadcast_in_dim.258
  11.3 0.1 broadcast_in_dim.264
  11.4 0.1 broadcast_in_dim.270
  11.5 0.1 broadcast_in_dim.276
  11.7 0.1 broadcast_in_dim.288
  12.0 0.8 reshape.62
  12.8 0.1 select_select_fusion
  12.9 0.8 broadcast_in_dim.306
  13.7 3.9 %all-to-all-start.17 = ((bf16[8,48,512]{2,1,0:T(8,128)(2,1)}), bf16[8,48,512]{2,1,0:T(8,128)(2,1)S(1)}, u32[]{:S(2)}, u32[]{:S(2)}) async-start(bf16[8,48,512]{2,1,0:T(8,128)(2,1)} %broadcast_in_dim.306), calls=%async_computation.17 | async-start | bytes 786432 | tf_op jit(solution)/shard_map/all_to_all | solution.py:18
  17.6 2.2 collective-permute-start.17
  19.8 12.0 %all-to-all-done.17 = bf16[8,48,512]{2,1,0:T(8,128)(2,1)S(1)} async-done(((bf16[8,48,512]{2,1,0:T(8,128)(2,1)}), bf16[8,48,512]{2,1,0:T(8,128)(2,1)S(1)}, u32[]{:S(2)}, u32[]{:S(2)}) %all-to-all-start.17) | async-done | bytes 393248 | tf_op jit(solution)/shard_map/all_to_all | solution.py:18
  31.7 2.4 convolution_convert_fusion.5
  34.2 2.0 convolution_convert_fusion.6
  36.2 1.2 pad_maximum_fusion.12
  37.5 10.0 %all-to-all-start.18 = ((bf16[8,48,1792]{2,1,0:T(8,128)(2,1)}), bf16[8,48,1792]{2,1,0:T(8,128)(2,1)S(1)}, u32[]{:S(2)}, u32[]{:S(2)}) async-start(bf16[8,48,1792]{2,1,0:T(8,128)(2,1)} %pad_maximum_fusion.12), calls=%async_computation.18 | async-start | bytes 2752512 | tf_op jit(solution)/shard_map/all_to_all | solution.py:38
  47.5 1.6 collective-permute-start.20
  49.1 1.6 collective-permute-start.21
  50.7 1.6 pad_maximum_fusion.10
  52.3 31.4 %all-to-all-done.18 = bf16[8,48,1792]{2,1,0:T(8,128)(2,1)S(1)} async-done(((bf16[8,48,1792]{2,1,0:T(8,128)(2,1)}), bf16[8,48,1792]{2,1,0:T(8,128)(2,1)S(1)}, u32[]{:S(2)}, u32[]{:S(2)}) %all-to-all-start.18) | async-done | bytes 1376288 | tf_op jit(solution)/shard_map/all_to_all | solution.py:38
  83.7 0.2 convert_reduce_fusion.7
  84.0 1.6 conditional.6
  84.0 1.0 broadcast.87
  85.0 0.6 broadcast.86
  85.6 0.7 collective-permute-start.19
  86.2 2.6 pad_maximum_fusion.11
  88.8 3.4 conditional.7
  88.8 1.3 broadcast.88
  90.2 1.4 broadcast.89
  91.5 0.7 broadcast.90
  92.2 1.6 conditional.8
  92.2 0.9 broadcast.91
  93.1 0.6 broadcast_in_dim.189
  93.8 0.7 collective-permute-start.22
  94.5 1.4 collective-permute-start.23
  95.9 0.7 fusion.92
  96.6 29.8 %conditional.10 = (bf16[16,24,512]{2,1,0:T(8,128)(2,1)S(1)}, bf16[16,24,896]{2,1,0:T(8,128)(2,1)S(1)}) conditional(s32[]{:T(128)} %convert_element_type.142, () %tuple.75, (bf16[8,24,512]{2,1,0:T(8,128)(2,1)S(1)}, bf16[24,1792]{1,0:T(8,128)(2,1)S(1)}) %tuple.76), branch_computations={%region_14.15_spmd, %region_15.16_spmd} | conditional | flops 540672 | bytes 7852128 | solution.py:199
  96.7 22.9 %all_to_all.88 = bf16[8,24,1792]{2,1,0:T(8,128)(2,1)S(1)} all-to-all(bf16[8,24,1792]{2,1,0:T(8,128)(2,1)S(1)} %broadcast_in_dim.194), channel_id=1, replica_groups=mesh['pipe'=4,'dp'=16,'tensor'=8] {'tensor'}, dimensions={0} | all-to-all | bytes 1376256 | tf_op jit(solution)/shard_map/cond/branch_1_fun/all_to_all | solution.py:38
  119.6 3.4 collective-permute-start.4
  123.0 1.9 collective-permute-start.3
  124.9 1.4 collective-permute-done.3
  126.5 120.8 %collective-permute-done.23 = bf16[24,512]{1,0:T(8,128)(2,1)S(1)} collective-permute-done((bf16[24,512]{1,0:T(8,128)(2,1)S(1)}, bf16[24,512]{1,0:T(8,128)(2,1)S(1)}, u32[]{:S(2)}, u32[]{:S(2)}) %collective-permute-start.23) | collective-permute-done | bytes 24608 | tf_op jit(solution)/shard_map/ppermute | solution.py:207
  247.3 91.6 %conditional.11 = (bf16[24,512]{1,0:T(8,128)(2,1)S(1)}, bf16[1,512,896]{2,1,0:T(8,128)(2,1)S(1)}, bf16[1,896,512]{2,1,0:T(8,128)(2,1)S(1)}) conditional(s32[]{:T(128)} %clamp.3, (bf16[24,512]{1,0:T(8,128)(2,1)S(1)}, bf16[1792,512]{1,0:T(8,128)(2,1)}, f32[24,1792]{1,0:T(8,128)S(1)}, bf16[512,1792]{1,0:T(8,128)(2,1)S(1)}, ...), branch_computations={%region_16.19_spmd, %region_19.20_spmd, %region_20.21_spmd} | conditional | flops 1412237312 | bytes 32055556 | solution.py:220
  247.4 16.8 %all_to_all.89 = bf16[8,24,512]{2,1,0:T(8,128)(2,1)S(1)} all-to-all(bf16[8,24,512]{2,1,0:T(8,128)(2,1)S(1)} %broadcast_in_dim.195), channel_id=1, replica_groups={{0,16,32,48,64,80,96,112},{8,24,40,56,72,88,104,120},{1,17,33,49,65,81,..., dimensions={0} | all-to-all | bytes 393216 | tf_op jit(solution)/shard_map/cond/branch_0_fun/all_to_all | solution.py:18
  264.2 2.2 convolution_convert_fusion.4
  266.5 16.3 %all_to_all.90 = bf16[8,24,1792]{2,1,0:T(8,128)(2,1)S(1)} all-to-all(bf16[8,24,1792]{2,1,0:T(8,128)(2,1)S(1)} %convolution_convert_fusion.4), channel_id=1, replica_groups=mesh['pipe'=4,'dp'=16,'tensor'=8] {'tensor'}, dimensions={0} | all-to-all | bytes 1376256 | tf_op jit(solution)/shard_map/cond/branch_0_fun/all_to_all | solution.py:38
  282.7 0.1 convert_reduce_fusion.5
  282.9 22.5 %all_to_all.91 = bf16[8,24,1792]{2,1,0:T(8,128)(2,1)S(1)} all-to-all(bf16[8,24,1792]{2,1,0:T(8,128)(2,1)S(1)} %broadcast_in_dim.196), channel_id=1, replica_groups=mesh['pipe'=4,'dp'=16,'tensor'=8] {'tensor'}, dimensions={0} | all-to-all | bytes 1376256 | tf_op jit(solution)/shard_map/cond/branch_0_fun/all_to_all | solution.py:38
  305.4 1.4 fusion.34
  306.9 1.3 slice.120
  308.1 3.4 all-to-all-start.16
  312.7 0.6 broadcast_select_fusion
  313.4 19.3 %collective-permute-start.16 = (bf16[8,24,512]{2,1,0:T(8,128)(2,1)S(1)}, bf16[8,24,512]{2,1,0:T(8,128)(2,1)S(1)}, u32[]{:S(2)}, u32[]{:S(2)}) collective-permute-start(bf16[8,24,512]{2,1,0:T(8,128)(2,1)S(1)} %broadcast_select_fusion), channel_id=1, source_target_pairs={{0,8},{8,0},{16,24},{24,16},{32,40},{40,32},{48,56},{56,48},{64,72... | collective-permute-start | bytes 589832 | tf_op jit(solution)/shard_map/cond/branch_0_fun/ppermute | solution.py:12
  332.8 1.9 collective-permute-start.15
  334.7 0.7 fusion.33
  335.4 0.5 copy.11
  336.0 0.5 collective-permute-done.15
  336.4 1.6 fusion.32
  338.1 0.6 copy.10
  339.0 0.7 reshape.63
  339.7 0.2 copy-done.10
  339.9 0.3 copy-done.11
  (73 shorter events, 1.1 us)
Async XLA Ops:
  0.6 31.1 %collective-permute-start.18 = (bf16[896,512]{1,0:T(8,128)(2,1)}, bf16[896,512]{1,0:T(8,128)(2,1)S(1)}, u32[]{:S(2)}, u32[]{:S(2)}) collective-permute-start(bf16[896,512]{1,0:T(8,128)(2,1)} %bitcast.45), channel_id=1, source_target_pairs={{0,8},{8,0},{16,24},{24,16},{32,40},{40,32},{48,56},{56,48},{64,72... | collective-permute-start | bytes 2752520 | tf_op jit(solution)/shard_map/ppermute | solution.py:12
  13.7 18.1 %all-to-all-start.17 = ((bf16[8,48,512]{2,1,0:T(8,128)(2,1)}), bf16[8,48,512]{2,1,0:T(8,128)(2,1)S(1)}, u32[]{:S(2)}, u32[]{:S(2)}) async-start(bf16[8,48,512]{2,1,0:T(8,128)(2,1)} %broadcast_in_dim.306), calls=%async_computation.17 | async-start | bytes 786432 | tf_op jit(solution)/shard_map/all_to_all | solution.py:18
  17.6 16.6 %collective-permute-start.17 = (bf16[512,896]{1,0:T(8,128)(2,1)}, bf16[512,896]{1,0:T(8,128)(2,1)S(1)}, u32[]{:S(2)}, u32[]{:S(2)}) collective-permute-start(bf16[512,896]{1,0:T(8,128)(2,1)} %bitcast.43), channel_id=1, source_target_pairs={{0,8},{8,0},{16,24},{24,16},{32,40},{40,32},{48,56},{56,48},{64,72... | collective-permute-start | bytes 2752520 | tf_op jit(solution)/shard_map/ppermute | solution.py:12
  31.7 2.4 copy-start.5
  31.7 2.4 copy-start.7
  34.2 2.1 copy-start.9
  37.5 46.3 %all-to-all-start.18 = ((bf16[8,48,1792]{2,1,0:T(8,128)(2,1)}), bf16[8,48,1792]{2,1,0:T(8,128)(2,1)S(1)}, u32[]{:S(2)}, u32[]{:S(2)}) async-start(bf16[8,48,1792]{2,1,0:T(8,128)(2,1)} %pad_maximum_fusion.12), calls=%async_computation.18 | async-start | bytes 2752512 | tf_op jit(solution)/shard_map/all_to_all | solution.py:38
  47.5 41.3 %collective-permute-start.20 = (bf16[512,896]{1,0:T(8,128)(2,1)}, bf16[512,896]{1,0:T(8,128)(2,1)}, u32[]{:S(2)}, u32[]{:S(2)}) collective-permute-start(bf16[512,896]{1,0:T(8,128)(2,1)} %bitcast.43), channel_id=1, source_target_pairs={{128,144},{136,152},{144,128},{152,136},{160,176},{168,184},{176,1... | collective-permute-start | bytes 2752520 | tf_op jit(solution)/shard_map/ppermute | solution.py:30
  49.1 39.7 %collective-permute-start.21 = (bf16[896,512]{1,0:T(8,128)(2,1)}, bf16[896,512]{1,0:T(8,128)(2,1)}, u32[]{:S(2)}, u32[]{:S(2)}) collective-permute-start(bf16[896,512]{1,0:T(8,128)(2,1)} %bitcast.45), channel_id=1, source_target_pairs={{128,144},{136,152},{144,128},{152,136},{160,176},{168,184},{176,1... | collective-permute-start | bytes 2752520 | tf_op jit(solution)/shard_map/ppermute | solution.py:30
  84.0 2.3 copy-start.8
  85.6 6.7 %collective-permute-start.19 = (bf16[24,512]{1,0:T(8,128)(2,1)}, bf16[24,512]{1,0:T(8,128)(2,1)S(1)}, u32[]{:S(2)}, u32[]{:S(2)}) collective-permute-start(bf16[24,512]{1,0:T(8,128)(2,1)} %get-tuple-element.166), channel_id=1, source_target_pairs={{384,256},{385,257},{386,258},{387,259},{388,260},{389,261},{390,2... | collective-permute-start | bytes 73736 | tf_op jit(solution)/shard_map/ppermute | solution.py:189
  93.8 0.7 collective-permute-start.22
  94.5 1.5 copy-start.6
  94.5 152.8 %collective-permute-start.23 = (bf16[24,512]{1,0:T(8,128)(2,1)S(1)}, bf16[24,512]{1,0:T(8,128)(2,1)S(1)}, u32[]{:S(2)}, u32[]{:S(2)}) collective-permute-start(bf16[24,512]{1,0:T(8,128)(2,1)S(1)} %get-tuple-element.171), channel_id=1, source_target_pairs={{128,0},{129,1},{130,2},{131,3},{132,4},{133,5},{134,6},{135,7},{1... | collective-permute-start | bytes 73736 | tf_op jit(solution)/shard_map/ppermute | solution.py:207
  96.6 150.7 %copy-start.4 = (bf16[4,24,512]{2,1,0:T(8,128)(2,1)S(1)}, bf16[4,24,512]{2,1,0:T(8,128)(2,1)}, u32[]{:S(2)}) copy-start(bf16[4,24,512]{2,1,0:T(8,128)(2,1)} %get-tuple-element.175) | copy-start | bytes 294916
  119.6 6.8 %collective-permute-start.4 = (bf16[8,24,896]{2,1,0:T(8,128)(2,1)S(1)}, bf16[8,24,896]{2,1,0:T(8,128)(2,1)S(1)}, u32[]{:S(2)}, u32[]{:S(2)}) collective-permute-start(bf16[8,24,896]{2,1,0:T(8,128)(2,1)S(1)} %get-tuple-element.209), channel_id=1, source_target_pairs={{0,8},{8,0},{16,24},{24,16},{32,40},{40,32},{48,56},{56,48},{64,72... | collective-permute-start | bytes 1032200 | tf_op jit(solution)/shard_map/cond/branch_1_fun/ppermute | solution.py:12
  123.0 3.3 collective-permute-start.3
  247.3 16.9 %copy-start.12 = (bf16[16,24,896]{2,1,0:T(8,128)(2,1)}, bf16[16,24,896]{2,1,0:T(8,128)(2,1)S(1)}, u32[]{:S(2)}) copy-start(bf16[16,24,896]{2,1,0:T(8,128)(2,1)S(1)} %get-tuple-element.135) | copy-start | bytes 2064388 | tf_op jit(solution)/shard_map/cond
  247.3 16.9 %copy-start.14 = (bf16[16,24,512]{2,1,0:T(8,128)(2,1)}, bf16[16,24,512]{2,1,0:T(8,128)(2,1)S(1)}, u32[]{:S(2)}) copy-start(bf16[16,24,512]{2,1,0:T(8,128)(2,1)S(1)} %get-tuple-element.134) | copy-start | bytes 1179652 | tf_op jit(solution)/shard_map/cond
  306.9 27.8 %copy-start.13 = (bf16[16,24,896]{2,1,0:T(8,128)(2,1)S(1)}, bf16[16,24,896]{2,1,0:T(8,128)(2,1)}, u32[]{:S(2)}) copy-start(bf16[16,24,896]{2,1,0:T(8,128)(2,1)} %copy-done.12) | copy-start | bytes 2064388 | tf_op jit(solution)/shard_map/cond
  308.1 30.6 %all-to-all-start.16 = ((bf16[8,24,512]{2,1,0:T(8,128)(2,1)}), bf16[8,24,512]{2,1,0:T(8,128)(2,1)S(1)}, u32[]{:S(2)}, u32[]{:S(2)}) async-start(bf16[8,24,512]{2,1,0:T(8,128)(2,1)} %fusion.34), calls=%async_computation.16 | async-start | bytes 393216 | tf_op jit(solution)/shard_map/cond/branch_0_fun/all_to_all | solution.py:18
  313.4 21.3 %collective-permute-start.16 = (bf16[8,24,512]{2,1,0:T(8,128)(2,1)S(1)}, bf16[8,24,512]{2,1,0:T(8,128)(2,1)S(1)}, u32[]{:S(2)}, u32[]{:S(2)}) collective-permute-start(bf16[8,24,512]{2,1,0:T(8,128)(2,1)S(1)} %broadcast_select_fusion), channel_id=1, source_target_pairs={{0,8},{8,0},{16,24},{24,16},{32,40},{40,32},{48,56},{56,48},{64,72... | collective-permute-start | bytes 589832 | tf_op jit(solution)/shard_map/cond/branch_0_fun/ppermute | solution.py:12
  332.8 3.7 %collective-permute-start.15 = (bf16[8,24,896]{2,1,0:T(8,128)(2,1)S(1)}, bf16[8,24,896]{2,1,0:T(8,128)(2,1)}, u32[]{:S(2)}, u32[]{:S(2)}) collective-permute-start(bf16[8,24,896]{2,1,0:T(8,128)(2,1)S(1)} %get-tuple-element.211), channel_id=1, source_target_pairs={{0,8},{8,0},{16,24},{24,16},{32,40},{40,32},{48,56},{56,48},{64,72... | collective-permute-start | bytes 1032200 | tf_op jit(solution)/shard_map/cond/branch_0_fun/ppermute | solution.py:12
  335.4 1.0 copy-start.15
  338.9 0.9 copy-start.10
  339.0 1.2 copy-start.11

commit v5 on v4

--- a/solution.py
+++ b/solution.py
@@ -1,3 +1,5 @@
+import functools
+
 import jax
 import jax.numpy as jnp
 from jax import lax
@@ -24,9 +26,28 @@
     return lax.all_to_all(x, "dp", 0, 0, axis_index_groups=groups, tiled=True)
 
 
+def rows_from_above(x, at):
+    segments, peers = lax.axis_size("pipe"), lax.axis_size("dp")
+    few = peers // 4
+    others = [p for p in range(segments) if p not in (at, at + 1)]
+    groups = [
+        [p * peers + 4 * k + r for p in two for k in range(few)]
+        for two in ([at, at + 1], others)
+        for r in range(4)
+    ]
+    x = lax.all_to_all(copies(x, 2 * few), ("pipe", "dp"), 0, 0, axis_index_groups=groups, tiled=True)
+    return x[few:]
+
+
 def swap_middle(x, mate):
     segments, peers = lax.axis_size("pipe"), lax.axis_size("dp")
     pairs = [(p * peers + i, p * peers + (i ^ mate)) for p in range(1, segments - 1) for i in range(peers)]
+    return lax.ppermute(x, ("pipe", "dp"), pairs)
+
+
+def swap_in_group(x, group, mate):
+    peers = lax.axis_size("dp")
+    pairs = [(group * peers + i, group * peers + (i ^ mate)) for i in range(peers)]
     return lax.ppermute(x, ("pipe", "dp"), pairs)
 
 
@@ -109,12 +130,6 @@
                 place = (units_y ^ tokens_y) * few + z // 2
                 moves.append(((group * peers + i) * parts + z, (group * peers + to) * parts + place))
 
-    def middle_weights():
-        return (
-            jnp.concatenate([up_other, swap_middle(up_other, 1)], axis=1),
-            jnp.concatenate([down_other, swap_middle(down_other, 1)], axis=0),
-            lax.ppermute(slope, ("pipe", "dp", "tensor"), moves),
-        )
 
     def second_half(arriving, back):
         d_up = (back * slope).astype(BF16)
@@ -133,8 +148,7 @@
         return own_units(features_exchange(copies(hidden, parts)))
 
     def after(x, y):
-        first = y[(0,) * y.ndim]
-        return jnp.where(jnp.isnan(first), first, x)
+        return jnp.where(jnp.isnan(y), y, x)
 
     def weight_grads(all_in, all_hidden, full_back, full_d_up):
         grad_up = by_rows(all_in, own_units(full_d_up)).astype(BF16)
@@ -147,15 +161,16 @@
         out, full_d_up, part = second_half(arriving, back)
         return out, after(full_back, part), full_d_up
 
-    def middle_tick(arriving):
-        row_back = row_exchange(copies(arriving, few))
+    def middle_tick(at, row_back):
+        up_mate = jnp.concatenate([up_other, swap_in_group(up_other, at, 1)], axis=1)
+        arriving = lax.dynamic_index_in_dim(row_back, lax.axis_index("dp") // 4, 0, keepdims=False)
         part = jnp.concatenate([by_cols(row_back, down_w), by_cols(row_back, down_mate)], axis=0)
         back = add_blocks(features_exchange(part))
         d_up = (back * middle_slope).astype(BF16)
         row_d_up = features_exchange(copies(d_up, parts))
         part = cols_product(row_d_up[:few], up_w) + cols_product(row_d_up[few:], up_mate)
         mixed = add_blocks(row_exchange(part.astype(BF16)))
-        return (arriving.astype(F32) + mixed).astype(BF16), row_back, row_d_up
+        return (arriving.astype(F32) + mixed).astype(BF16), row_d_up
 
     def own_row_first(x):
         x = x.reshape((few, 2) + x.shape[1:])
@@ -165,37 +180,43 @@
         )
 
     def middle_grads(row_back, row_d_up):
+        full_hidden = features_exchange(copies(hidden, parts))
+        row_d_up = after(row_d_up, full_hidden)
+        row_back = after(row_back, full_hidden[:few, :, :width])
         all_back = jnp.concatenate([row_back, swap_mates(row_back, 2)], axis=0)
         all_d_up = jnp.concatenate([row_d_up[:few], swap_mates(row_d_up[few:], 2)], axis=0)
-        all_hidden = own_units(own_row_first(features_exchange(copies(hidden, parts))))
+        all_hidden = own_units(own_row_first(full_hidden))
         return weight_grads(both_cores(own_row_first(full_in)), all_hidden, all_back, all_d_up)
 
     def first_tick():
-        return second_half(fresh, sums[block:])[:2]
-
-    out, full_d_up = lax.cond(
-        segment == last,
-        first_tick,
-        lambda: (jnp.zeros((block, width), BF16), jnp.zeros((parts, block, 2 * units), BF16)),
-    )
-    up_mate, down_mate, middle_slope = lax.cond(
+        return second_half(fresh, sums[block:])[:2] + (jnp.zeros(slope.shape, BF16),)
+
+    down_mate = lax.cond(
         jnp.logical_and(segment > 0, segment < last),
-        middle_weights,
-        lambda: (jnp.zeros_like(up_w), jnp.zeros_like(down_w), jnp.zeros_like(slope)),
-    )
-    row_back = jnp.zeros((few, block, width), BF16)
-    row_d_up = jnp.zeros((parts, block, 2 * units), BF16)
+        lambda: jnp.concatenate([down_other, swap_middle(down_other, 1)], axis=0),
+        lambda: jnp.zeros_like(down_w),
+    )
+
+    def skip_first():
+        moved = lax.ppermute(slope.astype(BF16), ("pipe", "dp", "tensor"), moves)
+        return down_mate[:block], jnp.zeros((parts, block, 2 * units), BF16), moved
+
+    out, full_d_up, middle_slope = lax.cond(segment == last, first_tick, skip_first)
+    outs, kept_back, kept_d_up = [out], [], []
     for at in range(last - 1, 0, -1):
-        received = lax.ppermute(out, "pipe", [(at + 1, at)])
-        out, row_back, row_d_up = lax.cond(
+        row_back = rows_from_above(out, at)
+        out, row_d_up = lax.cond(
             segment == at,
-            lambda received, out, row_back, row_d_up: middle_tick(received),
-            lambda received, out, row_back, row_d_up: (out, row_back, row_d_up),
-            received,
-            out,
+            functools.partial(middle_tick, at),
+            lambda row_back: (
+                jnp.zeros((block, width), BF16),
+                jnp.zeros((parts, block, 2 * units), BF16),
+            ),
             row_back,
-            row_d_up,
         )
+        outs.append(out)
+        kept_back.append(row_back)
+        kept_d_up.append(row_d_up)
     all_in, all_hidden = lax.cond(
         segment == 0,
         lambda: (both_cores(full_in), own_hidden()),
@@ -210,14 +231,14 @@
         out, full_back, full_d_up = tick(received)
         return (out,) + weight_grads(all_in, all_hidden, full_back, full_d_up)
 
-    def end_middle():
-        return (out,) + middle_grads(row_back, row_d_up)
+    def end_middle(k):
+        return lambda: (outs[k + 1],) + middle_grads(kept_back[k], kept_d_up[k])
 
     def end_highest():
-        return (out,) + weight_grads(both_cores(full_in), own_hidden(), full_back, full_d_up)
-
-    which = jnp.where(segment == 0, 0, jnp.where(segment == last, 2, 1))
-    out, grad_up, grad_down = lax.switch(which, (end_lowest, end_middle, end_highest))
+        return (outs[0],) + weight_grads(both_cores(full_in), own_hidden(), full_back, full_d_up)
+
+    ends = [end_lowest] + [end_middle(last - 1 - at) for at in range(1, last)] + [end_highest]
+    out, grad_up, grad_down = lax.switch(segment, ends)
     grads_in = jnp.swapaxes(out.reshape(rows, micro_count, width), 0, 1)
     return grads_in[None], grad_up[None], grad_down[None]
 

time: 342 us -> 335 us (0.980)
  starting transfers between devices: 60.7 us -> 102 us
  waiting for transfers between devices: 166 us -> 131 us
  blocking collectives: 78.5 us -> 67 us
    ppermute x1, waiting for transfers between devices: 121 us -> 75.5 us  [body(): received = lax.ppermute(out, 'pipe', [(1, 0)])]
    all_to_all x0 -> x2, starting transfers between devices: none -> 39.7 us  [rows_from_above(): lax.all_to_all(copies(x, 2 * few), ('pipe', 'dp'), 0, 0, axis_index_group...]
    all_to_all x0 -> x2, waiting for transfers between devices: none -> 10.9 us  [rows_from_above(): lax.all_to_all(copies(x, 2 * few), ('pipe', 'dp'), 0, 0, axis_index_group...]
    all_to_all x3, blocking collectives: 61.7 us -> 54.3 us  [features_exchange(): return lax.all_to_all(x, 'tensor', 0, 0, tiled=True)]
    all_to_all x1, blocking collectives: 16.8 us -> 12.8 us  [chips_exchange(): return lax.all_to_all(x, 'dp', 0, 0, axis_index_groups=groups, tiled=True)]
    another operation x9 -> x8, local copies, waits for them, and re-layouts: 6.99 us -> 4.04 us
  transfers between devices with their start and end apart: 14 -> 15, of which waited for: 5 -> 6; matrix products, arithmetic and copies ran while one was open for 6% -> 5% of each run, Pallas kernels for 0% -> 0%
where the time goes in v5:
time: 335 us; the launch traced here: 332 us
  waiting for transfers between devices  131 us (39%)
  starting transfers between devices  102 us (30%)
  blocking collectives  67 us (20%)
  local copies, waits for them, and re-layouts  14.5 us (4%)
  matrix products  10.1 us (3%)
  other arithmetic  6.64 us (2%)
    ppermute x1, waiting for transfers between devices, body(): received = lax.ppermute(out, 'pipe', [(1, 0)])  75.5 us
    all_to_all x3, blocking collectives, features_exchange(): return lax.all_to_all(x, 'tensor', 0, 0, tiled=True)  54.3 us
    ppermute x6, starting transfers between devices, swap_cores(): return lax.ppermute(x, 'dp', [(i, i ^ 1) for i in range(peers)])  40.5 us
    all_to_all x2, starting transfers between devices, rows_from_above(): lax.all_to_all(copies(x, 2 * few), ('pipe', 'dp'), 0, 0, axis_index_group...  39.7 us
    all_to_all x1, waiting for transfers between devices, features_exchange(): return lax.all_to_all(x, 'tensor', 0, 0, tiled=True)  30.9 us
    all_to_all x1, blocking collectives, chips_exchange(): return lax.all_to_all(x, 'dp', 0, 0, axis_index_groups=groups, tiled=True)  12.8 us
    all_to_all x2, waiting for transfers between devices, chips_exchange(): return lax.all_to_all(x, 'dp', 0, 0, axis_index_groups=groups, tiled=True)  11.9 us
    all_to_all x2, waiting for transfers between devices, rows_from_above(): lax.all_to_all(copies(x, 2 * few), ('pipe', 'dp'), 0, 0, axis_index_group...  10.9 us
  transfers between devices with their start and end apart: 15, of which 6 were waited for; matrix products, arithmetic and copies ran while one was open for 5% of the time, Pallas kernels for 0%

profile of v5, /device:TPU:1, one launch (start us, length us, event | category | flops | bytes accessed | tf_op | source)
XLA Modules:
  0.0 332.2 jit_solution(16337663165551836504)
XLA Ops:
  0.6 8.9 %collective-permute-start.25 = (bf16[512,896]{1,0:T(8,128)(2,1)}, bf16[512,896]{1,0:T(8,128)(2,1)S(1)}, u32[]{:S(2)}, u32[]{:S(2)}) collective-permute-start(bf16[512,896]{1,0:T(8,128)(2,1)} %bitcast.55), channel_id=1, source_target_pairs={{0,8},{8,0},{16,24},{24,16},{32,40},{40,32},{48,56},{56,48},{64,72... | collective-permute-start | bytes 2752520 | tf_op jit(solution)/shard_map/ppermute | solution.py:14
  9.6 0.7 broadcast_compare_fusion.7
  11.0 0.8 reshape.81
  11.8 0.8 copy.34
  12.9 0.1 select_select_fusion
  13.0 0.8 broadcast_in_dim.311
  13.8 3.9 %all-to-all-start.16 = ((bf16[8,48,512]{2,1,0:T(8,128)(2,1)}), bf16[8,48,512]{2,1,0:T(8,128)(2,1)S(1)}, u32[]{:S(2)}, u32[]{:S(2)}) async-start(bf16[8,48,512]{2,1,0:T(8,128)(2,1)} %broadcast_in_dim.311), calls=%async_computation.16 | async-start | bytes 786432 | tf_op jit(solution)/shard_map/all_to_all | solution.py:20
  17.7 2.2 collective-permute-start.26
  19.9 11.9 %all-to-all-done.16 = bf16[8,48,512]{2,1,0:T(8,128)(2,1)S(1)} async-done(((bf16[8,48,512]{2,1,0:T(8,128)(2,1)}), bf16[8,48,512]{2,1,0:T(8,128)(2,1)S(1)}, u32[]{:S(2)}, u32[]{:S(2)}) %all-to-all-start.16) | async-done | bytes 393248 | tf_op jit(solution)/shard_map/all_to_all | solution.py:20
  31.9 2.2 convolution_convert_fusion.6
  34.1 0.7 convolution_convert_fusion.5
  34.8 0.2 copy-done.8
  35.0 1.2 pad_maximum_fusion.15
  36.2 10.0 %all-to-all-start.17 = ((bf16[8,48,1792]{2,1,0:T(8,128)(2,1)}), bf16[8,48,1792]{2,1,0:T(8,128)(2,1)S(1)}, u32[]{:S(2)}, u32[]{:S(2)}) async-start(bf16[8,48,1792]{2,1,0:T(8,128)(2,1)} %pad_maximum_fusion.15), calls=%async_computation.17 | async-start | bytes 2752512 | tf_op jit(solution)/shard_map/all_to_all | solution.py:59
  46.2 0.7 collective-permute-start.24
  46.9 1.6 collective-permute-start.27
  48.6 0.1 conditional.6
  48.6 0.1 broadcast.97
  48.7 1.2 copy-done
  49.9 1.6 pad_maximum_fusion.13
  51.5 30.9 %all-to-all-done.17 = bf16[8,48,1792]{2,1,0:T(8,128)(2,1)S(1)} async-done(((bf16[8,48,1792]{2,1,0:T(8,128)(2,1)}), bf16[8,48,1792]{2,1,0:T(8,128)(2,1)S(1)}, u32[]{:S(2)}, u32[]{:S(2)}) %all-to-all-start.17) | async-done | bytes 1376288 | tf_op jit(solution)/shard_map/all_to_all | solution.py:59
  82.4 0.2 convert_reduce_fusion.7
  82.7 2.5 conditional.7
  82.8 0.8 collective-permute-start
  83.6 0.7 slice.98
  84.3 0.9 broadcast.98
  85.2 0.7 broadcast_in_dim.312
  85.9 6.8 %all-to-all-start.18 = ((bf16[8,24,512]{2,1,0:T(8,128)(2,1)}), bf16[8,24,512]{2,1,0:T(8,128)(2,1)S(1)}, u32[]{:S(2)}, u32[]{:S(2)}) async-start(bf16[8,24,512]{2,1,0:T(8,128)(2,1)} %broadcast_in_dim.312), calls=%async_computation.18 | async-start | bytes 393216 | tf_op jit(solution)/shard_map/all_to_all | solution.py:38
  92.7 2.6 pad_maximum_fusion.14
  95.3 3.4 %all-to-all-done.18 = bf16[8,24,512]{2,1,0:T(8,128)(2,1)S(1)} async-done(((bf16[8,24,512]{2,1,0:T(8,128)(2,1)}), bf16[8,24,512]{2,1,0:T(8,128)(2,1)S(1)}, u32[]{:S(2)}, u32[]{:S(2)}) %all-to-all-start.18) | async-done | bytes 196640 | tf_op jit(solution)/shard_map/all_to_all | solution.py:38
  98.7 0.9 conditional.8
  98.7 0.9 broadcast.101
  99.6 0.7 broadcast_in_dim.313
  100.3 32.8 %all-to-all-start.19 = ((bf16[8,24,512]{2,1,0:T(8,128)(2,1)}), bf16[8,24,512]{2,1,0:T(8,128)(2,1)S(1)}, u32[]{:S(2)}, u32[]{:S(2)}) async-start(bf16[8,24,512]{2,1,0:T(8,128)(2,1)} %broadcast_in_dim.313), calls=%async_computation.19 | async-start | bytes 393216 | tf_op jit(solution)/shard_map/all_to_all | solution.py:38
  133.1 7.6 %all-to-all-done.19 = bf16[8,24,512]{2,1,0:T(8,128)(2,1)S(1)} async-done(((bf16[8,24,512]{2,1,0:T(8,128)(2,1)}), bf16[8,24,512]{2,1,0:T(8,128)(2,1)S(1)}, u32[]{:S(2)}, u32[]{:S(2)}) %all-to-all-start.19) | async-done | bytes 196640 | tf_op jit(solution)/shard_map/all_to_all | solution.py:38
  140.7 1.0 conditional.9
  140.8 1.0 broadcast.103
  141.7 1.3 collective-permute-start.28
  143.0 0.7 fusion.113
  143.7 29.8 %conditional.10 = (bf16[16,24,512]{2,1,0:T(8,128)(2,1)S(1)}, bf16[16,24,896]{2,1,0:T(8,128)(2,1)S(1)}) conditional(s32[]{:T(128)} %convert_element_type.163, () %tuple.77, (bf16[8,24,512]{2,1,0:T(8,128)(2,1)S(1)}, bf16[24,1792]{1,0:T(8,128)(2,1)S(1)}) %tuple.78), branch_computations={%region_14.15_spmd, %region_15.16_spmd} | conditional | flops 540672 | bytes 7852128 | solution.py:220
  143.8 17.7 %all_to_all.88 = bf16[8,24,1792]{2,1,0:T(8,128)(2,1)S(1)} all-to-all(bf16[8,24,1792]{2,1,0:T(8,128)(2,1)S(1)} %broadcast_in_dim.195), channel_id=1, replica_groups=mesh['pipe'=4,'dp'=16,'tensor'=8] {'tensor'}, dimensions={0} | all-to-all | bytes 1376256 | tf_op jit(solution)/shard_map/cond/branch_1_fun/all_to_all | solution.py:59
  161.6 8.6 %collective-permute-start.3 = (bf16[8,24,896]{2,1,0:T(8,128)(2,1)S(1)}, bf16[8,24,896]{2,1,0:T(8,128)(2,1)S(1)}, u32[]{:S(2)}, u32[]{:S(2)}) collective-permute-start(bf16[8,24,896]{2,1,0:T(8,128)(2,1)S(1)} %get-tuple-element.169), channel_id=1, source_target_pairs={{0,8},{8,0},{16,24},{24,16},{32,40},{40,32},{48,56},{56,48},{64,72... | collective-permute-start | bytes 1032200 | tf_op jit(solution)/shard_map/cond/branch_1_fun/ppermute | solution.py:14
  170.1 1.9 collective-permute-start.2
  172.1 1.4 collective-permute-done.2
  173.6 75.5 %collective-permute-done.28 = bf16[24,512]{1,0:T(8,128)(2,1)S(1)} collective-permute-done((bf16[24,512]{1,0:T(8,128)(2,1)S(1)}, bf16[24,512]{1,0:T(8,128)(2,1)S(1)}, u32[]{:S(2)}, u32[]{:S(2)}) %collective-permute-start.28) | collective-permute-done | bytes 24608 | tf_op jit(solution)/shard_map/ppermute | solution.py:228
  249.0 81.9 %conditional.11 = (bf16[24,512]{1,0:T(8,128)(2,1)S(1)}, bf16[1,512,896]{2,1,0:T(8,128)(2,1)S(1)}, bf16[1,896,512]{2,1,0:T(8,128)(2,1)S(1)}) conditional(s32[]{:T(128)} %clamp.3, (bf16[24,512]{1,0:T(8,128)(2,1)S(1)}, bf16[1792,512]{1,0:T(8,128)(2,1)}, f32[24,1792]{1,0:T(8,128)S(1)}, bf16[512,1792]{1,0:T(8,128)(2,1)S(1)}, ...), branch_computations={%region_16.19_spmd, %region_19.20_spmd, %region_20.21_spmd, %regio... | conditional | flops 1412335616 | bytes 27926748 | solution.py:241
  249.1 12.8 %all_to_all.89 = bf16[8,24,512]{2,1,0:T(8,128)(2,1)S(1)} all-to-all(bf16[8,24,512]{2,1,0:T(8,128)(2,1)S(1)} %broadcast_in_dim.196), channel_id=1, replica_groups={{0,16,32,48,64,80,96,112},{8,24,40,56,72,88,104,120},{1,17,33,49,65,81,..., dimensions={0} | all-to-all | bytes 393216 | tf_op jit(solution)/shard_map/cond/branch_0_fun/all_to_all | solution.py:20
  261.8 2.2 convolution_convert_fusion.4
  264.1 17.3 %all_to_all.90 = bf16[8,24,1792]{2,1,0:T(8,128)(2,1)S(1)} all-to-all(bf16[8,24,1792]{2,1,0:T(8,128)(2,1)S(1)} %convolution_convert_fusion.4), channel_id=1, replica_groups=mesh['pipe'=4,'dp'=16,'tensor'=8] {'tensor'}, dimensions={0} | all-to-all | bytes 1376256 | tf_op jit(solution)/shard_map/cond/branch_0_fun/all_to_all | solution.py:59
  281.4 0.1 convert_reduce_fusion.5
  281.6 19.3 %all_to_all.91 = bf16[8,24,1792]{2,1,0:T(8,128)(2,1)S(1)} all-to-all(bf16[8,24,1792]{2,1,0:T(8,128)(2,1)S(1)} %broadcast_in_dim.197), channel_id=1, replica_groups=mesh['pipe'=4,'dp'=16,'tensor'=8] {'tensor'}, dimensions={0} | all-to-all | bytes 1376256 | tf_op jit(solution)/shard_map/cond/branch_0_fun/all_to_all | solution.py:59
  300.8 1.5 compare_select_fusion
  302.4 3.4 %all-to-all-start.15 = ((bf16[8,24,512]{2,1,0:T(8,128)(2,1)}), bf16[8,24,512]{2,1,0:T(8,128)(2,1)S(1)}, u32[]{:S(2)}, u32[]{:S(2)}) async-start(bf16[8,24,512]{2,1,0:T(8,128)(2,1)} %get-tuple-element.173), calls=%async_computation.15 | async-start | bytes 393216 | tf_op jit(solution)/shard_map/cond/branch_0_fun/all_to_all | solution.py:20
  305.7 16.9 %collective-permute-start.23 = (bf16[8,24,512]{2,1,0:T(8,128)(2,1)}, bf16[8,24,512]{2,1,0:T(8,128)(2,1)S(1)}, u32[]{:S(2)}, u32[]{:S(2)}) collective-permute-start(bf16[8,24,512]{2,1,0:T(8,128)(2,1)} %get-tuple-element.172), channel_id=1, source_target_pairs={{0,8},{8,0},{16,24},{24,16},{32,40},{40,32},{48,56},{56,48},{64,72... | collective-permute-start | bytes 589832 | tf_op jit(solution)/shard_map/cond/branch_0_fun/ppermute | solution.py:14
  322.7 0.8 fusion.108
  323.5 1.9 collective-permute-start.22
  325.4 1.6 fusion.31
  327.1 0.5 copy.15
  327.7 0.7 copy-done.15
  328.4 1.8 fusion.30
  330.2 0.6 copy.14
  331.0 0.7 reshape.82
  331.7 0.2 copy-done.10
  331.9 0.3 copy-done.11
  (77 shorter events, 1.5 us)
Async XLA Ops:
  0.6 17.1 %copy-start.5 = (bf16[1,896,512]{2,1,0:T(8,128)(2,1)S(1)}, bf16[1,896,512]{2,1,0:T(8,128)(2,1)}, u32[]{:S(2)}) copy-start(bf16[1,896,512]{2,1,0:T(8,128)(2,1)} %param.23) | copy-start | bytes 2752516
  0.6 31.2 %collective-permute-start.25 = (bf16[512,896]{1,0:T(8,128)(2,1)}, bf16[512,896]{1,0:T(8,128)(2,1)S(1)}, u32[]{:S(2)}, u32[]{:S(2)}) collective-permute-start(bf16[512,896]{1,0:T(8,128)(2,1)} %bitcast.55), channel_id=1, source_target_pairs={{0,8},{8,0},{16,24},{24,16},{32,40},{40,32},{48,56},{56,48},{64,72... | collective-permute-start | bytes 2752520 | tf_op jit(solution)/shard_map/ppermute | solution.py:14
  13.8 18.1 %all-to-all-start.16 = ((bf16[8,48,512]{2,1,0:T(8,128)(2,1)}), bf16[8,48,512]{2,1,0:T(8,128)(2,1)S(1)}, u32[]{:S(2)}, u32[]{:S(2)}) async-start(bf16[8,48,512]{2,1,0:T(8,128)(2,1)} %broadcast_in_dim.311), calls=%async_computation.16 | async-start | bytes 786432 | tf_op jit(solution)/shard_map/all_to_all | solution.py:20
  17.7 16.4 %collective-permute-start.26 = (bf16[896,512]{1,0:T(8,128)(2,1)S(1)}, bf16[896,512]{1,0:T(8,128)(2,1)S(1)}, u32[]{:S(2)}, u32[]{:S(2)}) collective-permute-start(bf16[896,512]{1,0:T(8,128)(2,1)S(1)} %bitcast.223), channel_id=1, source_target_pairs={{0,8},{8,0},{16,24},{24,16},{32,40},{40,32},{48,56},{56,48},{64,72... | collective-permute-start | bytes 2752520 | tf_op jit(solution)/shard_map/ppermute | solution.py:14
  31.9 2.2 copy-start.3
  31.9 2.2 copy-start.7
  34.1 0.9 copy-start.8
  36.2 46.2 %all-to-all-start.17 = ((bf16[8,48,1792]{2,1,0:T(8,128)(2,1)}), bf16[8,48,1792]{2,1,0:T(8,128)(2,1)S(1)}, u32[]{:S(2)}, u32[]{:S(2)}) async-start(bf16[8,48,1792]{2,1,0:T(8,128)(2,1)} %pad_maximum_fusion.15), calls=%async_computation.17 | async-start | bytes 2752512 | tf_op jit(solution)/shard_map/all_to_all | solution.py:59
  46.2 2.3 collective-permute-start.24
  46.9 51.7 %collective-permute-start.27 = (bf16[512,896]{1,0:T(8,128)(2,1)}, bf16[512,896]{1,0:T(8,128)(2,1)}, u32[]{:S(2)}, u32[]{:S(2)}) collective-permute-start(bf16[512,896]{1,0:T(8,128)(2,1)} %bitcast.55), channel_id=1, source_target_pairs={{128,144},{136,152},{144,128},{152,136},{160,176},{168,184},{176,1... | collective-permute-start | bytes 2752520 | tf_op jit(solution)/shard_map/ppermute | solution.py:45
  48.7 1.2 copy-start
  82.7 10.0 %copy-start.6 = (bf16[1,896,512]{2,1,0:T(8,128)(2,1)S(1)}, bf16[1,896,512]{2,1,0:T(8,128)(2,1)}, u32[]{:S(2)}) copy-start(bf16[1,896,512]{2,1,0:T(8,128)(2,1)} %param.23) | copy-start | bytes 2752516
  82.8 1.5 collective-permute-start
  85.9 12.8 %all-to-all-start.18 = ((bf16[8,24,512]{2,1,0:T(8,128)(2,1)}), bf16[8,24,512]{2,1,0:T(8,128)(2,1)S(1)}, u32[]{:S(2)}, u32[]{:S(2)}) async-start(bf16[8,24,512]{2,1,0:T(8,128)(2,1)} %broadcast_in_dim.312), calls=%async_computation.18 | async-start | bytes 393216 | tf_op jit(solution)/shard_map/all_to_all | solution.py:38
  100.3 40.4 %all-to-all-start.19 = ((bf16[8,24,512]{2,1,0:T(8,128)(2,1)}), bf16[8,24,512]{2,1,0:T(8,128)(2,1)S(1)}, u32[]{:S(2)}, u32[]{:S(2)}) async-start(bf16[8,24,512]{2,1,0:T(8,128)(2,1)} %broadcast_in_dim.313), calls=%async_computation.19 | async-start | bytes 393216 | tf_op jit(solution)/shard_map/all_to_all | solution.py:38
  140.7 2.3 copy-start.4
  141.7 107.3 %collective-permute-start.28 = (bf16[24,512]{1,0:T(8,128)(2,1)S(1)}, bf16[24,512]{1,0:T(8,128)(2,1)S(1)}, u32[]{:S(2)}, u32[]{:S(2)}) collective-permute-start(bf16[24,512]{1,0:T(8,128)(2,1)S(1)} %get-tuple-element.153), channel_id=1, source_target_pairs={{128,0},{129,1},{130,2},{131,3},{132,4},{133,5},{134,6},{135,7},{1... | collective-permute-start | bytes 73736 | tf_op jit(solution)/shard_map/ppermute | solution.py:228
  161.6 11.9 %collective-permute-start.3 = (bf16[8,24,896]{2,1,0:T(8,128)(2,1)S(1)}, bf16[8,24,896]{2,1,0:T(8,128)(2,1)S(1)}, u32[]{:S(2)}, u32[]{:S(2)}) collective-permute-start(bf16[8,24,896]{2,1,0:T(8,128)(2,1)S(1)} %get-tuple-element.169), channel_id=1, source_target_pairs={{0,8},{8,0},{16,24},{24,16},{32,40},{40,32},{48,56},{56,48},{64,72... | collective-permute-start | bytes 1032200 | tf_op jit(solution)/shard_map/cond/branch_1_fun/ppermute | solution.py:14
  170.1 3.3 %collective-permute-start.2 = (bf16[8,24,512]{2,1,0:T(8,128)(2,1)S(1)}, bf16[8,24,512]{2,1,0:T(8,128)(2,1)S(1)}, u32[]{:S(2)}, u32[]{:S(2)}) collective-permute-start(bf16[8,24,512]{2,1,0:T(8,128)(2,1)S(1)} %get-tuple-element.110), channel_id=1, source_target_pairs={{0,8},{8,0},{16,24},{24,16},{32,40},{40,32},{48,56},{56,48},{64,72... | collective-permute-start | bytes 589832 | tf_op jit(solution)/shard_map/cond/branch_1_fun/ppermute | solution.py:14
  249.0 12.8 %copy-start.12 = (bf16[16,24,512]{2,1,0:T(8,128)(2,1)}, bf16[16,24,512]{2,1,0:T(8,128)(2,1)S(1)}, u32[]{:S(2)}) copy-start(bf16[16,24,512]{2,1,0:T(8,128)(2,1)S(1)} %get-tuple-element.116) | copy-start | bytes 1179652 | tf_op jit(solution)/shard_map/cond
  302.4 25.3 %all-to-all-start.15 = ((bf16[8,24,512]{2,1,0:T(8,128)(2,1)}), bf16[8,24,512]{2,1,0:T(8,128)(2,1)S(1)}, u32[]{:S(2)}, u32[]{:S(2)}) async-start(bf16[8,24,512]{2,1,0:T(8,128)(2,1)} %get-tuple-element.173), calls=%async_computation.15 | async-start | bytes 393216 | tf_op jit(solution)/shard_map/cond/branch_0_fun/all_to_all | solution.py:20
  305.7 19.7 %collective-permute-start.23 = (bf16[8,24,512]{2,1,0:T(8,128)(2,1)}, bf16[8,24,512]{2,1,0:T(8,128)(2,1)S(1)}, u32[]{:S(2)}, u32[]{:S(2)}) collective-permute-start(bf16[8,24,512]{2,1,0:T(8,128)(2,1)} %get-tuple-element.172), channel_id=1, source_target_pairs={{0,8},{8,0},{16,24},{24,16},{32,40},{40,32},{48,56},{56,48},{64,72... | collective-permute-start | bytes 589832 | tf_op jit(solution)/shard_map/cond/branch_0_fun/ppermute | solution.py:14
  323.5 4.2 %collective-permute-start.22 = (bf16[8,24,896]{2,1,0:T(8,128)(2,1)S(1)}, bf16[8,24,896]{2,1,0:T(8,128)(2,1)S(1)}, u32[]{:S(2)}, u32[]{:S(2)}) collective-permute-start(bf16[8,24,896]{2,1,0:T(8,128)(2,1)S(1)} %get-tuple-element.171), channel_id=1, source_target_pairs={{0,8},{8,0},{16,24},{24,16},{32,40},{40,32},{48,56},{56,48},{64,72... | collective-permute-start | bytes 1032200 | tf_op jit(solution)/shard_map/cond/branch_0_fun/ppermute | solution.py:14
  327.1 1.4 copy-start.13
  327.7 0.7 copy-start.15
  331.0 0.9 copy-start.10
  331.0 1.2 copy-start.11

commit v6 on v5

--- a/solution.py
+++ b/solution.py
@@ -131,8 +131,12 @@
                 moves.append(((group * peers + i) * parts + z, (group * peers + to) * parts + place))
 
 
-    def second_half(arriving, back):
+    def second_half(arriving, back, stagger=False):
         d_up = (back * slope).astype(BF16)
+        if stagger:
+            pairs = [(last * peers + i, last * peers + (i ^ 4)) for i in range(0, peers, 2)]
+            step = lax.ppermute(d_up, ("pipe", "dp"), pairs)
+            d_up = after(d_up, step)
         full_d_up = features_exchange(copies(d_up, parts))
         part = by_cols(full_d_up, up_w)
         mixed = add_blocks(chips_exchange(part))
@@ -150,16 +154,19 @@
     def after(x, y):
         return jnp.where(jnp.isnan(y), y, x)
 
+    def weight_products(all_in, all_hidden, all_back, full_d_up):
+        grad_up = by_rows(all_in, own_units(full_d_up)).astype(BF16)
+        grad_down = by_rows(all_hidden, all_back).astype(BF16)
+        return grad_up, grad_down
+
     def weight_grads(all_in, all_hidden, full_back, full_d_up):
-        grad_up = by_rows(all_in, own_units(full_d_up)).astype(BF16)
-        grad_down = by_rows(all_hidden, both_cores(full_back)).astype(BF16)
-        return grad_up, grad_down
+        return weight_products(all_in, all_hidden, both_cores(full_back), full_d_up)
 
     def tick(arriving):
         full_back = chips_exchange(copies(arriving, chips))
         back = add_blocks(features_exchange(by_cols(full_back, down_w)))
         out, full_d_up, part = second_half(arriving, back)
-        return out, after(full_back, part), full_d_up
+        return out, full_back, full_d_up, part
 
     def middle_tick(at, row_back):
         up_mate = jnp.concatenate([up_other, swap_in_group(up_other, at, 1)], axis=1)
@@ -189,7 +196,7 @@
         return weight_grads(both_cores(own_row_first(full_in)), all_hidden, all_back, all_d_up)
 
     def first_tick():
-        return second_half(fresh, sums[block:])[:2] + (jnp.zeros(slope.shape, BF16),)
+        return second_half(fresh, sums[block:], True)[:2] + (jnp.zeros(slope.shape, BF16),)
 
     down_mate = lax.cond(
         jnp.logical_and(segment > 0, segment < last),
@@ -228,8 +235,10 @@
     received = lax.ppermute(out, "pipe", [(1, 0)])
 
     def end_lowest():
-        out, full_back, full_d_up = tick(received)
-        return (out,) + weight_grads(all_in, all_hidden, full_back, full_d_up)
+        out, full_back, full_d_up, part = tick(received)
+        held = after(full_back[:1], part[:1])
+        all_back = jnp.concatenate([held, full_back[1:], swap_cores(full_back)], axis=0)
+        return (out,) + weight_products(all_in, all_hidden, all_back, full_d_up)
 
     def end_middle(k):
         return lambda: (outs[k + 1],) + middle_grads(kept_back[k], kept_d_up[k])

time: 335 us -> 328 us (0.979)
  blocking collectives: 67 us -> 49.3 us
  starting transfers between devices: 102 us -> 118 us
  waiting for transfers between devices: 131 us -> 126 us
    ppermute x6, starting transfers between devices: 40.5 us -> 58.8 us  [swap_cores(): return lax.ppermute(x, 'dp', [(i, i ^ 1) for i in range(peers)])]
    all_to_all x3 -> x2, blocking collectives: 54.3 us -> 37.2 us  [features_exchange(): return lax.all_to_all(x, 'tensor', 0, 0, tiled=True)]
    ppermute x1, waiting for transfers between devices: 75.5 us -> 69.3 us  [body(): received = lax.ppermute(out, 'pipe', [(1, 0)])]
    all_to_all x2, starting transfers between devices: 39.7 us -> 33.8 us  [rows_from_above(): lax.all_to_all(copies(x, 2 * few), ('pipe', 'dp'), 0, 0, axis_index_group...]
    all_to_all x1 -> x2, starting transfers between devices: 10 us -> 13.6 us  [features_exchange(): return lax.all_to_all(x, 'tensor', 0, 0, tiled=True)]
    all_to_all x1 -> x2, waiting for transfers between devices: 30.9 us -> 30.9 us  [features_exchange(): return lax.all_to_all(x, 'tensor', 0, 0, tiled=True)]
  transfers between devices with their start and end apart: 15 -> 16, of which waited for: 6 -> 7; matrix products, arithmetic and copies ran while one was open for 5% -> 6% of each run, Pallas kernels for 0% -> 0%
where the time goes in v6:
time: 328 us; the launch traced here: 325 us
  waiting for transfers between devices  126 us (38%)
  starting transfers between devices  118 us (36%)
  blocking collectives  49.3 us (15%)
  local copies, waits for them, and re-layouts  13.9 us (4%)
  matrix products  9.19 us (3%)
  other arithmetic  7.37 us (2%)
    ppermute x1, waiting for transfers between devices, body(): received = lax.ppermute(out, 'pipe', [(1, 0)])  69.3 us
    ppermute x6, starting transfers between devices, swap_cores(): return lax.ppermute(x, 'dp', [(i, i ^ 1) for i in range(peers)])  58.8 us
    all_to_all x2, blocking collectives, features_exchange(): return lax.all_to_all(x, 'tensor', 0, 0, tiled=True)  37.2 us
    all_to_all x2, starting transfers between devices, rows_from_above(): lax.all_to_all(copies(x, 2 * few), ('pipe', 'dp'), 0, 0, axis_index_group...  33.8 us
    all_to_all x2, waiting for transfers between devices, features_exchange(): return lax.all_to_all(x, 'tensor', 0, 0, tiled=True)  30.9 us
    all_to_all x2, starting transfers between devices, features_exchange(): return lax.all_to_all(x, 'tensor', 0, 0, tiled=True)  13.6 us
    all_to_all x1, blocking collectives, chips_exchange(): return lax.all_to_all(x, 'dp', 0, 0, axis_index_groups=groups, tiled=True)  12.1 us
    all_to_all x2, waiting for transfers between devices, chips_exchange(): return lax.all_to_all(x, 'dp', 0, 0, axis_index_groups=groups, tiled=True)  11.9 us
  transfers between devices with their start and end apart: 16, of which 7 were waited for; matrix products, arithmetic and copies ran while one was open for 6% of the time, Pallas kernels for 0%

profile of v6, /device:TPU:1, one launch (start us, length us, event | category | flops | bytes accessed | tf_op | source)
XLA Modules:
  0.0 324.9 jit_solution(5501962350982367682)
XLA Ops:
  0.6 8.9 %collective-permute-start.26 = (bf16[512,896]{1,0:T(8,128)(2,1)}, bf16[512,896]{1,0:T(8,128)(2,1)S(1)}, u32[]{:S(2)}, u32[]{:S(2)}) collective-permute-start(bf16[512,896]{1,0:T(8,128)(2,1)} %bitcast.55), channel_id=1, source_target_pairs={{0,8},{8,0},{16,24},{24,16},{32,40},{40,32},{48,56},{56,48},{64,72... | collective-permute-start | bytes 2752520 | tf_op jit(solution)/shard_map/ppermute | solution.py:14
  9.6 0.7 broadcast_compare_fusion.7
  11.0 0.8 reshape.81
  11.8 0.8 copy.34
  12.9 0.1 select_select_fusion
  13.0 0.8 broadcast_in_dim.311
  13.8 3.9 %all-to-all-start.16 = ((bf16[8,48,512]{2,1,0:T(8,128)(2,1)}), bf16[8,48,512]{2,1,0:T(8,128)(2,1)S(1)}, u32[]{:S(2)}, u32[]{:S(2)}) async-start(bf16[8,48,512]{2,1,0:T(8,128)(2,1)} %broadcast_in_dim.311), calls=%async_computation.16 | async-start | bytes 786432 | tf_op jit(solution)/shard_map/all_to_all | solution.py:20
  17.7 2.2 collective-permute-start.27
  19.9 11.9 %all-to-all-done.16 = bf16[8,48,512]{2,1,0:T(8,128)(2,1)S(1)} async-done(((bf16[8,48,512]{2,1,0:T(8,128)(2,1)}), bf16[8,48,512]{2,1,0:T(8,128)(2,1)S(1)}, u32[]{:S(2)}, u32[]{:S(2)}) %all-to-all-start.16) | async-done | bytes 393248 | tf_op jit(solution)/shard_map/all_to_all | solution.py:20
  31.9 2.2 convolution_convert_fusion.6
  34.1 0.7 convolution_convert_fusion.5
  34.8 0.2 copy-done.8
  35.0 1.2 pad_maximum_fusion.15
  36.2 10.0 %all-to-all-start.17 = ((bf16[8,48,1792]{2,1,0:T(8,128)(2,1)}), bf16[8,48,1792]{2,1,0:T(8,128)(2,1)S(1)}, u32[]{:S(2)}, u32[]{:S(2)}) async-start(bf16[8,48,1792]{2,1,0:T(8,128)(2,1)} %pad_maximum_fusion.15), calls=%async_computation.17 | async-start | bytes 2752512 | tf_op jit(solution)/shard_map/all_to_all | solution.py:59
  46.2 0.7 collective-permute-start.25
  46.9 1.6 collective-permute-start.28
  48.6 0.1 conditional.6
  48.6 0.1 broadcast.97
  48.7 1.2 copy-done
  49.9 1.6 pad_maximum_fusion.13
  51.5 30.9 %all-to-all-done.17 = bf16[8,48,1792]{2,1,0:T(8,128)(2,1)S(1)} async-done(((bf16[8,48,1792]{2,1,0:T(8,128)(2,1)}), bf16[8,48,1792]{2,1,0:T(8,128)(2,1)S(1)}, u32[]{:S(2)}, u32[]{:S(2)}) %all-to-all-start.17) | async-done | bytes 1376288 | tf_op jit(solution)/shard_map/all_to_all | solution.py:59
  82.4 0.2 convert_reduce_fusion.7
  82.7 2.5 conditional.7
  82.8 0.8 collective-permute-start
  83.6 0.7 slice.104
  84.3 0.9 broadcast.98
  85.2 0.7 broadcast_in_dim.312
  85.9 6.8 %all-to-all-start.18 = ((bf16[8,24,512]{2,1,0:T(8,128)(2,1)}), bf16[8,24,512]{2,1,0:T(8,128)(2,1)S(1)}, u32[]{:S(2)}, u32[]{:S(2)}) async-start(bf16[8,24,512]{2,1,0:T(8,128)(2,1)} %broadcast_in_dim.312), calls=%async_computation.18 | async-start | bytes 393216 | tf_op jit(solution)/shard_map/all_to_all | solution.py:38
  92.7 2.5 pad_maximum_fusion.14
  95.3 3.4 %all-to-all-done.18 = bf16[8,24,512]{2,1,0:T(8,128)(2,1)S(1)} async-done(((bf16[8,24,512]{2,1,0:T(8,128)(2,1)}), bf16[8,24,512]{2,1,0:T(8,128)(2,1)S(1)}, u32[]{:S(2)}, u32[]{:S(2)}) %all-to-all-start.18) | async-done | bytes 196640 | tf_op jit(solution)/shard_map/all_to_all | solution.py:38
  98.7 0.9 conditional.8
  98.7 0.9 broadcast.101
  99.6 0.7 broadcast_in_dim.313
  100.3 26.9 %all-to-all-start.19 = ((bf16[8,24,512]{2,1,0:T(8,128)(2,1)}), bf16[8,24,512]{2,1,0:T(8,128)(2,1)S(1)}, u32[]{:S(2)}, u32[]{:S(2)}) async-start(bf16[8,24,512]{2,1,0:T(8,128)(2,1)} %broadcast_in_dim.313), calls=%async_computation.19 | async-start | bytes 393216 | tf_op jit(solution)/shard_map/all_to_all | solution.py:38
  127.3 7.6 %all-to-all-done.19 = bf16[8,24,512]{2,1,0:T(8,128)(2,1)S(1)} async-done(((bf16[8,24,512]{2,1,0:T(8,128)(2,1)}), bf16[8,24,512]{2,1,0:T(8,128)(2,1)S(1)}, u32[]{:S(2)}, u32[]{:S(2)}) %all-to-all-start.19) | async-done | bytes 196640 | tf_op jit(solution)/shard_map/all_to_all | solution.py:38
  134.9 1.0 conditional.9
  134.9 1.0 broadcast.103
  135.8 1.3 collective-permute-start.29
  137.1 0.7 fusion.115
  137.9 35.1 %conditional.10 = (bf16[16,24,512]{2,1,0:T(8,128)(2,1)S(1)}, bf16[16,24,896]{2,1,0:T(8,128)(2,1)S(1)}) conditional(s32[]{:T(128)} %convert_element_type.163, () %tuple.77, (bf16[8,24,512]{2,1,0:T(8,128)(2,1)S(1)}, bf16[24,1792]{1,0:T(8,128)(2,1)S(1)}) %tuple.78), branch_computations={%region_14.15_spmd, %region_15.16_spmd} | conditional | flops 540672 | bytes 7852128 | solution.py:227
  137.9 16.7 %all_to_all.88 = bf16[8,24,1792]{2,1,0:T(8,128)(2,1)S(1)} all-to-all(bf16[8,24,1792]{2,1,0:T(8,128)(2,1)S(1)} %broadcast_in_dim.195), channel_id=1, replica_groups=mesh['pipe'=4,'dp'=16,'tensor'=8] {'tensor'}, dimensions={0} | all-to-all | bytes 1376256 | tf_op jit(solution)/shard_map/cond/branch_1_fun/all_to_all | solution.py:59
  154.7 14.9 %collective-permute-start.3 = (bf16[8,24,896]{2,1,0:T(8,128)(2,1)S(1)}, bf16[8,24,896]{2,1,0:T(8,128)(2,1)S(1)}, u32[]{:S(2)}, u32[]{:S(2)}) collective-permute-start(bf16[8,24,896]{2,1,0:T(8,128)(2,1)S(1)} %get-tuple-element.169), channel_id=1, source_target_pairs={{0,8},{8,0},{16,24},{24,16},{32,40},{40,32},{48,56},{56,48},{64,72... | collective-permute-start | bytes 1032200 | tf_op jit(solution)/shard_map/cond/branch_1_fun/ppermute | solution.py:14
  169.5 1.9 collective-permute-start.2
  171.5 1.4 collective-permute-done.2
  173.0 69.3 %collective-permute-done.29 = bf16[24,512]{1,0:T(8,128)(2,1)S(1)} collective-permute-done((bf16[24,512]{1,0:T(8,128)(2,1)S(1)}, bf16[24,512]{1,0:T(8,128)(2,1)S(1)}, u32[]{:S(2)}, u32[]{:S(2)}) %collective-permute-start.29) | collective-permute-done | bytes 24608 | tf_op jit(solution)/shard_map/ppermute | solution.py:235
  242.3 81.3 %conditional.11 = (bf16[24,512]{1,0:T(8,128)(2,1)S(1)}, bf16[1,512,896]{2,1,0:T(8,128)(2,1)S(1)}, bf16[1,896,512]{2,1,0:T(8,128)(2,1)S(1)}) conditional(s32[]{:T(128)} %clamp.3, (bf16[24,512]{1,0:T(8,128)(2,1)S(1)}, bf16[1792,512]{1,0:T(8,128)(2,1)}, f32[24,1792]{1,0:T(8,128)S(1)}, bf16[512,1792]{1,0:T(8,128)(2,1)S(1)}, ...), branch_computations={%region_16.19_spmd, %region_19.20_spmd, %region_20.21_spmd, %regio... | conditional | flops 1412360192 | bytes 26869956 | solution.py:250
  242.3 12.1 %all_to_all.89 = bf16[8,24,512]{2,1,0:T(8,128)(2,1)S(1)} all-to-all(bf16[8,24,512]{2,1,0:T(8,128)(2,1)S(1)} %broadcast_in_dim.196), channel_id=1, replica_groups={{0,16,32,48,64,80,96,112},{8,24,40,56,72,88,104,120},{1,17,33,49,65,81,..., dimensions={0} | all-to-all | bytes 393216 | tf_op jit(solution)/shard_map/cond/branch_0_fun/all_to_all | solution.py:20
  254.5 2.2 convolution_convert_fusion.4
  256.7 20.5 %all_to_all.90 = bf16[8,24,1792]{2,1,0:T(8,128)(2,1)S(1)} all-to-all(bf16[8,24,1792]{2,1,0:T(8,128)(2,1)S(1)} %convolution_convert_fusion.4), channel_id=1, replica_groups=mesh['pipe'=4,'dp'=16,'tensor'=8] {'tensor'}, dimensions={0} | all-to-all | bytes 1376256 | tf_op jit(solution)/shard_map/cond/branch_0_fun/all_to_all | solution.py:59
  277.4 0.9 broadcast_in_dim.197
  278.2 3.5 %all-to-all-start.14 = ((bf16[8,24,1792]{2,1,0:T(8,128)(2,1)}), bf16[8,24,1792]{2,1,0:T(8,128)(2,1)S(1)}, u32[]{:S(2)}, u32[]{:S(2)}) async-start(bf16[8,24,1792]{2,1,0:T(8,128)(2,1)} %broadcast_in_dim.197), calls=%async_computation.14 | async-start | bytes 1376256 | tf_op jit(solution)/shard_map/cond/branch_0_fun/all_to_all | solution.py:59
  281.8 16.0 %collective-permute-start.24 = (bf16[8,24,512]{2,1,0:T(8,128)(2,1)S(1)}, bf16[8,24,512]{2,1,0:T(8,128)(2,1)}, u32[]{:S(2)}, u32[]{:S(2)}) collective-permute-start(bf16[8,24,512]{2,1,0:T(8,128)(2,1)S(1)} %all_to_all.89), channel_id=1, source_target_pairs={{0,8},{8,0},{16,24},{24,16},{32,40},{40,32},{48,56},{56,48},{64,72... | collective-permute-start | bytes 589832 | tf_op jit(solution)/shard_map/cond/branch_0_fun/ppermute | solution.py:14
  297.9 1.4 fusion.32
  299.3 3.4 %all-to-all-start.15 = ((bf16[8,24,512]{2,1,0:T(8,128)(2,1)}), bf16[8,24,512]{2,1,0:T(8,128)(2,1)S(1)}, u32[]{:S(2)}, u32[]{:S(2)}) async-start(bf16[8,24,512]{2,1,0:T(8,128)(2,1)} %fusion.32), calls=%async_computation.15 | async-start | bytes 393216 | tf_op jit(solution)/shard_map/cond/branch_0_fun/all_to_all | solution.py:20
  302.7 0.7 compare_select_fusion.1
  303.5 1.9 fusion.31
  305.4 0.5 copy.15
  306.0 14.9 %collective-permute-start.23 = (bf16[8,24,896]{2,1,0:T(8,128)(2,1)S(1)}, bf16[8,24,896]{2,1,0:T(8,128)(2,1)S(1)}, u32[]{:S(2)}, u32[]{:S(2)}) collective-permute-start(bf16[8,24,896]{2,1,0:T(8,128)(2,1)S(1)} %get-tuple-element.171), channel_id=1, source_target_pairs={{0,8},{8,0},{16,24},{24,16},{32,40},{40,32},{48,56},{56,48},{64,72... | collective-permute-start | bytes 1032200 | tf_op jit(solution)/shard_map/cond/branch_0_fun/ppermute | solution.py:14
  321.0 1.2 collective-permute-done.23
  322.2 0.7 fusion.30
  322.8 0.6 copy.14
  323.7 0.7 reshape.82
  324.4 0.2 copy-done.10
  324.6 0.3 copy-done.11
  (76 shorter events, 1.6 us)
Async XLA Ops:
  0.6 17.1 %copy-start.5 = (bf16[1,896,512]{2,1,0:T(8,128)(2,1)S(1)}, bf16[1,896,512]{2,1,0:T(8,128)(2,1)}, u32[]{:S(2)}) copy-start(bf16[1,896,512]{2,1,0:T(8,128)(2,1)} %param.23) | copy-start | bytes 2752516
  0.6 31.2 %collective-permute-start.26 = (bf16[512,896]{1,0:T(8,128)(2,1)}, bf16[512,896]{1,0:T(8,128)(2,1)S(1)}, u32[]{:S(2)}, u32[]{:S(2)}) collective-permute-start(bf16[512,896]{1,0:T(8,128)(2,1)} %bitcast.55), channel_id=1, source_target_pairs={{0,8},{8,0},{16,24},{24,16},{32,40},{40,32},{48,56},{56,48},{64,72... | collective-permute-start | bytes 2752520 | tf_op jit(solution)/shard_map/ppermute | solution.py:14
  13.8 18.1 %all-to-all-start.16 = ((bf16[8,48,512]{2,1,0:T(8,128)(2,1)}), bf16[8,48,512]{2,1,0:T(8,128)(2,1)S(1)}, u32[]{:S(2)}, u32[]{:S(2)}) async-start(bf16[8,48,512]{2,1,0:T(8,128)(2,1)} %broadcast_in_dim.311), calls=%async_computation.16 | async-start | bytes 786432 | tf_op jit(solution)/shard_map/all_to_all | solution.py:20
  17.7 16.4 %collective-permute-start.27 = (bf16[896,512]{1,0:T(8,128)(2,1)S(1)}, bf16[896,512]{1,0:T(8,128)(2,1)S(1)}, u32[]{:S(2)}, u32[]{:S(2)}) collective-permute-start(bf16[896,512]{1,0:T(8,128)(2,1)S(1)} %bitcast.221), channel_id=1, source_target_pairs={{0,8},{8,0},{16,24},{24,16},{32,40},{40,32},{48,56},{56,48},{64,72... | collective-permute-start | bytes 2752520 | tf_op jit(solution)/shard_map/ppermute | solution.py:14
  31.9 2.2 copy-start.3
  31.9 2.2 copy-start.7
  34.1 0.9 copy-start.8
  36.2 46.2 %all-to-all-start.17 = ((bf16[8,48,1792]{2,1,0:T(8,128)(2,1)}), bf16[8,48,1792]{2,1,0:T(8,128)(2,1)S(1)}, u32[]{:S(2)}, u32[]{:S(2)}) async-start(bf16[8,48,1792]{2,1,0:T(8,128)(2,1)} %pad_maximum_fusion.15), calls=%async_computation.17 | async-start | bytes 2752512 | tf_op jit(solution)/shard_map/all_to_all | solution.py:59
  46.2 2.3 collective-permute-start.25
  46.9 51.7 %collective-permute-start.28 = (bf16[512,896]{1,0:T(8,128)(2,1)}, bf16[512,896]{1,0:T(8,128)(2,1)}, u32[]{:S(2)}, u32[]{:S(2)}) collective-permute-start(bf16[512,896]{1,0:T(8,128)(2,1)} %bitcast.55), channel_id=1, source_target_pairs={{128,144},{136,152},{144,128},{152,136},{160,176},{168,184},{176,1... | collective-permute-start | bytes 2752520 | tf_op jit(solution)/shard_map/ppermute | solution.py:45
  48.7 1.2 copy-start
  82.7 10.0 %copy-start.6 = (bf16[1,896,512]{2,1,0:T(8,128)(2,1)S(1)}, bf16[1,896,512]{2,1,0:T(8,128)(2,1)}, u32[]{:S(2)}) copy-start(bf16[1,896,512]{2,1,0:T(8,128)(2,1)} %param.23) | copy-start | bytes 2752516
  82.8 1.5 collective-permute-start
  85.9 12.8 %all-to-all-start.18 = ((bf16[8,24,512]{2,1,0:T(8,128)(2,1)}), bf16[8,24,512]{2,1,0:T(8,128)(2,1)S(1)}, u32[]{:S(2)}, u32[]{:S(2)}) async-start(bf16[8,24,512]{2,1,0:T(8,128)(2,1)} %broadcast_in_dim.312), calls=%async_computation.18 | async-start | bytes 393216 | tf_op jit(solution)/shard_map/all_to_all | solution.py:38
  100.3 34.5 %all-to-all-start.19 = ((bf16[8,24,512]{2,1,0:T(8,128)(2,1)}), bf16[8,24,512]{2,1,0:T(8,128)(2,1)S(1)}, u32[]{:S(2)}, u32[]{:S(2)}) async-start(bf16[8,24,512]{2,1,0:T(8,128)(2,1)} %broadcast_in_dim.313), calls=%async_computation.19 | async-start | bytes 393216 | tf_op jit(solution)/shard_map/all_to_all | solution.py:38
  134.8 2.3 copy-start.4
  135.8 106.5 %collective-permute-start.29 = (bf16[24,512]{1,0:T(8,128)(2,1)S(1)}, bf16[24,512]{1,0:T(8,128)(2,1)S(1)}, u32[]{:S(2)}, u32[]{:S(2)}) collective-permute-start(bf16[24,512]{1,0:T(8,128)(2,1)S(1)} %get-tuple-element.153), channel_id=1, source_target_pairs={{128,0},{129,1},{130,2},{131,3},{132,4},{133,5},{134,6},{135,7},{1... | collective-permute-start | bytes 73736 | tf_op jit(solution)/shard_map/ppermute | solution.py:235
  154.7 18.2 %collective-permute-start.3 = (bf16[8,24,896]{2,1,0:T(8,128)(2,1)S(1)}, bf16[8,24,896]{2,1,0:T(8,128)(2,1)S(1)}, u32[]{:S(2)}, u32[]{:S(2)}) collective-permute-start(bf16[8,24,896]{2,1,0:T(8,128)(2,1)S(1)} %get-tuple-element.169), channel_id=1, source_target_pairs={{0,8},{8,0},{16,24},{24,16},{32,40},{40,32},{48,56},{56,48},{64,72... | collective-permute-start | bytes 1032200 | tf_op jit(solution)/shard_map/cond/branch_1_fun/ppermute | solution.py:14
  169.5 3.3 %collective-permute-start.2 = (bf16[8,24,512]{2,1,0:T(8,128)(2,1)S(1)}, bf16[8,24,512]{2,1,0:T(8,128)(2,1)S(1)}, u32[]{:S(2)}, u32[]{:S(2)}) collective-permute-start(bf16[8,24,512]{2,1,0:T(8,128)(2,1)S(1)} %get-tuple-element.110), channel_id=1, source_target_pairs={{0,8},{8,0},{16,24},{24,16},{32,40},{40,32},{48,56},{56,48},{64,72... | collective-permute-start | bytes 589832 | tf_op jit(solution)/shard_map/cond/branch_1_fun/ppermute | solution.py:14
  242.3 12.1 %copy-start.12 = (bf16[16,24,896]{2,1,0:T(8,128)(2,1)}, bf16[16,24,896]{2,1,0:T(8,128)(2,1)S(1)}, u32[]{:S(2)}) copy-start(bf16[16,24,896]{2,1,0:T(8,128)(2,1)S(1)} %get-tuple-element.117) | copy-start | bytes 2064388 | tf_op jit(solution)/shard_map/cond
  278.2 19.6 %all-to-all-start.14 = ((bf16[8,24,1792]{2,1,0:T(8,128)(2,1)}), bf16[8,24,1792]{2,1,0:T(8,128)(2,1)S(1)}, u32[]{:S(2)}, u32[]{:S(2)}) async-start(bf16[8,24,1792]{2,1,0:T(8,128)(2,1)} %broadcast_in_dim.197), calls=%async_computation.14 | async-start | bytes 1376256 | tf_op jit(solution)/shard_map/cond/branch_0_fun/all_to_all | solution.py:59
  281.8 21.6 %collective-permute-start.24 = (bf16[8,24,512]{2,1,0:T(8,128)(2,1)S(1)}, bf16[8,24,512]{2,1,0:T(8,128)(2,1)}, u32[]{:S(2)}, u32[]{:S(2)}) collective-permute-start(bf16[8,24,512]{2,1,0:T(8,128)(2,1)S(1)} %all_to_all.89), channel_id=1, source_target_pairs={{0,8},{8,0},{16,24},{24,16},{32,40},{40,32},{48,56},{56,48},{64,72... | collective-permute-start | bytes 589832 | tf_op jit(solution)/shard_map/cond/branch_0_fun/ppermute | solution.py:14
  299.3 21.6 %all-to-all-start.15 = ((bf16[8,24,512]{2,1,0:T(8,128)(2,1)}), bf16[8,24,512]{2,1,0:T(8,128)(2,1)S(1)}, u32[]{:S(2)}, u32[]{:S(2)}) async-start(bf16[8,24,512]{2,1,0:T(8,128)(2,1)} %fusion.32), calls=%async_computation.15 | async-start | bytes 393216 | tf_op jit(solution)/shard_map/cond/branch_0_fun/all_to_all | solution.py:20
  306.0 16.2 %collective-permute-start.23 = (bf16[8,24,896]{2,1,0:T(8,128)(2,1)S(1)}, bf16[8,24,896]{2,1,0:T(8,128)(2,1)S(1)}, u32[]{:S(2)}, u32[]{:S(2)}) collective-permute-start(bf16[8,24,896]{2,1,0:T(8,128)(2,1)S(1)} %get-tuple-element.171), channel_id=1, source_target_pairs={{0,8},{8,0},{16,24},{24,16},{32,40},{40,32},{48,56},{56,48},{64,72... | collective-permute-start | bytes 1032200 | tf_op jit(solution)/shard_map/cond/branch_0_fun/ppermute | solution.py:14
  323.7 0.9 copy-start.10
  323.7 1.2 copy-start.11

commit v7 on v6

--- a/solution.py
+++ b/solution.py
@@ -37,6 +37,11 @@
     ]
     x = lax.all_to_all(copies(x, 2 * few), ("pipe", "dp"), 0, 0, axis_index_groups=groups, tiled=True)
     return x[few:]
+
+
+def row_sums_from_above(x, at):
+    got = rows_from_above(x.reshape((-1,) + x.shape[2:]), at)
+    return add_blocks(got).astype(BF16).reshape(x.shape)
 
 
 def swap_middle(x, mate):
@@ -169,13 +174,17 @@
         return out, full_back, full_d_up, part
 
     def middle_tick(at, row_back):
+        row = lax.axis_index("dp") // 4
         up_mate = jnp.concatenate([up_other, swap_in_group(up_other, at, 1)], axis=1)
-        arriving = lax.dynamic_index_in_dim(row_back, lax.axis_index("dp") // 4, 0, keepdims=False)
+        arriving = lax.dynamic_index_in_dim(row_back, row, 0, keepdims=False)
         part = jnp.concatenate([by_cols(row_back, down_w), by_cols(row_back, down_mate)], axis=0)
         back = add_blocks(features_exchange(part))
         d_up = (back * middle_slope).astype(BF16)
         row_d_up = features_exchange(copies(d_up, parts))
         part = cols_product(row_d_up[:few], up_w) + cols_product(row_d_up[few:], up_mate)
+        if at == last - 1:
+            mine = jnp.arange(few)[:, None, None] == row
+            return (part + jnp.where(mine, row_back.astype(F32), 0.0)).astype(BF16), row_d_up
         mixed = add_blocks(row_exchange(part.astype(BF16)))
         return (arriving.astype(F32) + mixed).astype(BF16), row_d_up
 
@@ -211,19 +220,25 @@
     out, full_d_up, middle_slope = lax.cond(segment == last, first_tick, skip_first)
     outs, kept_back, kept_d_up = [out], [], []
     for at in range(last - 1, 0, -1):
-        row_back = rows_from_above(out, at)
+        if at == last - 1:
+            row_back = rows_from_above(out, at)
+            shape = row_back.shape
+        else:
+            row_back = row_sums_from_above(out, at)
+            outs.append(lax.dynamic_index_in_dim(row_back, lax.axis_index("dp") // 4, 0, keepdims=False))
+            shape = (block, width)
         out, row_d_up = lax.cond(
             segment == at,
             functools.partial(middle_tick, at),
-            lambda row_back: (
-                jnp.zeros((block, width), BF16),
+            lambda row_back, shape=shape: (
+                jnp.zeros(shape, BF16),
                 jnp.zeros((parts, block, 2 * units), BF16),
             ),
             row_back,
         )
-        outs.append(out)
         kept_back.append(row_back)
         kept_d_up.append(row_d_up)
+    outs.append(out)
     all_in, all_hidden = lax.cond(
         segment == 0,
         lambda: (both_cores(full_in), own_hidden()),

time: 328 us -> 322 us (0.982)
  waiting for transfers between devices: 126 us -> 118 us
    ppermute x1, waiting for transfers between devices: 69.3 us -> 58.8 us  [body(): received = lax.ppermute(out, 'pipe', [(1, 0)])]
where the time goes in v7:
time: 322 us; the launch traced here: 319 us
  starting transfers between devices  119 us (37%)
  waiting for transfers between devices  118 us (37%)
  blocking collectives  49 us (15%)
  local copies, waits for them, and re-layouts  14.2 us (4%)
  matrix products  10.2 us (3%)
  other arithmetic  7.42 us (2%)
    ppermute x6, starting transfers between devices, swap_cores(): return lax.ppermute(x, 'dp', [(i, i ^ 1) for i in range(peers)])  60.3 us
    ppermute x1, waiting for transfers between devices, body(): received = lax.ppermute(out, 'pipe', [(1, 0)])  58.8 us
    all_to_all x2, blocking collectives, features_exchange(): return lax.all_to_all(x, 'tensor', 0, 0, tiled=True)  36.9 us
    all_to_all x2, starting transfers between devices, rows_from_above(): lax.all_to_all(copies(x, 2 * few), ('pipe', 'dp'), 0, 0, axis_index_group...  33.8 us
    all_to_all x2, waiting for transfers between devices, features_exchange(): return lax.all_to_all(x, 'tensor', 0, 0, tiled=True)  30.9 us
    all_to_all x2, starting transfers between devices, features_exchange(): return lax.all_to_all(x, 'tensor', 0, 0, tiled=True)  13.6 us
    all_to_all x2, waiting for transfers between devices, rows_from_above(): lax.all_to_all(copies(x, 2 * few), ('pipe', 'dp'), 0, 0, axis_index_group...  13.3 us
    all_to_all x1, blocking collectives, chips_exchange(): return lax.all_to_all(x, 'dp', 0, 0, axis_index_groups=groups, tiled=True)  12.1 us
  transfers between devices with their start and end apart: 16, of which 7 were waited for; matrix products, arithmetic and copies ran while one was open for 6% of the time, Pallas kernels for 0%

profile of v7, /device:TPU:1, one launch (start us, length us, event | category | flops | bytes accessed | tf_op | source)
XLA Modules:
  0.0 319.3 jit_solution(12840397024175011923)
XLA Ops:
  0.6 8.9 %collective-permute-start.26 = (bf16[512,896]{1,0:T(8,128)(2,1)}, bf16[512,896]{1,0:T(8,128)(2,1)S(1)}, u32[]{:S(2)}, u32[]{:S(2)}) collective-permute-start(bf16[512,896]{1,0:T(8,128)(2,1)} %bitcast.55), channel_id=1, source_target_pairs={{0,8},{8,0},{16,24},{24,16},{32,40},{40,32},{48,56},{56,48},{64,72... | collective-permute-start | bytes 2752520 | tf_op jit(solution)/shard_map/ppermute | solution.py:14
  9.6 0.7 broadcast_compare_fusion.7
  11.0 0.8 reshape.87
  11.8 0.8 copy.45
  12.9 0.1 select_select_fusion
  13.0 0.8 broadcast_in_dim.325
  13.8 3.9 %all-to-all-start.15 = ((bf16[8,48,512]{2,1,0:T(8,128)(2,1)}), bf16[8,48,512]{2,1,0:T(8,128)(2,1)S(1)}, u32[]{:S(2)}, u32[]{:S(2)}) async-start(bf16[8,48,512]{2,1,0:T(8,128)(2,1)} %broadcast_in_dim.325), calls=%async_computation.15 | async-start | bytes 786432 | tf_op jit(solution)/shard_map/all_to_all | solution.py:20
  17.7 2.2 collective-permute-start.27
  19.9 11.9 %all-to-all-done.15 = bf16[8,48,512]{2,1,0:T(8,128)(2,1)S(1)} async-done(((bf16[8,48,512]{2,1,0:T(8,128)(2,1)}), bf16[8,48,512]{2,1,0:T(8,128)(2,1)S(1)}, u32[]{:S(2)}, u32[]{:S(2)}) %all-to-all-start.15) | async-done | bytes 393248 | tf_op jit(solution)/shard_map/all_to_all | solution.py:20
  31.9 2.2 convolution_convert_fusion.6
  34.1 0.8 convolution_convert_fusion.5
  34.9 0.2 copy-done.8
  35.0 1.2 pad_maximum_fusion.15
  36.2 10.0 %all-to-all-start.16 = ((bf16[8,48,1792]{2,1,0:T(8,128)(2,1)}), bf16[8,48,1792]{2,1,0:T(8,128)(2,1)S(1)}, u32[]{:S(2)}, u32[]{:S(2)}) async-start(bf16[8,48,1792]{2,1,0:T(8,128)(2,1)} %pad_maximum_fusion.15), calls=%async_computation.16 | async-start | bytes 2752512 | tf_op jit(solution)/shard_map/all_to_all | solution.py:64
  46.2 0.7 collective-permute-start.25
  47.0 1.6 collective-permute-start.28
  48.6 0.1 conditional.6
  48.6 0.1 broadcast.102
  48.7 1.2 copy-done
  50.0 1.6 pad_maximum_fusion.13
  51.5 30.9 %all-to-all-done.16 = bf16[8,48,1792]{2,1,0:T(8,128)(2,1)S(1)} async-done(((bf16[8,48,1792]{2,1,0:T(8,128)(2,1)}), bf16[8,48,1792]{2,1,0:T(8,128)(2,1)S(1)}, u32[]{:S(2)}, u32[]{:S(2)}) %all-to-all-start.16) | async-done | bytes 1376288 | tf_op jit(solution)/shard_map/all_to_all | solution.py:64
  82.5 0.2 convert_reduce_fusion.6
  82.7 2.5 conditional.7
  82.8 0.8 collective-permute-start
  83.6 0.7 slice.104
  84.3 0.9 broadcast.103
  85.2 0.7 broadcast_in_dim.326
  85.9 6.8 %all-to-all-start.17 = ((bf16[8,24,512]{2,1,0:T(8,128)(2,1)}), bf16[8,24,512]{2,1,0:T(8,128)(2,1)S(1)}, u32[]{:S(2)}, u32[]{:S(2)}) async-start(bf16[8,24,512]{2,1,0:T(8,128)(2,1)} %broadcast_in_dim.326), calls=%async_computation.17 | async-start | bytes 393216 | tf_op jit(solution)/shard_map/all_to_all | solution.py:38
  92.8 2.5 pad_maximum_fusion.14
  95.3 3.4 %all-to-all-done.17 = bf16[8,24,512]{2,1,0:T(8,128)(2,1)S(1)} async-done(((bf16[8,24,512]{2,1,0:T(8,128)(2,1)}), bf16[8,24,512]{2,1,0:T(8,128)(2,1)S(1)}, u32[]{:S(2)}, u32[]{:S(2)}) %all-to-all-start.17) | async-done | bytes 196640 | tf_op jit(solution)/shard_map/all_to_all | solution.py:38
  98.7 0.9 conditional.8
  98.7 0.9 broadcast.106
  99.6 0.9 broadcast_in_dim.328
  100.6 26.9 %all-to-all-start.18 = ((bf16[8,96,512]{2,1,0:T(8,128)(2,1)}), bf16[8,96,512]{2,1,0:T(8,128)(2,1)S(1)}, u32[]{:S(2)}, u32[]{:S(2)}) async-start(bf16[8,96,512]{2,1,0:T(8,128)(2,1)} %broadcast_in_dim.328), calls=%async_computation.18 | async-start | bytes 1572864 | tf_op jit(solution)/shard_map/all_to_all | solution.py:38
  127.5 10.0 %all-to-all-done.18 = bf16[8,96,512]{2,1,0:T(8,128)(2,1)S(1)} async-done(((bf16[8,96,512]{2,1,0:T(8,128)(2,1)}), bf16[8,96,512]{2,1,0:T(8,128)(2,1)S(1)}, u32[]{:S(2)}, u32[]{:S(2)}) %all-to-all-start.18) | async-done | bytes 786464 | tf_op jit(solution)/shard_map/all_to_all | solution.py:38
  137.6 1.0 conditional.9
  137.6 1.0 broadcast.108
  138.6 1.3 collective-permute-start.29
  139.9 0.7 fusion.115
  140.6 36.9 %conditional.10 = (bf16[16,24,512]{2,1,0:T(8,128)(2,1)S(1)}, bf16[16,24,896]{2,1,0:T(8,128)(2,1)S(1)}) conditional(s32[]{:T(128)} %convert_element_type.156, () %tuple.77, (bf16[8,24,512]{2,1,0:T(8,128)(2,1)S(1)}, bf16[24,1792]{1,0:T(8,128)(2,1)S(1)}) %tuple.78), branch_computations={%region_14.15_spmd, %region_15.16_spmd} | conditional | flops 540672 | bytes 7852128 | solution.py:242
  140.6 16.7 %all_to_all.84 = bf16[8,24,1792]{2,1,0:T(8,128)(2,1)S(1)} all-to-all(bf16[8,24,1792]{2,1,0:T(8,128)(2,1)S(1)} %broadcast_in_dim.208), channel_id=1, replica_groups=mesh['pipe'=4,'dp'=16,'tensor'=8] {'tensor'}, dimensions={0} | all-to-all | bytes 1376256 | tf_op jit(solution)/shard_map/cond/branch_1_fun/all_to_all | solution.py:64
  157.4 16.6 %collective-permute-start.3 = (bf16[8,24,896]{2,1,0:T(8,128)(2,1)S(1)}, bf16[8,24,896]{2,1,0:T(8,128)(2,1)S(1)}, u32[]{:S(2)}, u32[]{:S(2)}) collective-permute-start(bf16[8,24,896]{2,1,0:T(8,128)(2,1)S(1)} %get-tuple-element.210), channel_id=1, source_target_pairs={{0,8},{8,0},{16,24},{24,16},{32,40},{40,32},{48,56},{56,48},{64,72... | collective-permute-start | bytes 1032200 | tf_op jit(solution)/shard_map/cond/branch_1_fun/ppermute | solution.py:14
  174.0 1.9 collective-permute-start.2
  175.9 1.4 collective-permute-done.2
  177.5 58.8 %collective-permute-done.29 = bf16[24,512]{1,0:T(8,128)(2,1)S(1)} collective-permute-done((bf16[24,512]{1,0:T(8,128)(2,1)S(1)}, bf16[24,512]{1,0:T(8,128)(2,1)S(1)}, u32[]{:S(2)}, u32[]{:S(2)}) %collective-permute-start.29) | collective-permute-done | bytes 24608 | tf_op jit(solution)/shard_map/ppermute | solution.py:250
  236.3 81.7 %conditional.11 = (bf16[24,512]{1,0:T(8,128)(2,1)S(1)}, bf16[1,512,896]{2,1,0:T(8,128)(2,1)S(1)}, bf16[1,896,512]{2,1,0:T(8,128)(2,1)S(1)}) conditional(s32[]{:T(128)} %clamp.3, (bf16[24,512]{1,0:T(8,128)(2,1)S(1)}, bf16[1792,512]{1,0:T(8,128)(2,1)}, f32[24,1792]{1,0:T(8,128)S(1)}, bf16[512,1792]{1,0:T(8,128)(2,1)S(1)}, ...), branch_computations={%region_16.19_spmd, %region_19.20_spmd, %region_20.21_spmd, %regio... | conditional | flops 1412360192 | bytes 28442848 | solution.py:265
  236.3 12.1 %all_to_all.85 = bf16[8,24,512]{2,1,0:T(8,128)(2,1)S(1)} all-to-all(bf16[8,24,512]{2,1,0:T(8,128)(2,1)S(1)} %broadcast_in_dim.209), channel_id=1, replica_groups={{0,16,32,48,64,80,96,112},{8,24,40,56,72,88,104,120},{1,17,33,49,65,81,..., dimensions={0} | all-to-all | bytes 393216 | tf_op jit(solution)/shard_map/cond/branch_0_fun/all_to_all | solution.py:20
  248.4 2.2 convolution_convert_fusion.4
  250.7 20.2 %all_to_all.86 = bf16[8,24,1792]{2,1,0:T(8,128)(2,1)S(1)} all-to-all(bf16[8,24,1792]{2,1,0:T(8,128)(2,1)S(1)} %convolution_convert_fusion.4), channel_id=1, replica_groups=mesh['pipe'=4,'dp'=16,'tensor'=8] {'tensor'}, dimensions={0} | all-to-all | bytes 1376256 | tf_op jit(solution)/shard_map/cond/branch_0_fun/all_to_all | solution.py:64
  271.0 0.9 broadcast_in_dim.210
  271.9 3.5 %all-to-all-start.13 = ((bf16[8,24,1792]{2,1,0:T(8,128)(2,1)}), bf16[8,24,1792]{2,1,0:T(8,128)(2,1)S(1)}, u32[]{:S(2)}, u32[]{:S(2)}) async-start(bf16[8,24,1792]{2,1,0:T(8,128)(2,1)} %broadcast_in_dim.210), calls=%async_computation.13 | async-start | bytes 1376256 | tf_op jit(solution)/shard_map/cond/branch_0_fun/all_to_all | solution.py:64
  275.5 15.7 %collective-permute-start.24 = (bf16[8,24,512]{2,1,0:T(8,128)(2,1)S(1)}, bf16[8,24,512]{2,1,0:T(8,128)(2,1)}, u32[]{:S(2)}, u32[]{:S(2)}) collective-permute-start(bf16[8,24,512]{2,1,0:T(8,128)(2,1)S(1)} %all_to_all.85), channel_id=1, source_target_pairs={{0,8},{8,0},{16,24},{24,16},{32,40},{40,32},{48,56},{56,48},{64,72... | collective-permute-start | bytes 589832 | tf_op jit(solution)/shard_map/cond/branch_0_fun/ppermute | solution.py:14
  291.2 1.4 fusion.32
  292.7 3.4 %all-to-all-start.14 = ((bf16[8,24,512]{2,1,0:T(8,128)(2,1)}), bf16[8,24,512]{2,1,0:T(8,128)(2,1)S(1)}, u32[]{:S(2)}, u32[]{:S(2)}) async-start(bf16[8,24,512]{2,1,0:T(8,128)(2,1)} %fusion.32), calls=%async_computation.14 | async-start | bytes 393216 | tf_op jit(solution)/shard_map/cond/branch_0_fun/all_to_all | solution.py:20
  296.1 0.7 compare_select_fusion.1
  296.8 1.9 fusion.31
  298.8 0.5 copy.26
  299.4 14.9 %collective-permute-start.23 = (bf16[8,24,896]{2,1,0:T(8,128)(2,1)S(1)}, bf16[8,24,896]{2,1,0:T(8,128)(2,1)S(1)}, u32[]{:S(2)}, u32[]{:S(2)}) collective-permute-start(bf16[8,24,896]{2,1,0:T(8,128)(2,1)S(1)} %get-tuple-element.212), channel_id=1, source_target_pairs={{0,8},{8,0},{16,24},{24,16},{32,40},{40,32},{48,56},{56,48},{64,72... | collective-permute-start | bytes 1032200 | tf_op jit(solution)/shard_map/cond/branch_0_fun/ppermute | solution.py:14
  314.3 1.2 collective-permute-done.23
  315.5 1.7 fusion.30
  317.2 0.6 copy.25
  318.0 0.7 reshape.89
  318.7 0.2 copy-done.10
  319.0 0.3 copy-done.11
  (78 shorter events, 1.6 us)
Async XLA Ops:
  0.6 17.1 %copy-start.5 = (bf16[1,896,512]{2,1,0:T(8,128)(2,1)S(1)}, bf16[1,896,512]{2,1,0:T(8,128)(2,1)}, u32[]{:S(2)}) copy-start(bf16[1,896,512]{2,1,0:T(8,128)(2,1)} %param.23) | copy-start | bytes 2752516
  0.6 31.2 %collective-permute-start.26 = (bf16[512,896]{1,0:T(8,128)(2,1)}, bf16[512,896]{1,0:T(8,128)(2,1)S(1)}, u32[]{:S(2)}, u32[]{:S(2)}) collective-permute-start(bf16[512,896]{1,0:T(8,128)(2,1)} %bitcast.55), channel_id=1, source_target_pairs={{0,8},{8,0},{16,24},{24,16},{32,40},{40,32},{48,56},{56,48},{64,72... | collective-permute-start | bytes 2752520 | tf_op jit(solution)/shard_map/ppermute | solution.py:14
  13.8 18.1 %all-to-all-start.15 = ((bf16[8,48,512]{2,1,0:T(8,128)(2,1)}), bf16[8,48,512]{2,1,0:T(8,128)(2,1)S(1)}, u32[]{:S(2)}, u32[]{:S(2)}) async-start(bf16[8,48,512]{2,1,0:T(8,128)(2,1)} %broadcast_in_dim.325), calls=%async_computation.15 | async-start | bytes 786432 | tf_op jit(solution)/shard_map/all_to_all | solution.py:20
  17.7 16.4 %collective-permute-start.27 = (bf16[896,512]{1,0:T(8,128)(2,1)S(1)}, bf16[896,512]{1,0:T(8,128)(2,1)S(1)}, u32[]{:S(2)}, u32[]{:S(2)}) collective-permute-start(bf16[896,512]{1,0:T(8,128)(2,1)S(1)} %bitcast.227), channel_id=1, source_target_pairs={{0,8},{8,0},{16,24},{24,16},{32,40},{40,32},{48,56},{56,48},{64,72... | collective-permute-start | bytes 2752520 | tf_op jit(solution)/shard_map/ppermute | solution.py:14
  31.9 2.2 copy-start.3
  31.9 2.2 copy-start.7
  34.1 0.9 copy-start.8
  36.2 46.2 %all-to-all-start.16 = ((bf16[8,48,1792]{2,1,0:T(8,128)(2,1)}), bf16[8,48,1792]{2,1,0:T(8,128)(2,1)S(1)}, u32[]{:S(2)}, u32[]{:S(2)}) async-start(bf16[8,48,1792]{2,1,0:T(8,128)(2,1)} %pad_maximum_fusion.15), calls=%async_computation.16 | async-start | bytes 2752512 | tf_op jit(solution)/shard_map/all_to_all | solution.py:64
  46.2 2.3 collective-permute-start.25
  47.0 51.7 %collective-permute-start.28 = (bf16[512,896]{1,0:T(8,128)(2,1)}, bf16[512,896]{1,0:T(8,128)(2,1)}, u32[]{:S(2)}, u32[]{:S(2)}) collective-permute-start(bf16[512,896]{1,0:T(8,128)(2,1)} %bitcast.55), channel_id=1, source_target_pairs={{128,144},{136,152},{144,128},{152,136},{160,176},{168,184},{176,1... | collective-permute-start | bytes 2752520 | tf_op jit(solution)/shard_map/ppermute | solution.py:50
  48.7 1.2 copy-start
  82.7 10.0 %copy-start.6 = (bf16[1,896,512]{2,1,0:T(8,128)(2,1)S(1)}, bf16[1,896,512]{2,1,0:T(8,128)(2,1)}, u32[]{:S(2)}) copy-start(bf16[1,896,512]{2,1,0:T(8,128)(2,1)} %param.23) | copy-start | bytes 2752516
  82.8 1.5 collective-permute-start
  85.9 12.8 %all-to-all-start.17 = ((bf16[8,24,512]{2,1,0:T(8,128)(2,1)}), bf16[8,24,512]{2,1,0:T(8,128)(2,1)S(1)}, u32[]{:S(2)}, u32[]{:S(2)}) async-start(bf16[8,24,512]{2,1,0:T(8,128)(2,1)} %broadcast_in_dim.326), calls=%async_computation.17 | async-start | bytes 393216 | tf_op jit(solution)/shard_map/all_to_all | solution.py:38
  100.6 36.9 %all-to-all-start.18 = ((bf16[8,96,512]{2,1,0:T(8,128)(2,1)}), bf16[8,96,512]{2,1,0:T(8,128)(2,1)S(1)}, u32[]{:S(2)}, u32[]{:S(2)}) async-start(bf16[8,96,512]{2,1,0:T(8,128)(2,1)} %broadcast_in_dim.328), calls=%async_computation.18 | async-start | bytes 1572864 | tf_op jit(solution)/shard_map/all_to_all | solution.py:38
  137.6 2.3 copy-start.4
  138.6 97.7 %collective-permute-start.29 = (bf16[24,512]{1,0:T(8,128)(2,1)S(1)}, bf16[24,512]{1,0:T(8,128)(2,1)S(1)}, u32[]{:S(2)}, u32[]{:S(2)}) collective-permute-start(bf16[24,512]{1,0:T(8,128)(2,1)S(1)} %get-tuple-element.191), channel_id=1, source_target_pairs={{128,0},{129,1},{130,2},{131,3},{132,4},{133,5},{134,6},{135,7},{1... | collective-permute-start | bytes 73736 | tf_op jit(solution)/shard_map/ppermute | solution.py:250
  157.4 20.0 %collective-permute-start.3 = (bf16[8,24,896]{2,1,0:T(8,128)(2,1)S(1)}, bf16[8,24,896]{2,1,0:T(8,128)(2,1)S(1)}, u32[]{:S(2)}, u32[]{:S(2)}) collective-permute-start(bf16[8,24,896]{2,1,0:T(8,128)(2,1)S(1)} %get-tuple-element.210), channel_id=1, source_target_pairs={{0,8},{8,0},{16,24},{24,16},{32,40},{40,32},{48,56},{56,48},{64,72... | collective-permute-start | bytes 1032200 | tf_op jit(solution)/shard_map/cond/branch_1_fun/ppermute | solution.py:14
  174.0 3.3 %collective-permute-start.2 = (bf16[8,24,512]{2,1,0:T(8,128)(2,1)S(1)}, bf16[8,24,512]{2,1,0:T(8,128)(2,1)S(1)}, u32[]{:S(2)}, u32[]{:S(2)}) collective-permute-start(bf16[8,24,512]{2,1,0:T(8,128)(2,1)S(1)} %get-tuple-element.145), channel_id=1, source_target_pairs={{0,8},{8,0},{16,24},{24,16},{32,40},{40,32},{48,56},{56,48},{64,72... | collective-permute-start | bytes 589832 | tf_op jit(solution)/shard_map/cond/branch_1_fun/ppermute | solution.py:14
  236.3 12.1 %copy-start.12 = (bf16[16,24,896]{2,1,0:T(8,128)(2,1)}, bf16[16,24,896]{2,1,0:T(8,128)(2,1)S(1)}, u32[]{:S(2)}) copy-start(bf16[16,24,896]{2,1,0:T(8,128)(2,1)S(1)} %get-tuple-element.152) | copy-start | bytes 2064388 | tf_op jit(solution)/shard_map/cond
  236.3 12.1 %copy-start.13 = (bf16[16,24,512]{2,1,0:T(8,128)(2,1)}, bf16[16,24,512]{2,1,0:T(8,128)(2,1)S(1)}, u32[]{:S(2)}) copy-start(bf16[16,24,512]{2,1,0:T(8,128)(2,1)S(1)} %get-tuple-element.151) | copy-start | bytes 1179652 | tf_op jit(solution)/shard_map/cond
  271.9 19.3 %all-to-all-start.13 = ((bf16[8,24,1792]{2,1,0:T(8,128)(2,1)}), bf16[8,24,1792]{2,1,0:T(8,128)(2,1)S(1)}, u32[]{:S(2)}, u32[]{:S(2)}) async-start(bf16[8,24,1792]{2,1,0:T(8,128)(2,1)} %broadcast_in_dim.210), calls=%async_computation.13 | async-start | bytes 1376256 | tf_op jit(solution)/shard_map/cond/branch_0_fun/all_to_all | solution.py:64
  275.5 21.3 %collective-permute-start.24 = (bf16[8,24,512]{2,1,0:T(8,128)(2,1)S(1)}, bf16[8,24,512]{2,1,0:T(8,128)(2,1)}, u32[]{:S(2)}, u32[]{:S(2)}) collective-permute-start(bf16[8,24,512]{2,1,0:T(8,128)(2,1)S(1)} %all_to_all.85), channel_id=1, source_target_pairs={{0,8},{8,0},{16,24},{24,16},{32,40},{40,32},{48,56},{56,48},{64,72... | collective-permute-start | bytes 589832 | tf_op jit(solution)/shard_map/cond/branch_0_fun/ppermute | solution.py:14
  292.7 21.6 %all-to-all-start.14 = ((bf16[8,24,512]{2,1,0:T(8,128)(2,1)}), bf16[8,24,512]{2,1,0:T(8,128)(2,1)S(1)}, u32[]{:S(2)}, u32[]{:S(2)}) async-start(bf16[8,24,512]{2,1,0:T(8,128)(2,1)} %fusion.32), calls=%async_computation.14 | async-start | bytes 393216 | tf_op jit(solution)/shard_map/cond/branch_0_fun/all_to_all | solution.py:20
  299.4 16.2 %collective-permute-start.23 = (bf16[8,24,896]{2,1,0:T(8,128)(2,1)S(1)}, bf16[8,24,896]{2,1,0:T(8,128)(2,1)S(1)}, u32[]{:S(2)}, u32[]{:S(2)}) collective-permute-start(bf16[8,24,896]{2,1,0:T(8,128)(2,1)S(1)} %get-tuple-element.212), channel_id=1, source_target_pairs={{0,8},{8,0},{16,24},{24,16},{32,40},{40,32},{48,56},{56,48},{64,72... | collective-permute-start | bytes 1032200 | tf_op jit(solution)/shard_map/cond/branch_0_fun/ppermute | solution.py:14
  318.0 0.9 copy-start.10
  318.0 1.2 copy-start.11

commit v8 on v7

--- a/solution.py
+++ b/solution.py
@@ -103,7 +103,8 @@
     up_w = jnp.concatenate([w_up[0], swap_cores(w_up[0])], axis=1)
     down_w = jnp.concatenate([w_down[0], swap_cores(w_down[0])], axis=0)
 
-    up_other = swap_middle(w_up[0], 2)
+    up_other = swap_in_group(w_up[0], last - 1, 2)
+    up_other_low = swap_in_group(w_up[0], last - 2, 2)
     down_other = swap_middle(w_down[0], 2)
 
     samples = jnp.swapaxes(pool, 0, 1)
@@ -136,6 +137,9 @@
                 moves.append(((group * peers + i) * parts + z, (group * peers + to) * parts + place))
 
 
+    def after(x, y):
+        return jnp.where(jnp.isnan(y), y, x)
+
     def second_half(arriving, back, stagger=False):
         d_up = (back * slope).astype(BF16)
         if stagger:
@@ -156,26 +160,30 @@
     def own_hidden():
         return own_units(features_exchange(copies(hidden, parts)))
 
-    def after(x, y):
-        return jnp.where(jnp.isnan(y), y, x)
-
-    def weight_products(all_in, all_hidden, all_back, full_d_up):
-        grad_up = by_rows(all_in, own_units(full_d_up)).astype(BF16)
+    def weight_products(all_in, all_hidden, all_back, all_d_up):
+        grad_up = by_rows(all_in, all_d_up).astype(BF16)
         grad_down = by_rows(all_hidden, all_back).astype(BF16)
         return grad_up, grad_down
 
     def weight_grads(all_in, all_hidden, full_back, full_d_up):
-        return weight_products(all_in, all_hidden, both_cores(full_back), full_d_up)
+        return weight_products(all_in, all_hidden, both_cores(full_back), own_units(full_d_up))
+
+    def one_step_later(x):
+        return after(x, lax.ppermute(x, ("pipe", "dp"), [(i, i ^ 4) for i in range(1, peers, 2)]))
 
     def tick(arriving):
-        full_back = chips_exchange(copies(arriving, chips))
+        sent = lax.cond(lax.axis_index("dp") % 2 == 1, one_step_later, lambda x: x, arriving)
+        full_back = chips_exchange(copies(sent, chips))
         back = add_blocks(features_exchange(by_cols(full_back, down_w)))
         out, full_d_up, part = second_half(arriving, back)
         return out, full_back, full_d_up, part
 
     def middle_tick(at, row_back):
         row = lax.axis_index("dp") // 4
-        up_mate = jnp.concatenate([up_other, swap_in_group(up_other, at, 1)], axis=1)
+        if at == last - 1:
+            up_mate = jnp.concatenate([up_other, swap_in_group(up_other, at, 1)], axis=1)
+        else:
+            up_mate = up_mate_low
         arriving = lax.dynamic_index_in_dim(row_back, row, 0, keepdims=False)
         part = jnp.concatenate([by_cols(row_back, down_w), by_cols(row_back, down_mate)], axis=0)
         back = add_blocks(features_exchange(part))
@@ -213,9 +221,15 @@
         lambda: jnp.zeros_like(down_w),
     )
 
+    up_mate_low = lax.cond(
+        segment == last - 2,
+        lambda: jnp.concatenate([up_other_low, swap_in_group(up_other_low, last - 2, 1)], axis=1),
+        lambda: jnp.zeros_like(up_w),
+    )
+
     def skip_first():
         moved = lax.ppermute(slope.astype(BF16), ("pipe", "dp", "tensor"), moves)
-        return down_mate[:block], jnp.zeros((parts, block, 2 * units), BF16), moved
+        return down_mate[:block] + up_mate_low[:block, :width], jnp.zeros((parts, block, 2 * units), BF16), moved
 
     out, full_d_up, middle_slope = lax.cond(segment == last, first_tick, skip_first)
     outs, kept_back, kept_d_up = [out], [], []
@@ -253,7 +267,11 @@
         out, full_back, full_d_up, part = tick(received)
         held = after(full_back[:1], part[:1])
         all_back = jnp.concatenate([held, full_back[1:], swap_cores(full_back)], axis=0)
-        return (out,) + weight_products(all_in, all_hidden, all_back, full_d_up)
+        other = full_d_up[..., units:]
+        first = jnp.concatenate([after(other[:1, :, :width], part[:1]), other[:1, :, width:]], axis=2)
+        other = jnp.concatenate([first, other[1:]], axis=0)
+        all_d_up = jnp.concatenate([full_d_up[..., :units], swap_cores(other)], axis=0)
+        return (out,) + weight_products(all_in, all_hidden, all_back, all_d_up)
 
     def end_middle(k):
         return lambda: (outs[k + 1],) + middle_grads(kept_back[k], kept_d_up[k])

time: 322 us -> 320 us (level)
  waiting for transfers between devices: 118 us -> 107 us
  blocking collectives: 49 us -> 58.4 us
  starting transfers between devices: 119 us -> 115 us
    all_to_all x2, blocking collectives: 36.9 us -> 46.3 us  [features_exchange(): return lax.all_to_all(x, 'tensor', 0, 0, tiled=True)]
    ppermute x6, starting transfers between devices: 60.3 us -> 51 us  [swap_cores(): return lax.ppermute(x, 'dp', [(i, i ^ 1) for i in range(peers)])]
    ppermute x1, waiting for transfers between devices: 58.8 us -> 50.6 us  [body(): received = lax.ppermute(out, 'pipe', [(1, 0)])]
    ppermute x0 -> x3, starting transfers between devices: none -> 5.45 us  [the longest x2 3.27 us: swap_in_group(): return lax.ppermute(x, ('pipe', 'dp'), pairs)]
    all_to_all x2, waiting for transfers between devices: 30.9 us -> 27 us  [features_exchange(): return lax.all_to_all(x, 'tensor', 0, 0, tiled=True)]
  transfers between devices with their start and end apart: 16 -> 18, of which waited for: 7 -> 7; matrix products, arithmetic and copies ran while one was open for 6% -> 7% of each run, Pallas kernels for 0% -> 0%
where the time goes in v8:
time: 320 us; the launch traced here: 318 us
  starting transfers between devices  115 us (36%)
  waiting for transfers between devices  107 us (33%)
  blocking collectives  58.4 us (18%)
  local copies, waits for them, and re-layouts  16 us (5%)
  other arithmetic  9.91 us (3%)
  matrix products  9.48 us (3%)
    ppermute x6, starting transfers between devices, swap_cores(): return lax.ppermute(x, 'dp', [(i, i ^ 1) for i in range(peers)])  51 us
    ppermute x1, waiting for transfers between devices, body(): received = lax.ppermute(out, 'pipe', [(1, 0)])  50.6 us
    all_to_all x2, blocking collectives, features_exchange(): return lax.all_to_all(x, 'tensor', 0, 0, tiled=True)  46.3 us
    all_to_all x2, starting transfers between devices, rows_from_above(): lax.all_to_all(copies(x, 2 * few), ('pipe', 'dp'), 0, 0, axis_index_group...  33 us
    all_to_all x2, waiting for transfers between devices, features_exchange(): return lax.all_to_all(x, 'tensor', 0, 0, tiled=True)  27 us
    all_to_all x2, waiting for transfers between devices, rows_from_above(): lax.all_to_all(copies(x, 2 * few), ('pipe', 'dp'), 0, 0, axis_index_group...  14.2 us
    all_to_all x2, starting transfers between devices, features_exchange(): return lax.all_to_all(x, 'tensor', 0, 0, tiled=True)  13.6 us
    all_to_all x1, blocking collectives, chips_exchange(): return lax.all_to_all(x, 'dp', 0, 0, axis_index_groups=groups, tiled=True)  12.1 us
  transfers between devices with their start and end apart: 18, of which 7 were waited for; matrix products, arithmetic and copies ran while one was open for 7% of the time, Pallas kernels for 0%

profile of v8, /device:TPU:1, one launch (start us, length us, event | category | flops | bytes accessed | tf_op | source)
XLA Modules:
  0.0 317.8 jit_solution(3573782828218967176)
XLA Ops:
  0.7 8.9 %collective-permute-start.28 = (bf16[512,896]{1,0:T(8,128)(2,1)}, bf16[512,896]{1,0:T(8,128)(2,1)S(1)}, u32[]{:S(2)}, u32[]{:S(2)}) collective-permute-start(bf16[512,896]{1,0:T(8,128)(2,1)} %bitcast.231), channel_id=1, source_target_pairs={{0,8},{8,0},{16,24},{24,16},{32,40},{40,32},{48,56},{56,48},{64,72... | collective-permute-start | bytes 2752520 | tf_op jit(solution)/shard_map/ppermute | solution.py:14
  9.6 0.8 copy.45
  10.7 0.7 broadcast_compare_fusion.7
  12.2 0.8 reshape.87
  13.0 0.8 broadcast_in_dim.325
  13.8 3.9 %all-to-all-start.15 = ((bf16[8,48,512]{2,1,0:T(8,128)(2,1)}), bf16[8,48,512]{2,1,0:T(8,128)(2,1)S(1)}, u32[]{:S(2)}, u32[]{:S(2)}) async-start(bf16[8,48,512]{2,1,0:T(8,128)(2,1)} %broadcast_in_dim.325), calls=%async_computation.15 | async-start | bytes 786432 | tf_op jit(solution)/shard_map/all_to_all | solution.py:20
  17.7 2.2 collective-permute-start.29
  19.9 11.9 %all-to-all-done.15 = bf16[8,48,512]{2,1,0:T(8,128)(2,1)S(1)} async-done(((bf16[8,48,512]{2,1,0:T(8,128)(2,1)}), bf16[8,48,512]{2,1,0:T(8,128)(2,1)S(1)}, u32[]{:S(2)}, u32[]{:S(2)}) %all-to-all-start.15) | async-done | bytes 393248 | tf_op jit(solution)/shard_map/all_to_all | solution.py:20
  31.9 0.5 convolution_convert_fusion.6
  32.9 1.9 convolution_convert_fusion.5
  34.9 1.2 pad_maximum_fusion.17
  36.1 10.0 %all-to-all-start.16 = ((bf16[8,48,1792]{2,1,0:T(8,128)(2,1)}), bf16[8,48,1792]{2,1,0:T(8,128)(2,1)S(1)}, u32[]{:S(2)}, u32[]{:S(2)}) async-start(bf16[8,48,1792]{2,1,0:T(8,128)(2,1)} %pad_maximum_fusion.17), calls=%async_computation.16 | async-start | bytes 2752512 | tf_op jit(solution)/shard_map/all_to_all | solution.py:64
  46.1 1.6 collective-permute-start.26
  47.7 1.7 collective-permute-start.27
  49.4 1.6 collective-permute-start.30
  51.1 1.2 copy-done.2
  52.3 1.4 conditional.9
  52.3 1.4 broadcast.106
  53.8 1.6 pad_maximum_fusion.15
  55.4 27.0 %all-to-all-done.16 = bf16[8,48,1792]{2,1,0:T(8,128)(2,1)S(1)} async-done(((bf16[8,48,1792]{2,1,0:T(8,128)(2,1)}), bf16[8,48,1792]{2,1,0:T(8,128)(2,1)S(1)}, u32[]{:S(2)}, u32[]{:S(2)}) %all-to-all-start.16) | async-done | bytes 1376288 | tf_op jit(solution)/shard_map/all_to_all | solution.py:64
  82.6 2.5 conditional.10
  82.6 0.8 collective-permute-start.2
  83.4 0.8 slice_add_fusion
  84.2 0.9 broadcast.107
  85.1 0.7 broadcast_in_dim.326
  85.8 25.4 %all-to-all-start.17 = ((bf16[8,24,512]{2,1,0:T(8,128)(2,1)}), bf16[8,24,512]{2,1,0:T(8,128)(2,1)S(1)}, u32[]{:S(2)}, u32[]{:S(2)}) async-start(bf16[8,24,512]{2,1,0:T(8,128)(2,1)} %broadcast_in_dim.326), calls=%async_computation.17 | async-start | bytes 393216 | tf_op jit(solution)/shard_map/all_to_all | solution.py:38
  111.2 2.5 pad_maximum_fusion.16
  113.7 4.2 %all-to-all-done.17 = bf16[8,24,512]{2,1,0:T(8,128)(2,1)S(1)} async-done(((bf16[8,24,512]{2,1,0:T(8,128)(2,1)}), bf16[8,24,512]{2,1,0:T(8,128)(2,1)S(1)}, u32[]{:S(2)}, u32[]{:S(2)}) %all-to-all-start.17) | async-done | bytes 196640 | tf_op jit(solution)/shard_map/all_to_all | solution.py:38
  117.9 1.0 conditional.11
  117.9 1.0 broadcast.110
  118.9 0.9 broadcast_in_dim.328
  119.9 7.7 %all-to-all-start.18 = ((bf16[8,96,512]{2,1,0:T(8,128)(2,1)}), bf16[8,96,512]{2,1,0:T(8,128)(2,1)S(1)}, u32[]{:S(2)}, u32[]{:S(2)}) async-start(bf16[8,96,512]{2,1,0:T(8,128)(2,1)} %broadcast_in_dim.328), calls=%async_computation.18 | async-start | bytes 1572864 | tf_op jit(solution)/shard_map/all_to_all | solution.py:38
  127.5 10.0 %all-to-all-done.18 = bf16[8,96,512]{2,1,0:T(8,128)(2,1)S(1)} async-done(((bf16[8,96,512]{2,1,0:T(8,128)(2,1)}), bf16[8,96,512]{2,1,0:T(8,128)(2,1)S(1)}, u32[]{:S(2)}, u32[]{:S(2)}) %all-to-all-start.18) | async-done | bytes 786464 | tf_op jit(solution)/shard_map/all_to_all | solution.py:38
  137.6 0.9 conditional.12
  137.6 0.9 broadcast.112
  138.5 1.3 collective-permute-start.31
  139.8 0.7 fusion.116
  140.5 42.5 %conditional.13 = (bf16[16,24,512]{2,1,0:T(8,128)(2,1)S(1)}, bf16[16,24,896]{2,1,0:T(8,128)(2,1)S(1)}) conditional(s32[]{:T(128)} %convert_element_type.160, () %tuple.90, (bf16[8,24,512]{2,1,0:T(8,128)(2,1)S(1)}, bf16[24,1792]{1,0:T(8,128)(2,1)S(1)}) %tuple.91), branch_computations={%region_16.17_spmd, %region_17.18_spmd} | conditional | flops 540672 | bytes 7852128 | solution.py:256
  140.6 30.0 %all_to_all.85 = bf16[8,24,1792]{2,1,0:T(8,128)(2,1)S(1)} all-to-all(bf16[8,24,1792]{2,1,0:T(8,128)(2,1)S(1)} %broadcast_in_dim.208), channel_id=1, replica_groups=mesh['pipe'=4,'dp'=16,'tensor'=8] {'tensor'}, dimensions={0} | all-to-all | bytes 1376256 | tf_op jit(solution)/shard_map/cond/branch_1_fun/all_to_all | solution.py:64
  170.6 9.0 %collective-permute-start.5 = (bf16[8,24,896]{2,1,0:T(8,128)(2,1)S(1)}, bf16[8,24,896]{2,1,0:T(8,128)(2,1)S(1)}, u32[]{:S(2)}, u32[]{:S(2)}) collective-permute-start(bf16[8,24,896]{2,1,0:T(8,128)(2,1)S(1)} %get-tuple-element.222), channel_id=1, source_target_pairs={{0,8},{8,0},{16,24},{24,16},{32,40},{40,32},{48,56},{56,48},{64,72... | collective-permute-start | bytes 1032200 | tf_op jit(solution)/shard_map/cond/branch_1_fun/ppermute | solution.py:14
  179.6 1.9 collective-permute-start.4
  181.5 1.4 collective-permute-done.4
  183.1 50.6 %collective-permute-done.31 = bf16[24,512]{1,0:T(8,128)(2,1)S(1)} collective-permute-done((bf16[24,512]{1,0:T(8,128)(2,1)S(1)}, bf16[24,512]{1,0:T(8,128)(2,1)S(1)}, u32[]{:S(2)}, u32[]{:S(2)}) %collective-permute-start.31) | collective-permute-done | bytes 24608 | tf_op jit(solution)/shard_map/ppermute | solution.py:264
  233.7 82.9 %conditional.14 = (bf16[24,512]{1,0:T(8,128)(2,1)S(1)}, bf16[1,512,896]{2,1,0:T(8,128)(2,1)S(1)}, bf16[1,896,512]{2,1,0:T(8,128)(2,1)S(1)}) conditional(s32[]{:T(128)} %clamp.3, (bf16[24,512]{1,0:T(8,128)(2,1)S(1)}, bf16[1792,512]{1,0:T(8,128)(2,1)}, f32[24,1792]{1,0:T(8,128)S(1)}, bf16[512,1792]{1,0:T(8,128)(2,1)S(1)}, ...), branch_computations={%region_18.23_spmd, %region_23.24_spmd, %region_24.25_spmd, %regio... | conditional | flops 1413429248 | bytes 30482860 | solution.py:283
  233.7 0.8 copy-done.12
  234.5 4.6 %conditional = (bf16[24,512]{1,0:T(8,128)(2,1)S(1)}) conditional(s32[]{:T(128)} %convert_element_type.127, bf16[24,512]{1,0:T(8,128)(2,1)S(1)} %get-tuple-element.159, bf16[24,512]{1,0:T(8,128)(2,1)S(1)} %get-tuple-element.159), branch_computations={%region_19.19_spmd, %region_20.20_spmd} | conditional | flops 24576 | bytes 172080 | solution.py:175
  234.5 2.2 collective-permute-start.3
  236.7 2.4 collective-permute-done.3
  239.1 12.1 %all_to_all.86 = bf16[8,24,512]{2,1,0:T(8,128)(2,1)S(1)} all-to-all(bf16[8,24,512]{2,1,0:T(8,128)(2,1)S(1)} %broadcast_in_dim.209), channel_id=1, replica_groups={{0,16,32,48,64,80,96,112},{8,24,40,56,72,88,104,120},{1,17,33,49,65,81,..., dimensions={0} | all-to-all | bytes 393216 | tf_op jit(solution)/shard_map/cond/branch_0_fun/all_to_all | solution.py:20
  251.2 2.2 convolution_convert_fusion.4
  253.5 16.3 %all_to_all.87 = bf16[8,24,1792]{2,1,0:T(8,128)(2,1)S(1)} all-to-all(bf16[8,24,1792]{2,1,0:T(8,128)(2,1)S(1)} %convolution_convert_fusion.4), channel_id=1, replica_groups=mesh['pipe'=4,'dp'=16,'tensor'=8] {'tensor'}, dimensions={0} | all-to-all | bytes 1376256 | tf_op jit(solution)/shard_map/cond/branch_0_fun/all_to_all | solution.py:64
  269.9 0.9 broadcast_in_dim.210
  270.8 3.5 %all-to-all-start.13 = ((bf16[8,24,1792]{2,1,0:T(8,128)(2,1)}), bf16[8,24,1792]{2,1,0:T(8,128)(2,1)S(1)}, u32[]{:S(2)}, u32[]{:S(2)}) async-start(bf16[8,24,1792]{2,1,0:T(8,128)(2,1)} %broadcast_in_dim.210), calls=%async_computation.13 | async-start | bytes 1376256 | tf_op jit(solution)/shard_map/cond/branch_0_fun/all_to_all | solution.py:64
  274.3 14.3 %collective-permute-start.25 = (bf16[8,24,512]{2,1,0:T(8,128)(2,1)S(1)}, bf16[8,24,512]{2,1,0:T(8,128)(2,1)}, u32[]{:S(2)}, u32[]{:S(2)}) collective-permute-start(bf16[8,24,512]{2,1,0:T(8,128)(2,1)S(1)} %all_to_all.86), channel_id=1, source_target_pairs={{0,8},{8,0},{16,24},{24,16},{32,40},{40,32},{48,56},{56,48},{64,72... | collective-permute-start | bytes 589832 | tf_op jit(solution)/shard_map/cond/branch_0_fun/ppermute | solution.py:14
  288.6 1.5 fusion.34
  290.1 4.2 %all-to-all-start.14 = ((bf16[8,24,512]{2,1,0:T(8,128)(2,1)}), bf16[8,24,512]{2,1,0:T(8,128)(2,1)}, u32[]{:S(2)}, u32[]{:S(2)}) async-start(bf16[8,24,512]{2,1,0:T(8,128)(2,1)} %fusion.34), calls=%async_computation.14 | async-start | bytes 393216 | tf_op jit(solution)/shard_map/cond/branch_0_fun/all_to_all | solution.py:20
  294.3 0.7 compare_select_fusion.2
  295.1 0.8 pad_maximum_fusion.6
  295.8 14.7 %collective-permute-start.24 = (bf16[8,24,896]{2,1,0:T(8,128)(2,1)}, bf16[8,24,896]{2,1,0:T(8,128)(2,1)}, u32[]{:S(2)}, u32[]{:S(2)}) collective-permute-start(bf16[8,24,896]{2,1,0:T(8,128)(2,1)} %pad_maximum_fusion.6), channel_id=1, source_target_pairs={{0,8},{8,0},{16,24},{24,16},{32,40},{40,32},{48,56},{56,48},{64,72... | collective-permute-start | bytes 1032200 | tf_op jit(solution)/shard_map/cond/branch_0_fun/ppermute | solution.py:14
  310.6 1.6 fusion.33
  312.8 1.6 fusion.32
  314.5 0.6 copy.25
  315.1 1.0 convert_reduce_fusion.5
  316.6 0.7 reshape.89
  (89 shorter events, 3.7 us)
Async XLA Ops:
  0.6 31.2 %copy-start.8 = (bf16[1,512,896]{2,1,0:T(8,128)(2,1)S(1)}, bf16[1,512,896]{2,1,0:T(8,128)(2,1)}, u32[]{:S(2)}) copy-start(bf16[1,512,896]{2,1,0:T(8,128)(2,1)} %param.26) | copy-start | bytes 2752516
  0.6 17.1 %copy-start.6 = (bf16[1,896,512]{2,1,0:T(8,128)(2,1)S(1)}, bf16[1,896,512]{2,1,0:T(8,128)(2,1)}, u32[]{:S(2)}) copy-start(bf16[1,896,512]{2,1,0:T(8,128)(2,1)} %param.27) | copy-start | bytes 2752516
  0.7 31.2 %collective-permute-start.28 = (bf16[512,896]{1,0:T(8,128)(2,1)}, bf16[512,896]{1,0:T(8,128)(2,1)S(1)}, u32[]{:S(2)}, u32[]{:S(2)}) collective-permute-start(bf16[512,896]{1,0:T(8,128)(2,1)} %bitcast.231), channel_id=1, source_target_pairs={{0,8},{8,0},{16,24},{24,16},{32,40},{40,32},{48,56},{56,48},{64,72... | collective-permute-start | bytes 2752520 | tf_op jit(solution)/shard_map/ppermute | solution.py:14
  13.8 18.1 %all-to-all-start.15 = ((bf16[8,48,512]{2,1,0:T(8,128)(2,1)}), bf16[8,48,512]{2,1,0:T(8,128)(2,1)S(1)}, u32[]{:S(2)}, u32[]{:S(2)}) async-start(bf16[8,48,512]{2,1,0:T(8,128)(2,1)} %broadcast_in_dim.325), calls=%async_computation.15 | async-start | bytes 786432 | tf_op jit(solution)/shard_map/all_to_all | solution.py:20
  17.7 15.1 %collective-permute-start.29 = (bf16[896,512]{1,0:T(8,128)(2,1)S(1)}, bf16[896,512]{1,0:T(8,128)(2,1)}, u32[]{:S(2)}, u32[]{:S(2)}) collective-permute-start(bf16[896,512]{1,0:T(8,128)(2,1)S(1)} %bitcast.227), channel_id=1, source_target_pairs={{0,8},{8,0},{16,24},{24,16},{32,40},{40,32},{48,56},{56,48},{64,72... | collective-permute-start | bytes 2752520 | tf_op jit(solution)/shard_map/ppermute | solution.py:14
  31.9 1.0 copy-start.4
  31.9 1.0 copy-start.9
  36.1 46.2 %all-to-all-start.16 = ((bf16[8,48,1792]{2,1,0:T(8,128)(2,1)}), bf16[8,48,1792]{2,1,0:T(8,128)(2,1)S(1)}, u32[]{:S(2)}, u32[]{:S(2)}) async-start(bf16[8,48,1792]{2,1,0:T(8,128)(2,1)} %pad_maximum_fusion.17), calls=%async_computation.16 | async-start | bytes 2752512 | tf_op jit(solution)/shard_map/all_to_all | solution.py:64
  46.1 4.9 %collective-permute-start.26 = (bf16[896,512]{1,0:T(8,128)(2,1)S(1)}, bf16[896,512]{1,0:T(8,128)(2,1)}, u32[]{:S(2)}, u32[]{:S(2)}) collective-permute-start(bf16[896,512]{1,0:T(8,128)(2,1)S(1)} %bitcast.229), channel_id=1, source_target_pairs={{128,144},{136,152},{144,128},{152,136},{160,176},{168,184},{176,1... | collective-permute-start | bytes 2752520 | tf_op jit(solution)/shard_map/ppermute | solution.py:50
  47.7 3.4 %collective-permute-start.27 = (bf16[512,896]{1,0:T(8,128)(2,1)}, bf16[512,896]{1,0:T(8,128)(2,1)}, u32[]{:S(2)}, u32[]{:S(2)}) collective-permute-start(bf16[512,896]{1,0:T(8,128)(2,1)} %bitcast.232), channel_id=1, source_target_pairs={{128,144},{136,152},{144,128},{152,136},{160,176},{168,184},{176,1... | collective-permute-start | bytes 2752520 | tf_op jit(solution)/shard_map/ppermute | solution.py:56
  49.4 68.5 %collective-permute-start.30 = (bf16[512,896]{1,0:T(8,128)(2,1)}, bf16[512,896]{1,0:T(8,128)(2,1)}, u32[]{:S(2)}, u32[]{:S(2)}) collective-permute-start(bf16[512,896]{1,0:T(8,128)(2,1)} %bitcast.233), channel_id=1, source_target_pairs={{256,272},{264,280},{272,256},{280,264},{288,304},{296,312},{304,2... | collective-permute-start | bytes 2752520 | tf_op jit(solution)/shard_map/ppermute | solution.py:56
  51.1 1.2 copy-start.2
  82.6 28.6 %copy-start.7 = (bf16[1,896,512]{2,1,0:T(8,128)(2,1)S(1)}, bf16[1,896,512]{2,1,0:T(8,128)(2,1)}, u32[]{:S(2)}) copy-start(bf16[1,896,512]{2,1,0:T(8,128)(2,1)} %param.27) | copy-start | bytes 2752516
  82.6 1.6 collective-permute-start.2
  85.8 32.1 %all-to-all-start.17 = ((bf16[8,24,512]{2,1,0:T(8,128)(2,1)}), bf16[8,24,512]{2,1,0:T(8,128)(2,1)S(1)}, u32[]{:S(2)}, u32[]{:S(2)}) async-start(bf16[8,24,512]{2,1,0:T(8,128)(2,1)} %broadcast_in_dim.326), calls=%async_computation.17 | async-start | bytes 393216 | tf_op jit(solution)/shard_map/all_to_all | solution.py:38
  119.9 17.7 %all-to-all-start.18 = ((bf16[8,96,512]{2,1,0:T(8,128)(2,1)}), bf16[8,96,512]{2,1,0:T(8,128)(2,1)S(1)}, u32[]{:S(2)}, u32[]{:S(2)}) async-start(bf16[8,96,512]{2,1,0:T(8,128)(2,1)} %broadcast_in_dim.328), calls=%async_computation.18 | async-start | bytes 1572864 | tf_op jit(solution)/shard_map/all_to_all | solution.py:38
  137.6 2.2 copy-start.5
  138.5 95.2 %collective-permute-start.31 = (bf16[24,512]{1,0:T(8,128)(2,1)S(1)}, bf16[24,512]{1,0:T(8,128)(2,1)S(1)}, u32[]{:S(2)}, u32[]{:S(2)}) collective-permute-start(bf16[24,512]{1,0:T(8,128)(2,1)S(1)} %get-tuple-element.203), channel_id=1, source_target_pairs={{128,0},{129,1},{130,2},{131,3},{132,4},{133,5},{134,6},{135,7},{1... | collective-permute-start | bytes 73736 | tf_op jit(solution)/shard_map/ppermute | solution.py:264
  170.6 12.4 %collective-permute-start.5 = (bf16[8,24,896]{2,1,0:T(8,128)(2,1)S(1)}, bf16[8,24,896]{2,1,0:T(8,128)(2,1)S(1)}, u32[]{:S(2)}, u32[]{:S(2)}) collective-permute-start(bf16[8,24,896]{2,1,0:T(8,128)(2,1)S(1)} %get-tuple-element.222), channel_id=1, source_target_pairs={{0,8},{8,0},{16,24},{24,16},{32,40},{40,32},{48,56},{56,48},{64,72... | collective-permute-start | bytes 1032200 | tf_op jit(solution)/shard_map/cond/branch_1_fun/ppermute | solution.py:14
  179.6 3.3 %collective-permute-start.4 = (bf16[8,24,512]{2,1,0:T(8,128)(2,1)S(1)}, bf16[8,24,512]{2,1,0:T(8,128)(2,1)S(1)}, u32[]{:S(2)}, u32[]{:S(2)}) collective-permute-start(bf16[8,24,512]{2,1,0:T(8,128)(2,1)S(1)} %get-tuple-element.157), channel_id=1, source_target_pairs={{0,8},{8,0},{16,24},{24,16},{32,40},{40,32},{48,56},{56,48},{64,72... | collective-permute-start | bytes 589832 | tf_op jit(solution)/shard_map/cond/branch_1_fun/ppermute | solution.py:14
  233.7 0.8 copy-start.12
  234.5 4.6 %collective-permute-start.3 = (bf16[24,512]{1,0:T(8,128)(2,1)S(1)}, bf16[24,512]{1,0:T(8,128)(2,1)S(1)}, u32[]{:S(2)}, u32[]{:S(2)}) collective-permute-start(bf16[24,512]{1,0:T(8,128)(2,1)S(1)} %param.13), channel_id=1, source_target_pairs={{8,40},{24,56},{40,8},{56,24},{72,104},{88,120},{104,72},{120,88},... | collective-permute-start | bytes 73736 | tf_op jit(solution)/shard_map/cond/branch_0_fun/cond/branch_1_fun/ppermute | solution.py:172
  270.8 17.8 %all-to-all-start.13 = ((bf16[8,24,1792]{2,1,0:T(8,128)(2,1)}), bf16[8,24,1792]{2,1,0:T(8,128)(2,1)S(1)}, u32[]{:S(2)}, u32[]{:S(2)}) async-start(bf16[8,24,1792]{2,1,0:T(8,128)(2,1)} %broadcast_in_dim.210), calls=%async_computation.13 | async-start | bytes 1376256 | tf_op jit(solution)/shard_map/cond/branch_0_fun/all_to_all | solution.py:64
  274.3 36.2 %collective-permute-start.25 = (bf16[8,24,512]{2,1,0:T(8,128)(2,1)S(1)}, bf16[8,24,512]{2,1,0:T(8,128)(2,1)}, u32[]{:S(2)}, u32[]{:S(2)}) collective-permute-start(bf16[8,24,512]{2,1,0:T(8,128)(2,1)S(1)} %all_to_all.86), channel_id=1, source_target_pairs={{0,8},{8,0},{16,24},{24,16},{32,40},{40,32},{48,56},{56,48},{64,72... | collective-permute-start | bytes 589832 | tf_op jit(solution)/shard_map/cond/branch_0_fun/ppermute | solution.py:14
  290.1 20.5 %copy-start.13 = (bf16[16,24,896]{2,1,0:T(8,128)(2,1)S(1)}, bf16[16,24,896]{2,1,0:T(8,128)(2,1)}, u32[]{:S(2)}) copy-start(bf16[16,24,896]{2,1,0:T(8,128)(2,1)} %copy-done.12) | copy-start | bytes 2064388 | tf_op jit(solution)/shard_map/cond
  290.1 25.0 %all-to-all-start.14 = ((bf16[8,24,512]{2,1,0:T(8,128)(2,1)}), bf16[8,24,512]{2,1,0:T(8,128)(2,1)}, u32[]{:S(2)}, u32[]{:S(2)}) async-start(bf16[8,24,512]{2,1,0:T(8,128)(2,1)} %fusion.34), calls=%async_computation.14 | async-start | bytes 393216 | tf_op jit(solution)/shard_map/cond/branch_0_fun/all_to_all | solution.py:20
  295.8 17.0 %collective-permute-start.24 = (bf16[8,24,896]{2,1,0:T(8,128)(2,1)}, bf16[8,24,896]{2,1,0:T(8,128)(2,1)}, u32[]{:S(2)}, u32[]{:S(2)}) collective-permute-start(bf16[8,24,896]{2,1,0:T(8,128)(2,1)} %pad_maximum_fusion.6), channel_id=1, source_target_pairs={{0,8},{8,0},{16,24},{24,16},{32,40},{40,32},{48,56},{56,48},{64,72... | collective-permute-start | bytes 1032200 | tf_op jit(solution)/shard_map/cond/branch_0_fun/ppermute | solution.py:14
  316.6 0.9 copy-start.10
  316.6 1.2 copy-start.11

commit v9 on v8

--- a/solution.py
+++ b/solution.py
@@ -107,10 +107,8 @@
     up_other_low = swap_in_group(w_up[0], last - 2, 2)
     down_other = swap_middle(w_down[0], 2)
 
-    samples = jnp.swapaxes(pool, 0, 1)
-    fresh = jnp.zeros((rows, micro_count, width), BF16)
-    for sample in range(pool.shape[0]):
-        fresh = jnp.where((picked == sample)[None, :, None], samples[:, sample][:, None], fresh)
+    chosen = (picked[:, None] == jnp.arange(pool.shape[0])[None]).astype(BF16)
+    fresh = jnp.einsum("ms,srd->rmd", chosen, pool, preferred_element_type=F32).astype(BF16)
     fresh = fresh.reshape(block, width)
     inputs = jnp.swapaxes(saved[0], 0, 1).reshape(block, width)
 

time: 320 us -> 317 us (level)
  transfers between devices with their start and end apart: 18 -> 18, of which waited for: 7 -> 8; matrix products, arithmetic and copies ran while one was open for 7% -> 7% of each run, Pallas kernels for 0% -> 0%
where the time goes in v9:
time: 317 us; the launch traced here: 315 us
  starting transfers between devices  114 us (36%)
  waiting for transfers between devices  107 us (34%)
  blocking collectives  58.4 us (18%)
  local copies, waits for them, and re-layouts  15 us (5%)
  matrix products  10.9 us (3%)
  other arithmetic  8.48 us (3%)
    ppermute x6, starting transfers between devices, swap_cores(): return lax.ppermute(x, 'dp', [(i, i ^ 1) for i in range(peers)])  51.1 us
    ppermute x1, waiting for transfers between devices, body(): received = lax.ppermute(out, 'pipe', [(1, 0)])  50.6 us
    all_to_all x2, blocking collectives, features_exchange(): return lax.all_to_all(x, 'tensor', 0, 0, tiled=True)  46.3 us
    all_to_all x2, starting transfers between devices, rows_from_above(): lax.all_to_all(copies(x, 2 * few), ('pipe', 'dp'), 0, 0, axis_index_group...  33 us
    all_to_all x2, waiting for transfers between devices, features_exchange(): return lax.all_to_all(x, 'tensor', 0, 0, tiled=True)  27 us
    all_to_all x2, waiting for transfers between devices, rows_from_above(): lax.all_to_all(copies(x, 2 * few), ('pipe', 'dp'), 0, 0, axis_index_group...  13.9 us
    all_to_all x2, starting transfers between devices, features_exchange(): return lax.all_to_all(x, 'tensor', 0, 0, tiled=True)  13.6 us
    all_to_all x1, blocking collectives, chips_exchange(): return lax.all_to_all(x, 'dp', 0, 0, axis_index_groups=groups, tiled=True)  12.1 us
  transfers between devices with their start and end apart: 18, of which 8 were waited for; matrix products, arithmetic and copies ran while one was open for 7% of the time, Pallas kernels for 0%

profile of v9, /device:TPU:1, one launch (start us, length us, event | category | flops | bytes accessed | tf_op | source)
XLA Modules:
  0.0 315.2 jit_solution(8344985561180816862)
XLA Ops:
  0.6 8.9 %collective-permute-start.28 = (bf16[512,896]{1,0:T(8,128)(2,1)}, bf16[512,896]{1,0:T(8,128)(2,1)}, u32[]{:S(2)}, u32[]{:S(2)}) collective-permute-start(bf16[512,896]{1,0:T(8,128)(2,1)} %bitcast.218), channel_id=1, source_target_pairs={{0,8},{8,0},{16,24},{24,16},{32,40},{40,32},{48,56},{56,48},{64,72... | collective-permute-start | bytes 2752520 | tf_op jit(solution)/shard_map/ppermute | solution.py:14
  9.6 0.9 fusion.109
  10.5 0.8 reshape.66
  11.2 0.8 broadcast_in_dim.117
  12.0 3.9 %all-to-all-start.15 = ((bf16[8,48,512]{2,1,0:T(8,128)(2,1)}), bf16[8,48,512]{2,1,0:T(8,128)(2,1)S(1)}, u32[]{:S(2)}, u32[]{:S(2)}) async-start(bf16[8,48,512]{2,1,0:T(8,128)(2,1)} %broadcast_in_dim.117), calls=%async_computation.15 | async-start | bytes 786432 | tf_op jit(solution)/shard_map/all_to_all | solution.py:20
  15.9 2.3 collective-permute-start.29
  18.3 11.8 %all-to-all-done.15 = bf16[8,48,512]{2,1,0:T(8,128)(2,1)S(1)} async-done(((bf16[8,48,512]{2,1,0:T(8,128)(2,1)}), bf16[8,48,512]{2,1,0:T(8,128)(2,1)S(1)}, u32[]{:S(2)}, u32[]{:S(2)}) %all-to-all-start.15) | async-done | bytes 393248 | tf_op jit(solution)/shard_map/all_to_all | solution.py:20
  30.1 2.1 convolution_convert_fusion.6
  32.2 0.7 convolution_convert_fusion.5
  33.2 1.2 pad_maximum_fusion.17
  34.4 10.0 %all-to-all-start.16 = ((bf16[8,48,1792]{2,1,0:T(8,128)(2,1)}), bf16[8,48,1792]{2,1,0:T(8,128)(2,1)S(1)}, u32[]{:S(2)}, u32[]{:S(2)}) async-start(bf16[8,48,1792]{2,1,0:T(8,128)(2,1)} %pad_maximum_fusion.17), calls=%async_computation.16 | async-start | bytes 2752512 | tf_op jit(solution)/shard_map/all_to_all | solution.py:64
  44.4 1.6 collective-permute-start.26
  46.0 1.6 collective-permute-start.27
  47.6 1.7 collective-permute-start.30
  49.4 1.3 copy-done.3
  50.7 1.4 conditional.9
  50.7 1.4 broadcast.58
  52.1 1.6 pad_maximum_fusion.15
  53.6 27.0 %all-to-all-done.16 = bf16[8,48,1792]{2,1,0:T(8,128)(2,1)S(1)} async-done(((bf16[8,48,1792]{2,1,0:T(8,128)(2,1)}), bf16[8,48,1792]{2,1,0:T(8,128)(2,1)S(1)}, u32[]{:S(2)}, u32[]{:S(2)}) %all-to-all-start.16) | async-done | bytes 1376288 | tf_op jit(solution)/shard_map/all_to_all | solution.py:64
  80.9 2.4 conditional.10
  80.9 0.7 collective-permute-start.2
  81.6 0.8 slice_add_fusion
  82.3 0.9 broadcast.59
  83.3 0.7 broadcast_in_dim.118
  83.9 25.3 %all-to-all-start.17 = ((bf16[8,24,512]{2,1,0:T(8,128)(2,1)}), bf16[8,24,512]{2,1,0:T(8,128)(2,1)S(1)}, u32[]{:S(2)}, u32[]{:S(2)}) async-start(bf16[8,24,512]{2,1,0:T(8,128)(2,1)} %broadcast_in_dim.118), calls=%async_computation.17 | async-start | bytes 393216 | tf_op jit(solution)/shard_map/all_to_all | solution.py:38
  109.2 2.8 pad_maximum_fusion.16
  112.1 3.9 %all-to-all-done.17 = bf16[8,24,512]{2,1,0:T(8,128)(2,1)S(1)} async-done(((bf16[8,24,512]{2,1,0:T(8,128)(2,1)}), bf16[8,24,512]{2,1,0:T(8,128)(2,1)S(1)}, u32[]{:S(2)}, u32[]{:S(2)}) %all-to-all-start.17) | async-done | bytes 196640 | tf_op jit(solution)/shard_map/all_to_all | solution.py:38
  116.0 0.9 conditional.11
  116.0 0.9 broadcast.62
  116.9 0.9 broadcast_in_dim.120
  117.9 7.7 %all-to-all-start.18 = ((bf16[8,96,512]{2,1,0:T(8,128)(2,1)}), bf16[8,96,512]{2,1,0:T(8,128)(2,1)S(1)}, u32[]{:S(2)}, u32[]{:S(2)}) async-start(bf16[8,96,512]{2,1,0:T(8,128)(2,1)} %broadcast_in_dim.120), calls=%async_computation.18 | async-start | bytes 1572864 | tf_op jit(solution)/shard_map/all_to_all | solution.py:38
  125.6 10.0 %all-to-all-done.18 = bf16[8,96,512]{2,1,0:T(8,128)(2,1)S(1)} async-done(((bf16[8,96,512]{2,1,0:T(8,128)(2,1)}), bf16[8,96,512]{2,1,0:T(8,128)(2,1)S(1)}, u32[]{:S(2)}, u32[]{:S(2)}) %all-to-all-start.18) | async-done | bytes 786464 | tf_op jit(solution)/shard_map/all_to_all | solution.py:38
  135.6 1.0 conditional.12
  135.7 1.0 broadcast.64
  136.6 1.3 collective-permute-start.31
  137.9 0.7 fusion.120
  138.6 42.6 %conditional.13 = (bf16[16,24,512]{2,1,0:T(8,128)(2,1)S(1)}, bf16[16,24,896]{2,1,0:T(8,128)(2,1)S(1)}) conditional(s32[]{:T(128)} %convert_element_type.169, () %tuple.91, (bf16[8,24,512]{2,1,0:T(8,128)(2,1)S(1)}, bf16[24,1792]{1,0:T(8,128)(2,1)S(1)}) %tuple.92), branch_computations={%region_16.17_spmd, %region_17.18_spmd} | conditional | flops 540672 | bytes 7852128 | solution.py:254
  138.7 30.0 %all_to_all.85 = bf16[8,24,1792]{2,1,0:T(8,128)(2,1)S(1)} all-to-all(bf16[8,24,1792]{2,1,0:T(8,128)(2,1)S(1)} %broadcast_in_dim.62), channel_id=1, replica_groups=mesh['pipe'=4,'dp'=16,'tensor'=8] {'tensor'}, dimensions={0} | all-to-all | bytes 1376256 | tf_op jit(solution)/shard_map/cond/branch_1_fun/all_to_all | solution.py:64
  168.7 9.0 %collective-permute-start.5 = (bf16[8,24,896]{2,1,0:T(8,128)(2,1)S(1)}, bf16[8,24,896]{2,1,0:T(8,128)(2,1)S(1)}, u32[]{:S(2)}, u32[]{:S(2)}) collective-permute-start(bf16[8,24,896]{2,1,0:T(8,128)(2,1)S(1)} %get-tuple-element.222), channel_id=1, source_target_pairs={{0,8},{8,0},{16,24},{24,16},{32,40},{40,32},{48,56},{56,48},{64,72... | collective-permute-start | bytes 1032200 | tf_op jit(solution)/shard_map/cond/branch_1_fun/ppermute | solution.py:14
  177.8 1.9 collective-permute-start.4
  179.7 1.4 collective-permute-done.4
  181.2 50.6 %collective-permute-done.31 = bf16[24,512]{1,0:T(8,128)(2,1)S(1)} collective-permute-done((bf16[24,512]{1,0:T(8,128)(2,1)S(1)}, bf16[24,512]{1,0:T(8,128)(2,1)S(1)}, u32[]{:S(2)}, u32[]{:S(2)}) %collective-permute-start.31) | collective-permute-done | bytes 24608 | tf_op jit(solution)/shard_map/ppermute | solution.py:262
  231.8 82.2 %conditional.14 = (bf16[24,512]{1,0:T(8,128)(2,1)S(1)}, bf16[1,512,896]{2,1,0:T(8,128)(2,1)S(1)}, bf16[1,896,512]{2,1,0:T(8,128)(2,1)S(1)}) conditional(s32[]{:T(128)} %clamp.3, (bf16[24,512]{1,0:T(8,128)(2,1)S(1)}, bf16[1792,512]{1,0:T(8,128)(2,1)}, f32[24,1792]{1,0:T(8,128)S(1)}, bf16[512,1792]{1,0:T(8,128)(2,1)S(1)}, ...), branch_computations={%region_18.23_spmd, %region_23.24_spmd, %region_24.25_spmd, %regio... | conditional | flops 1413429248 | bytes 30876104 | solution.py:281
  231.8 0.8 copy-done.11
  232.6 0.7 copy-done.12
  233.4 4.6 %conditional = (bf16[24,512]{1,0:T(8,128)(2,1)S(1)}) conditional(s32[]{:T(128)} %convert_element_type.132, bf16[24,512]{1,0:T(8,128)(2,1)S(1)} %get-tuple-element.159, bf16[24,512]{1,0:T(8,128)(2,1)S(1)} %get-tuple-element.159), branch_computations={%region_19.19_spmd, %region_20.20_spmd} | conditional | flops 24576 | bytes 172080 | solution.py:173
  233.4 2.2 collective-permute-start.3
  235.6 2.4 collective-permute-done.3
  238.0 12.1 %all_to_all.86 = bf16[8,24,512]{2,1,0:T(8,128)(2,1)S(1)} all-to-all(bf16[8,24,512]{2,1,0:T(8,128)(2,1)S(1)} %broadcast_in_dim.71), channel_id=1, replica_groups={{0,16,32,48,64,80,96,112},{8,24,40,56,72,88,104,120},{1,17,33,49,65,81,..., dimensions={0} | all-to-all | bytes 393216 | tf_op jit(solution)/shard_map/cond/branch_0_fun/all_to_all | solution.py:20
  250.1 2.2 convolution_convert_fusion.4
  252.3 16.3 %all_to_all.87 = bf16[8,24,1792]{2,1,0:T(8,128)(2,1)S(1)} all-to-all(bf16[8,24,1792]{2,1,0:T(8,128)(2,1)S(1)} %convolution_convert_fusion.4), channel_id=1, replica_groups=mesh['pipe'=4,'dp'=16,'tensor'=8] {'tensor'}, dimensions={0} | all-to-all | bytes 1376256 | tf_op jit(solution)/shard_map/cond/branch_0_fun/all_to_all | solution.py:64
  268.8 0.9 broadcast_in_dim.72
  269.7 3.5 %all-to-all-start.13 = ((bf16[8,24,1792]{2,1,0:T(8,128)(2,1)}), bf16[8,24,1792]{2,1,0:T(8,128)(2,1)S(1)}, u32[]{:S(2)}, u32[]{:S(2)}) async-start(bf16[8,24,1792]{2,1,0:T(8,128)(2,1)} %broadcast_in_dim.72), calls=%async_computation.13 | async-start | bytes 1376256 | tf_op jit(solution)/shard_map/cond/branch_0_fun/all_to_all | solution.py:64
  273.2 14.1 %collective-permute-start.25 = (bf16[8,24,512]{2,1,0:T(8,128)(2,1)S(1)}, bf16[8,24,512]{2,1,0:T(8,128)(2,1)S(1)}, u32[]{:S(2)}, u32[]{:S(2)}) collective-permute-start(bf16[8,24,512]{2,1,0:T(8,128)(2,1)S(1)} %all_to_all.86), channel_id=1, source_target_pairs={{0,8},{8,0},{16,24},{24,16},{32,40},{40,32},{48,56},{56,48},{64,72... | collective-permute-start | bytes 589832 | tf_op jit(solution)/shard_map/cond/branch_0_fun/ppermute | solution.py:14
  287.4 1.4 fusion.34
  288.9 3.4 %all-to-all-start.14 = ((bf16[8,24,512]{2,1,0:T(8,128)(2,1)}), bf16[8,24,512]{2,1,0:T(8,128)(2,1)S(1)}, u32[]{:S(2)}, u32[]{:S(2)}) async-start(bf16[8,24,512]{2,1,0:T(8,128)(2,1)} %fusion.34), calls=%async_computation.14 | async-start | bytes 393216 | tf_op jit(solution)/shard_map/cond/branch_0_fun/all_to_all | solution.py:20
  292.3 0.7 compare_select_fusion.2
  293.1 0.8 pad_maximum_fusion.6
  293.8 14.8 %collective-permute-start.24 = (bf16[8,24,896]{2,1,0:T(8,128)(2,1)}, bf16[8,24,896]{2,1,0:T(8,128)(2,1)}, u32[]{:S(2)}, u32[]{:S(2)}) collective-permute-start(bf16[8,24,896]{2,1,0:T(8,128)(2,1)} %pad_maximum_fusion.6), channel_id=1, source_target_pairs={{0,8},{8,0},{16,24},{24,16},{32,40},{40,32},{48,56},{56,48},{64,72... | collective-permute-start | bytes 1032200 | tf_op jit(solution)/shard_map/cond/branch_0_fun/ppermute | solution.py:14
  308.7 1.8 fusion.33
  310.5 0.5 copy.25
  311.5 1.6 fusion.32
  313.1 0.6 copy.24
  314.0 0.7 reshape.69
  (55 shorter events, 2.3 us)
Async XLA Ops:
  0.6 8.9 %copy-start = (bf16[8,6,512]{2,0,1:T(8,128)(2,1)S(1)}, bf16[8,6,512]{2,0,1:T(8,128)(2,1)}, u32[]{:S(2)}) copy-start(bf16[8,6,512]{2,0,1:T(8,128)(2,1)} %param.24) | copy-start | bytes 147460
  0.6 29.4 %collective-permute-start.28 = (bf16[512,896]{1,0:T(8,128)(2,1)}, bf16[512,896]{1,0:T(8,128)(2,1)}, u32[]{:S(2)}, u32[]{:S(2)}) collective-permute-start(bf16[512,896]{1,0:T(8,128)(2,1)} %bitcast.218), channel_id=1, source_target_pairs={{0,8},{8,0},{16,24},{24,16},{32,40},{40,32},{48,56},{56,48},{64,72... | collective-permute-start | bytes 2752520 | tf_op jit(solution)/shard_map/ppermute | solution.py:14
  12.0 18.1 %all-to-all-start.15 = ((bf16[8,48,512]{2,1,0:T(8,128)(2,1)}), bf16[8,48,512]{2,1,0:T(8,128)(2,1)S(1)}, u32[]{:S(2)}, u32[]{:S(2)}) async-start(bf16[8,48,512]{2,1,0:T(8,128)(2,1)} %broadcast_in_dim.117), calls=%async_computation.15 | async-start | bytes 786432 | tf_op jit(solution)/shard_map/all_to_all | solution.py:20
  15.9 16.3 %copy-start.7 = (bf16[1,896,512]{2,1,0:T(8,128)(2,1)S(1)}, bf16[1,896,512]{2,1,0:T(8,128)(2,1)}, u32[]{:S(2)}) copy-start(bf16[1,896,512]{2,1,0:T(8,128)(2,1)} %param.27) | copy-start | bytes 2752516
  15.9 16.3 %collective-permute-start.29 = (bf16[896,512]{1,0:T(8,128)(2,1)}, bf16[896,512]{1,0:T(8,128)(2,1)S(1)}, u32[]{:S(2)}, u32[]{:S(2)}) collective-permute-start(bf16[896,512]{1,0:T(8,128)(2,1)} %bitcast.214), channel_id=1, source_target_pairs={{0,8},{8,0},{16,24},{24,16},{32,40},{40,32},{48,56},{56,48},{64,72... | collective-permute-start | bytes 2752520 | tf_op jit(solution)/shard_map/ppermute | solution.py:14
  30.1 2.1 copy-start.5
  32.2 0.9 copy-start.8
  34.4 46.3 %all-to-all-start.16 = ((bf16[8,48,1792]{2,1,0:T(8,128)(2,1)}), bf16[8,48,1792]{2,1,0:T(8,128)(2,1)S(1)}, u32[]{:S(2)}, u32[]{:S(2)}) async-start(bf16[8,48,1792]{2,1,0:T(8,128)(2,1)} %pad_maximum_fusion.17), calls=%async_computation.16 | async-start | bytes 2752512 | tf_op jit(solution)/shard_map/all_to_all | solution.py:64
  44.4 4.9 %collective-permute-start.26 = (bf16[896,512]{1,0:T(8,128)(2,1)S(1)}, bf16[896,512]{1,0:T(8,128)(2,1)}, u32[]{:S(2)}, u32[]{:S(2)}) collective-permute-start(bf16[896,512]{1,0:T(8,128)(2,1)S(1)} %bitcast.217), channel_id=1, source_target_pairs={{128,144},{136,152},{144,128},{152,136},{160,176},{168,184},{176,1... | collective-permute-start | bytes 2752520 | tf_op jit(solution)/shard_map/ppermute | solution.py:50
  46.0 3.4 %collective-permute-start.27 = (bf16[512,896]{1,0:T(8,128)(2,1)}, bf16[512,896]{1,0:T(8,128)(2,1)}, u32[]{:S(2)}, u32[]{:S(2)}) collective-permute-start(bf16[512,896]{1,0:T(8,128)(2,1)} %bitcast.220), channel_id=1, source_target_pairs={{128,144},{136,152},{144,128},{152,136},{160,176},{168,184},{176,1... | collective-permute-start | bytes 2752520 | tf_op jit(solution)/shard_map/ppermute | solution.py:56
  47.6 68.4 %collective-permute-start.30 = (bf16[512,896]{1,0:T(8,128)(2,1)}, bf16[512,896]{1,0:T(8,128)(2,1)}, u32[]{:S(2)}, u32[]{:S(2)}) collective-permute-start(bf16[512,896]{1,0:T(8,128)(2,1)} %bitcast.221), channel_id=1, source_target_pairs={{256,272},{264,280},{272,256},{280,264},{288,304},{296,312},{304,2... | collective-permute-start | bytes 2752520 | tf_op jit(solution)/shard_map/ppermute | solution.py:56
  49.4 1.3 copy-start.3
  80.9 1.4 collective-permute-start.2
  83.9 32.0 %all-to-all-start.17 = ((bf16[8,24,512]{2,1,0:T(8,128)(2,1)}), bf16[8,24,512]{2,1,0:T(8,128)(2,1)S(1)}, u32[]{:S(2)}, u32[]{:S(2)}) async-start(bf16[8,24,512]{2,1,0:T(8,128)(2,1)} %broadcast_in_dim.118), calls=%async_computation.17 | async-start | bytes 393216 | tf_op jit(solution)/shard_map/all_to_all | solution.py:38
  117.9 17.7 %all-to-all-start.18 = ((bf16[8,96,512]{2,1,0:T(8,128)(2,1)}), bf16[8,96,512]{2,1,0:T(8,128)(2,1)S(1)}, u32[]{:S(2)}, u32[]{:S(2)}) async-start(bf16[8,96,512]{2,1,0:T(8,128)(2,1)} %broadcast_in_dim.120), calls=%async_computation.18 | async-start | bytes 1572864 | tf_op jit(solution)/shard_map/all_to_all | solution.py:38
  135.6 2.3 copy-start.6
  136.6 95.2 %collective-permute-start.31 = (bf16[24,512]{1,0:T(8,128)(2,1)S(1)}, bf16[24,512]{1,0:T(8,128)(2,1)S(1)}, u32[]{:S(2)}, u32[]{:S(2)}) collective-permute-start(bf16[24,512]{1,0:T(8,128)(2,1)S(1)} %get-tuple-element.203), channel_id=1, source_target_pairs={{128,0},{129,1},{130,2},{131,3},{132,4},{133,5},{134,6},{135,7},{1... | collective-permute-start | bytes 73736 | tf_op jit(solution)/shard_map/ppermute | solution.py:262
  168.7 12.4 %collective-permute-start.5 = (bf16[8,24,896]{2,1,0:T(8,128)(2,1)S(1)}, bf16[8,24,896]{2,1,0:T(8,128)(2,1)S(1)}, u32[]{:S(2)}, u32[]{:S(2)}) collective-permute-start(bf16[8,24,896]{2,1,0:T(8,128)(2,1)S(1)} %get-tuple-element.222), channel_id=1, source_target_pairs={{0,8},{8,0},{16,24},{24,16},{32,40},{40,32},{48,56},{56,48},{64,72... | collective-permute-start | bytes 1032200 | tf_op jit(solution)/shard_map/cond/branch_1_fun/ppermute | solution.py:14
  177.8 3.3 %collective-permute-start.4 = (bf16[8,24,512]{2,1,0:T(8,128)(2,1)S(1)}, bf16[8,24,512]{2,1,0:T(8,128)(2,1)S(1)}, u32[]{:S(2)}, u32[]{:S(2)}) collective-permute-start(bf16[8,24,512]{2,1,0:T(8,128)(2,1)S(1)} %get-tuple-element.157), channel_id=1, source_target_pairs={{0,8},{8,0},{16,24},{24,16},{32,40},{40,32},{48,56},{56,48},{64,72... | collective-permute-start | bytes 589832 | tf_op jit(solution)/shard_map/cond/branch_1_fun/ppermute | solution.py:14
  231.8 0.8 copy-start.11
  232.6 0.7 copy-start.12
  233.4 4.6 %collective-permute-start.3 = (bf16[24,512]{1,0:T(8,128)(2,1)S(1)}, bf16[24,512]{1,0:T(8,128)(2,1)S(1)}, u32[]{:S(2)}, u32[]{:S(2)}) collective-permute-start(bf16[24,512]{1,0:T(8,128)(2,1)S(1)} %param.13), channel_id=1, source_target_pairs={{8,40},{24,56},{40,8},{56,24},{72,104},{88,120},{104,72},{120,88},... | collective-permute-start | bytes 73736 | tf_op jit(solution)/shard_map/cond/branch_0_fun/cond/branch_1_fun/ppermute | solution.py:170
  269.7 17.8 %all-to-all-start.13 = ((bf16[8,24,1792]{2,1,0:T(8,128)(2,1)}), bf16[8,24,1792]{2,1,0:T(8,128)(2,1)S(1)}, u32[]{:S(2)}, u32[]{:S(2)}) async-start(bf16[8,24,1792]{2,1,0:T(8,128)(2,1)} %broadcast_in_dim.72), calls=%async_computation.13 | async-start | bytes 1376256 | tf_op jit(solution)/shard_map/cond/branch_0_fun/all_to_all | solution.py:64
  273.2 35.5 %collective-permute-start.25 = (bf16[8,24,512]{2,1,0:T(8,128)(2,1)S(1)}, bf16[8,24,512]{2,1,0:T(8,128)(2,1)S(1)}, u32[]{:S(2)}, u32[]{:S(2)}) collective-permute-start(bf16[8,24,512]{2,1,0:T(8,128)(2,1)S(1)} %all_to_all.86), channel_id=1, source_target_pairs={{0,8},{8,0},{16,24},{24,16},{32,40},{40,32},{48,56},{56,48},{64,72... | collective-permute-start | bytes 589832 | tf_op jit(solution)/shard_map/cond/branch_0_fun/ppermute | solution.py:14
  288.9 24.9 %all-to-all-start.14 = ((bf16[8,24,512]{2,1,0:T(8,128)(2,1)}), bf16[8,24,512]{2,1,0:T(8,128)(2,1)S(1)}, u32[]{:S(2)}, u32[]{:S(2)}) async-start(bf16[8,24,512]{2,1,0:T(8,128)(2,1)} %fusion.34), calls=%async_computation.14 | async-start | bytes 393216 | tf_op jit(solution)/shard_map/cond/branch_0_fun/all_to_all | solution.py:20
  293.8 17.3 %collective-permute-start.24 = (bf16[8,24,896]{2,1,0:T(8,128)(2,1)}, bf16[8,24,896]{2,1,0:T(8,128)(2,1)}, u32[]{:S(2)}, u32[]{:S(2)}) collective-permute-start(bf16[8,24,896]{2,1,0:T(8,128)(2,1)} %pad_maximum_fusion.6), channel_id=1, source_target_pairs={{0,8},{8,0},{16,24},{24,16},{32,40},{40,32},{48,56},{56,48},{64,72... | collective-permute-start | bytes 1032200 | tf_op jit(solution)/shard_map/cond/branch_0_fun/ppermute | solution.py:14
  310.5 1.0 copy-start.13
  314.0 0.9 copy-start.9
  314.0 1.2 copy-start.10
